TPU v7x, 512 devices: a whole 4x8x8 slice. The times are simulated.
512 devices in a mesh: angle: 16 (over z, core), tx: 4 (over y_hi), ty: 8 (over y_lo, x).
Axes of the slice: x: 4, y: 8 (y_hi: 4, y_lo: 2; y = y_hi * 2 + y_lo), z: 8, core: 2. Of those that a mesh axis runs over, the one named last changes fastest.
Arguments:
- index: float32 [64, 512, 512], P('angle', 'ty', 'tx'), may hold values from -6 to 6
- measured: float32 [2, 16, 512, 512], P(None, 'angle', 'ty', 'tx'), may hold values from -6 to 6
- illum: int32 [16, 2], P('angle'), may hold values from -16 to 16
Outputs:
- gradient: float32 [64, 512, 512], P('angle', 'ty', 'tx')
- index_new: float32 [64, 512, 512], P('angle', 'ty', 'tx')
All inputs are finite; a program needn't handle non-finite values.
Results may differ from a plain program's by a relative error of at most 0.000054.
Values sent between devices are 32-bit elements; how exact they have to be, the bound alone decides.
No kernel may reach another device: no remote copies, remote signals or barrier semaphores. Data moves between devices by JAX's collectives and lax.ppermute only.
A program may use at most 64 MiB of HBM per device.

v0:
```python
import math

import jax
import jax.numpy as jnp
from jax import lax
from jax.sharding import PartitionSpec as P

DEPTH = 8
TV_STEPS = 3


damping = 0.2
disperse = 0.1
phase_scale = 0.1
step_size = 0.1
tv_rate = 0.05
tv_smooth = 0.1


def with_halo(block, sides, width):
    for axis, dim in sides:
        count = lax.axis_size(axis)
        forward = [(i, i + 1) for i in range(count - 1)]
        forward.append((count - 1, 0))
        backward = [(target, source) for source, target in forward]
        low = lax.ppermute(
            lax.slice_in_dim(block, block.shape[dim] - width, None, axis=dim), axis, forward
        )
        high = lax.ppermute(lax.slice_in_dim(block, 0, width, axis=dim), axis, backward)
        block = jnp.concatenate([low, block, high], axis=dim)
    return block


def crop(block, reach):
    return block[..., reach : block.shape[-2] - reach, reach : block.shape[-1] - reach]


def lateral(field):
    center = field[..., 1:-1, 1:-1]
    lap = (
        field[..., :-2, 1:-1]
        + field[..., 2:, 1:-1]
        + field[..., 1:-1, :-2]
        + field[..., 1:-1, 2:]
        - 4.0 * center
    )
    return (lap, center)


def forward_step(field, phase):
    lap, center = lateral(field)
    wre = center[0] + damping * lap[0] - disperse * lap[1]
    wim = center[1] + damping * lap[1] + disperse * lap[0]
    cosine = jnp.cos(phase)
    sine = jnp.sin(phase)
    return jnp.stack([cosine * wre - sine * wim, cosine * wim + sine * wre])


def advance(extended, block_rim, reach):
    fields = []
    field = extended
    for slot in range(reach):
        phase = phase_scale * crop(block_rim[slot], slot + 1)
        field = forward_step(field, phase)
        fields.append(field)
    return fields


def smooth(extended, reach, z_first, nz_total):
    length = extended.shape[0]
    base = extended[:-1, :-1, :-1]
    diff_z = extended[1:, :-1, :-1] - base
    diff_y = extended[:-1, 1:, :-1] - base
    diff_x = extended[:-1, :-1, 1:] - base
    depth_pos = (z_first - reach + jnp.arange(length - 1)) % nz_total
    diff_z = jnp.where(depth_pos[:, None, None] == nz_total - 1, 0.0, diff_z)
    magnitude = jnp.sqrt(
        diff_z * diff_z + diff_y * diff_y + diff_x * diff_x + tv_smooth * tv_smooth
    )
    flux_z = diff_z / magnitude
    flux_y = diff_y / magnitude
    flux_x = diff_x / magnitude
    divergence = (
        flux_z[1:, 1:, 1:]
        - flux_z[:-1, 1:, 1:]
        + flux_y[1:, 1:, 1:]
        - flux_y[1:, :-1, 1:]
        + flux_x[1:, 1:, 1:]
        - flux_x[1:, 1:, :-1]
    )
    return extended[1:-1, 1:-1, 1:-1] + tv_rate * divergence


def body(index, measured, illum):
    slab, rows, cols = index.shape
    nz_total = slab * lax.axis_size("angle")
    nx_total = cols * lax.axis_size("tx")
    ny_total = rows * lax.axis_size("ty")
    xs = (lax.axis_index("tx") * cols + jnp.arange(cols)).astype(jnp.float32)
    ys = (lax.axis_index("ty") * rows + jnp.arange(rows)).astype(jnp.float32)
    freq_x = illum[:, 0].astype(jnp.float32)[:, None, None]
    freq_y = illum[:, 1].astype(jnp.float32)[:, None, None]
    angle_q = (
        2.0
        * math.pi
        * (freq_x * xs[None, None, :] / nx_total + freq_y * ys[None, :, None] / ny_total)
    )
    start = jnp.stack([jnp.cos(angle_q), jnp.sin(angle_q)])
    reach = DEPTH
    blocks = nz_total // reach
    column = lax.all_gather(index, "angle", axis=0, tiled=True)
    rim = with_halo(column, (("tx", 2), ("ty", 1)), reach)
    rim_blocks = rim.reshape(blocks, reach, rim.shape[1], rim.shape[2])

    def forward_block(field, block_rim):
        extended = with_halo(field, (("tx", 3), ("ty", 2)), reach)
        fields = advance(extended, block_rim, reach)
        return (fields[-1], extended)

    final, saved = lax.scan(forward_block, start, rim_blocks)
    residual = final - measured

    def backward_block(cotangent, inputs):
        extended, block_rim = inputs
        fields = advance(extended, block_rim, reach)
        adjoint = with_halo(cotangent, (("tx", 3), ("ty", 2)), reach)
        layers = [None] * reach
        for slot in reversed(range(reach)):
            inner_adj = crop(adjoint, slot + 1)
            inner_fld = crop(fields[slot], reach - slot - 1)
            layers[slot] = phase_scale * jnp.sum(
                inner_adj[1] * inner_fld[0] - inner_adj[0] * inner_fld[1], axis=0
            )
            phase = phase_scale * crop(block_rim[slot], reach - slot - 1)
            cosine = jnp.cos(phase)
            sine = jnp.sin(phase)
            back_re = cosine * adjoint[0] + sine * adjoint[1]
            back_im = cosine * adjoint[1] - sine * adjoint[0]
            lap, center = lateral(jnp.stack([back_re, back_im]))
            adjoint = jnp.stack(
                [
                    center[0] + damping * lap[0] + disperse * lap[1],
                    center[1] + damping * lap[1] - disperse * lap[0],
                ]
            )
        return (adjoint, jnp.stack(layers))

    unused, grads = lax.scan(backward_block, residual, (saved, rim_blocks), reverse=True)
    grad_column = grads.reshape(nz_total, rows, cols)
    gradient = lax.psum_scatter(grad_column, "angle", scatter_dimension=0, tiled=True)
    volume = index - step_size * gradient
    z_first = lax.axis_index("angle") * slab
    width, rounds = (1, TV_STEPS)
    for turn in range(rounds):
        extended = with_halo(volume, (("angle", 0), ("tx", 2), ("ty", 1)), width)
        extended = smooth(extended, width, z_first, nz_total)
        volume = extended
    return (gradient, volume)


def solution(mesh):
    in_specs = (P("angle", "ty", "tx"), P(None, "angle", "ty", "tx"), P("angle", None))
    out_specs = (P("angle", "ty", "tx"), P("angle", "ty", "tx"))
    return jax.shard_map(body, mesh=mesh, in_specs=in_specs, out_specs=out_specs, check_vma=False)
```

profile of v0, /device:TPU:1, one launch (start us, length us, event | category | flops | bytes accessed | tf_op | source)
XLA Modules:
  0.0 779.3 jit_solution(12593633571083586954)
XLA Ops:
  10.0 49.3 %all-gather.2.cloned.1.call-done = f32[64,64,128]{2,1,0:T(8,128)} async-done(((f32[4,64,128]{2,1,0:T(8,128)}), f32[64,64,128]{2,1,0:T(8,128)}) %all-gather.2.cloned.1.call-update) | async-done | bytes 2097168 | tf_op jit(solution)/shard_map/all_gather | solution.py:111
  59.2 4.3 fusion.420
  65.7 4.0 collective-permute-start.8
  70.3 3.4 collective-permute-start.9
  74.4 5.9 collective-permute-done.8
  82.3 5.6 collective-permute-done.9
  94.9 4.3 collective-permute-start.11
  99.4 9.3 %collective-permute-done.10 = f32[64,8,144]{2,1,0:T(8,128)S(1)} collective-permute-done((f32[64,8,144]{2,1,0:T(8,128)S(1)}, f32[64,8,144]{2,1,0:T(8,128)S(1)}, u32[]{:S(2)}, u32[]{:S(2)}) %collective-permute-start.10) | collective-permute-done | bytes 294944 | tf_op jit(solution)/shard_map/ppermute | solution.py:26
  109.6 3.8 pad_maximum_fusion.32
  113.4 200.4 %while.28 = (s32[]{:T(128)}, f32[2,1,64,128]{3,2,1,0:T(8,128)S(1)}, f32[8,2,1,80,144]{4,3,1,2,0:T(8,128)}, f32[8,8,80,144]{3,2,1,0:T(8,128)}, s32[]{:T(128)}, /*...) while((s32[]{:T(128)}, f32[2,1,64,128]{3,2,1,0:T(8,128)S(1)}, ...), condition=%wide.region_1.2_spmd, body=%wide.region_0.1_spmd.sunk | while | flops 2696689 | bytes 5190781 | solution.py:120
  115.4 4.3 collective-permute-start.1
  122.6 6.9 collective-permute-start.2
  132.7 3.4 collective-permute-done.3
  148.4 3.6 collective-permute-done.1
  154.2 3.2 collective-permute-start.3
  166.5 4.6 collective-permute-start
  173.0 5.2 collective-permute-done.1
  180.3 3.2 collective-permute-start.3
  194.6 4.3 collective-permute-start.1
  203.8 3.3 collective-permute-start.3
  218.3 3.9 collective-permute-start.1
  227.6 3.2 collective-permute-start.3
  242.7 3.4 collective-permute-start.1
  246.1 3.7 collective-permute-done.1
  264.3 4.2 collective-permute-start
  270.6 5.4 collective-permute-done.1
  278.0 3.4 collective-permute-start.3
  292.3 4.1 collective-permute-start.1
  301.6 3.2 collective-permute-start.3
  314.0 261.9 %while.29 = (s32[]{:T(128)}, f32[2,1,64,128]{3,2,1,0:T(8,128)S(1)}, f32[8,8,64,128]{3,2,1,0:T(8,128)S(1)}, f32[8,8,80,144]{3,2,1,0:T(8,128)}, f32[8,2,1,80,144]{...) while((s32[]{:T(128)}, f32[2,1,64,128]{3,2,1,0:T(8,128)S(1)}, ...), condition=%wide.region_3.4_spmd, body=%wide.region_2.3_spmd.sunk | while | flops 5730673 | bytes 11808661 | solution.py:148
  316.5 4.0 collective-permute-start.5
  325.8 3.2 collective-permute-start.7
  346.2 4.3 collective-permute-start.4
  353.4 4.2 collective-permute-done.5
  359.6 3.4 collective-permute-start.7
  383.0 3.3 collective-permute-start.5
  392.1 3.4 collective-permute-start.7
  415.0 3.8 collective-permute-start.5
  424.1 3.4 collective-permute-start.7
  447.4 3.4 collective-permute-start.5
  451.7 3.6 collective-permute-done.5
  457.3 3.4 collective-permute-start.7
  477.8 3.8 collective-permute-start.4
  484.9 4.5 collective-permute-done.5
  491.4 3.4 collective-permute-start.7
  513.8 4.3 collective-permute-start.5
  522.9 3.4 collective-permute-start.7
  545.6 4.0 collective-permute-start.5
  558.4 3.6 collective-permute-done.7
  577.3 97.9 %reduce-scatter.2.cloned.1.call-done = f32[4,64,128]{2,1,0:T(8,128)} async-done(((f32[64,64,128]{2,1,0:T(8,128)}), f32[4,64,128]{2,1,0:T(8,128)}) %reduce-scatter.2.cloned.1.call-update) | async-done | bytes 131088 | tf_op jit(solution)/shard_map/reduce_scatter | solution.py:150
  681.2 4.0 collective-permute-start.14
  685.2 3.4 collective-permute-start.15
  690.7 6.8 collective-permute-done.15
  700.7 4.3 collective-permute-start.17
  706.7 4.1 collective-permute-start.18
  714.6 4.2 collective-permute-start.20
  718.8 3.2 collective-permute-start.21
  724.6 3.3 collective-permute-done.21
  730.7 6.3 collective-permute-start.23
  738.7 4.0 collective-permute-start.24
  748.8 5.0 collective-permute-start.27
  753.9 3.2 collective-permute-done.26
  757.1 5.2 collective-permute-done.27
  764.3 5.8 collective-permute-start.29
  (745 shorter events, 361.4 us)
Async XLA Ops:
  7.2 52.1 %all-gather.2.cloned.1.call-start = ((), (), s32[]{:S(2)}) async-start(), calls=%async_computation.1 | async-start | bytes 2228224 | tf_op jit(solution)/shard_map/all_gather | solution.py:111
  7.9 667.3 %reduce-scatter.2.cloned.1.call-start = ((), (), s32[]{:S(2)}) async-start(), calls=%async_computation.2 | async-start | bytes 2228224 | tf_op jit(solution)/shard_map/reduce_scatter | solution.py:150
  65.7 14.6 %collective-permute-start.8 = (f32[64,64,8]{1,2,0:T(8,128)S(1)}, f32[64,64,8]{1,2,0:T(8,128)S(1)}, u32[]{:S(2)}, u32[]{:S(2)}) collective-permute-start(f32[64,64,8]{1,2,0:T(8,128)S(1)} %copy.27), channel_id=1, source_target_pairs={{0,8},{8,16},{16,24},{24,0},{1,9},{9,17},{17,25},{25,1},{2,10},{10... | collective-permute-start | bytes 393224 | tf_op jit(solution)/shard_map/ppermute | solution.py:26
  70.3 17.6 %collective-permute-start.9 = (f32[64,64,8]{1,2,0:T(8,128)S(1)}, f32[64,64,8]{1,2,0:T(8,128)S(1)}, u32[]{:S(2)}, u32[]{:S(2)}) collective-permute-start(f32[64,64,8]{1,2,0:T(8,128)S(1)} %copy.28), channel_id=1, source_target_pairs={{8,0},{16,8},{24,16},{0,24},{9,1},{17,9},{25,17},{1,25},{10,2},{18... | collective-permute-start | bytes 393224 | tf_op jit(solution)/shard_map/ppermute | solution.py:29
  91.8 17.0 %collective-permute-start.10 = (f32[64,8,144]{2,1,0:T(8,128)S(1)}, f32[64,8,144]{2,1,0:T(8,128)S(1)}, u32[]{:S(2)}, u32[]{:S(2)}) collective-permute-start(f32[64,8,144]{2,1,0:T(8,128)S(1)} %get-tuple-element.239), channel_id=1, source_target_pairs={{0,1},{1,2},{2,3},{3,4},{4,5},{5,6},{6,7},{7,0},{8,9},{9,10},{10,1... | collective-permute-start | bytes 884744 | tf_op jit(solution)/shard_map/ppermute | solution.py:26
  94.9 14.7 %collective-permute-start.11 = (f32[64,8,144]{2,1,0:T(8,128)S(1)}, f32[64,8,144]{2,1,0:T(8,128)S(1)}, u32[]{:S(2)}, u32[]{:S(2)}) collective-permute-start(f32[64,8,144]{2,1,0:T(8,128)S(1)} %get-tuple-element.240), channel_id=1, source_target_pairs={{1,0},{2,1},{3,2},{4,3},{5,4},{6,5},{7,6},{0,7},{9,8},{10,9},{11,1... | collective-permute-start | bytes 884744 | tf_op jit(solution)/shard_map/ppermute | solution.py:29
  115.4 7.1 collective-permute-start.1
  122.6 10.1 %collective-permute-start.2 = (f32[2,1,8,144]{3,2,0,1:T(8,128)S(1)}, f32[2,1,8,144]{3,2,0,1:T(8,128)S(1)}, u32[]{:S(2)}, u32[]{:S(2)}) collective-permute-start(f32[2,1,8,144]{3,2,0,1:T(8,128)S(1)} %get-tuple-element.414), channel_id=1, source_target_pairs={{1,0},{2,1},{3,2},{4,3},{5,4},{6,5},{7,6},{0,7},{9,8},{10,9},{11,1... | collective-permute-start | bytes 27656 | tf_op jit(solution)/shard_map/while/body/eval_jaxpr/ppermute | solution.py:29
  129.5 6.6 collective-permute-start.3
  141.8 6.6 collective-permute-start
  144.9 7.1 collective-permute-start.1
  152.1 6.5 collective-permute-start.2
  154.2 6.6 collective-permute-start.3
  171.0 7.1 collective-permute-start.1
  178.2 6.5 collective-permute-start.2
  180.3 6.7 collective-permute-start.3
  194.6 7.1 collective-permute-start.1
  201.8 6.5 collective-permute-start.2
  203.8 6.6 collective-permute-start.3
  218.3 7.1 collective-permute-start.1
  225.5 6.5 collective-permute-start.2
  227.6 6.6 collective-permute-start.3
  242.7 7.1 collective-permute-start.1
  252.1 6.6 collective-permute-start.3
  268.5 7.4 collective-permute-start.1
  276.0 6.5 collective-permute-start.2
  278.0 6.6 collective-permute-start.3
  292.3 7.1 collective-permute-start.1
  301.6 6.6 collective-permute-start.3
  314.3 7.1 collective-permute-start.4
  316.5 7.1 collective-permute-start.5
  325.8 6.6 collective-permute-start.7
  346.2 7.2 collective-permute-start.4
  350.5 7.1 collective-permute-start.5
  359.6 6.6 collective-permute-start.7
  380.1 7.1 collective-permute-start.4
  383.0 7.1 collective-permute-start.5
  392.1 6.6 collective-permute-start.7
  412.6 7.1 collective-permute-start.4
  415.0 7.1 collective-permute-start.5
  424.1 6.6 collective-permute-start.7
  444.6 7.1 collective-permute-start.4
  447.4 7.9 %collective-permute-start.5 = (f32[2,1,64,8]{3,2,1,0:T(8,128)S(1)}, f32[2,1,64,8]{3,2,1,0:T(8,128)S(1)}, u32[]{:S(2)}, u32[]{:S(2)}) collective-permute-start(f32[2,1,64,8]{3,2,1,0:T(8,128)S(1)} %get-tuple-element.440), channel_id=1, source_target_pairs={{0,8},{8,16},{16,24},{24,0},{1,9},{9,17},{17,25},{25,1},{2,10},{10... | collective-permute-start | bytes 12296 | tf_op jit(solution)/shard_map/while/body/eval_jaxpr/ppermute | solution.py:26
  457.3 6.6 collective-permute-start.7
  477.8 7.1 collective-permute-start.4
  481.6 7.9 %collective-permute-start.5 = (f32[2,1,64,8]{3,2,1,0:T(8,128)S(1)}, f32[2,1,64,8]{3,2,1,0:T(8,128)S(1)}, u32[]{:S(2)}, u32[]{:S(2)}) collective-permute-start(f32[2,1,64,8]{3,2,1,0:T(8,128)S(1)} %get-tuple-element.440), channel_id=1, source_target_pairs={{0,8},{8,16},{16,24},{24,0},{1,9},{9,17},{17,25},{25,1},{2,10},{10... | collective-permute-start | bytes 12296 | tf_op jit(solution)/shard_map/while/body/eval_jaxpr/ppermute | solution.py:26
  491.4 6.6 collective-permute-start.7
  511.9 7.1 collective-permute-start.4
  513.8 7.1 collective-permute-start.5
  522.9 6.6 collective-permute-start.7
  543.4 7.1 collective-permute-start.4
  545.6 7.1 collective-permute-start.5
  555.4 6.6 collective-permute-start.7
  681.2 9.5 %collective-permute-start.14 = (f32[6,64,1]{2,1,0:T(8,128)S(1)}, f32[6,64,1]{2,1,0:T(8,128)S(1)}, u32[]{:S(2)}, u32[]{:S(2)}) collective-permute-start(f32[6,64,1]{2,1,0:T(8,128)S(1)} %get-tuple-element.259), channel_id=1, source_target_pairs={{0,8},{8,16},{16,24},{24,0},{1,9},{9,17},{17,25},{25,1},{2,10},{10... | collective-permute-start | bytes 4616 | tf_op jit(solution)/shard_map/ppermute | solution.py:26
  685.2 12.2 %collective-permute-start.15 = (f32[6,64,1]{2,1,0:T(8,128)S(1)}, f32[6,64,1]{2,1,0:T(8,128)S(1)}, u32[]{:S(2)}, u32[]{:S(2)}) collective-permute-start(f32[6,64,1]{2,1,0:T(8,128)S(1)} %get-tuple-element.260), channel_id=1, source_target_pairs={{8,0},{16,8},{24,16},{0,24},{9,1},{17,9},{25,17},{1,25},{10,2},{18... | collective-permute-start | bytes 4616 | tf_op jit(solution)/shard_map/ppermute | solution.py:29
  697.6 7.4 collective-permute-start.16
  714.6 10.0 %collective-permute-start.20 = (f32[6,64,1]{2,1,0:T(8,128)S(1)}, f32[6,64,1]{2,1,0:T(8,128)S(1)}, u32[]{:S(2)}, u32[]{:S(2)}) collective-permute-start(f32[6,64,1]{2,1,0:T(8,128)S(1)} %get-tuple-element.257), channel_id=1, source_target_pairs={{0,8},{8,16},{16,24},{24,0},{1,9},{9,17},{17,25},{25,1},{2,10},{10... | collective-permute-start | bytes 4616 | tf_op jit(solution)/shard_map/ppermute | solution.py:26
  718.8 9.1 %collective-permute-start.21 = (f32[6,64,1]{2,1,0:T(8,128)S(1)}, f32[6,64,1]{2,1,0:T(8,128)S(1)}, u32[]{:S(2)}, u32[]{:S(2)}) collective-permute-start(f32[6,64,1]{2,1,0:T(8,128)S(1)} %get-tuple-element.258), channel_id=1, source_target_pairs={{8,0},{16,8},{24,16},{0,24},{9,1},{17,9},{25,17},{1,25},{10,2},{18... | collective-permute-start | bytes 4616 | tf_op jit(solution)/shard_map/ppermute | solution.py:29
  728.0 9.0 %collective-permute-start.22 = (f32[6,1,130]{2,1,0:T(1,128)S(1)}, f32[6,1,130]{2,1,0:T(1,128)S(1)}, u32[]{:S(2)}, u32[]{:S(2)}) collective-permute-start(f32[6,1,130]{2,1,0:T(1,128)S(1)} %get-tuple-element.252), channel_id=1, source_target_pairs={{0,1},{1,2},{2,3},{3,4},{4,5},{5,6},{6,7},{7,0},{8,9},{9,10},{10,1... | collective-permute-start | bytes 9368 | tf_op jit(solution)/shard_map/ppermute | solution.py:26
  730.7 7.0 collective-permute-start.23
  746.5 10.6 %collective-permute-start.26 = (f32[6,64,1]{2,1,0:T(8,128)S(1)}, f32[6,64,1]{2,1,0:T(8,128)S(1)}, u32[]{:S(2)}, u32[]{:S(2)}) collective-permute-start(f32[6,64,1]{2,1,0:T(8,128)S(1)} %get-tuple-element.255), channel_id=1, source_target_pairs={{0,8},{8,16},{16,24},{24,0},{1,9},{9,17},{17,25},{25,1},{2,10},{10... | collective-permute-start | bytes 4616 | tf_op jit(solution)/shard_map/ppermute | solution.py:26
  748.8 13.4 %collective-permute-start.27 = (f32[6,64,1]{2,1,0:T(8,128)S(1)}, f32[6,64,1]{2,1,0:T(8,128)S(1)}, u32[]{:S(2)}, u32[]{:S(2)}) collective-permute-start(f32[6,64,1]{2,1,0:T(8,128)S(1)} %get-tuple-element.256), channel_id=1, source_target_pairs={{8,0},{16,8},{24,16},{0,24},{9,1},{17,9},{25,17},{1,25},{10,2},{18... | collective-permute-start | bytes 4616 | tf_op jit(solution)/shard_map/ppermute | solution.py:29
  762.4 7.8 collective-permute-start.28
  764.3 6.6 collective-permute-start.29
  (30 other events, 487.0 us)
Sparse Core Ops, SparseCore 0:
  10.1 49.0 all-gather.1
  577.4 97.7 reduce-scatter.1
where the time goes:
time: 785 us; the launch traced here: 779 us
  waiting for transfers between devices  300 us (38%)
  starting transfers between devices  260 us (33%)
  other arithmetic  166 us (21%)
  local copies, waits for them, and re-layouts  33.1 us (4%)
  between operations  15.8 us (2%)
    ppermute x43, starting transfers between devices, with_halo(): lax.ppermute(lax.slice_in_dim(block, block.shape[dim] - width, None, axis...  140 us
    ppermute x43, waiting for transfers between devices, with_halo(): lax.ppermute(lax.slice_in_dim(block, block.shape[dim] - width, None, axis...  122 us
    ppermute x43, starting transfers between devices, with_halo(): lax.ppermute(lax.slice_in_dim(block, 0, width, axis=dim), axis, backward)  120 us
    reduce_scatter x1, waiting for transfers between devices, body(): lax.psum_scatter(grad_column, 'angle', scatter_dimension=0, tiled=True)  97.9 us
    all_gather x1, waiting for transfers between devices, body(): column = lax.all_gather(index, 'angle', axis=0, tiled=True)  49.3 us
    sub x192, other arithmetic, lateral(): field[..., :-2, 1:-1] + field[..., 2:, 1:-1] + field[..., 1:-1, :-2]  42.3 us
    another operation x120, other arithmetic, forward_step(): return jnp.stack([cosine * wre - sine * wim, cosine * wim + sine * wre])  41.9 us
    another operation x104, other arithmetic, backward_block(): lap, center = lateral(jnp.stack([back_re, back_im]))  41.4 us
  transfers between devices with their start and end apart: 88, of which 54 were waited for; matrix products, arithmetic and copies ran while one was open for 3% of the time, Pallas kernels for 0%

commit v1 on v0

v1 whole, which is shorter than its diff:
```python
import functools
import math

import jax
import jax.numpy as jnp
import numpy as np
from jax import lax
from jax.experimental import pallas as pl
from jax.experimental.pallas import tpu as pltpu
from jax.sharding import PartitionSpec as P

TV_STEPS = 3
HALO = 64
GROUP = 8

damping = 0.2
disperse = 0.1
phase_scale = 0.1
step_size = 0.1
tv_rate = 0.05
tv_smooth = 0.1

SPREAD = complex(damping, disperse)
GAIN = abs(SPREAD)
TURN = SPREAD / GAIN


def _fit():
    nodes = np.cos((np.arange(400) + 0.5) * np.pi / 400)
    t = 3.05 * (nodes + 1.0)
    z = t * t
    scaled = z / z.max()
    even = np.linalg.lstsq(scaled[:, None] ** np.arange(5), GAIN * np.cos(phase_scale * t), rcond=None)[0]
    odd = np.linalg.lstsq(scaled[:, None] ** np.arange(5), GAIN * np.sin(phase_scale * t) / t, rcond=None)[0]
    powers = z.max() ** np.arange(5)
    return [float(v) for v in even / powers], [float(v) for v in odd / powers]


EVEN, ODD = _fit()


def phase_factor(t):
    z = t * t
    cosine = EVEN[4]
    for coef in EVEN[3::-1]:
        cosine = cosine * z + coef
    sine = ODD[4]
    for coef in ODD[3::-1]:
        sine = sine * z + coef
    return cosine, sine * t


def neighbours(buf, slot, part, row, first, last):
    mid = [buf[slot, 2 * part + half, pl.ds(row, 8), :] for half in range(2)]
    low = [pltpu.roll(m, 1, 1) for m in mid]
    high = [pltpu.roll(m, 127, 1) for m in mid]
    out = []
    for half in range(2):
        left = jnp.where(first, low[1 - half], low[half])
        right = jnp.where(last, high[1 - half], high[half])
        up = buf[slot, 2 * part + half, pl.ds(row - 1, 8), :]
        down = buf[slot, 2 * part + half, pl.ds(row + 1, 8), :]
        out.append((left + right) + (up + down))
    return mid, out


def lane_masks():
    lane = lax.broadcasted_iota(jnp.int32, (8, 128), 1)
    return lane == 0, lane == 127


def forward_kernel(rows, index_ref, start_ref, field_ref, buf):
    chunks = rows // 8
    pid = pl.program_id(0)
    first, last = lane_masks()

    @pl.when(pid == 0)
    def _():
        buf[...] = jnp.zeros_like(buf)
        for q in range(4):
            buf[0, q, 8 : 8 + rows, :] = start_ref[q // 2, q % 2]

    def step(j, parity, lo, hi):
        for c in range(lo, hi):
            row = 8 + 8 * c
            re, sum_re = neighbours(buf, parity, 0, row, first, last)
            im, sum_im = neighbours(buf, parity, 1, row, first, last)
            for half in range(2):
                cosine, sine = phase_factor(index_ref[j, half, pl.ds(8 * c, 8), :])
                wre = sum_re[half] + (im[half] + im[half])
                wim = sum_im[half] - (re[half] + re[half])
                nre = cosine * wre - sine * wim
                nim = cosine * wim + sine * wre
                buf[1 - parity, half, pl.ds(row, 8), :] = nre
                buf[1 - parity, 2 + half, pl.ds(row, 8), :] = nim
                if half == 0 and chunks // 3 <= c < 2 * chunks // 3:
                    own = 8 * (c - chunks // 3)
                    field_ref[j, 0, pl.ds(own, 8), :] = nre
                    field_ref[j, 1, pl.ds(own, 8), :] = nim

    for k in range(8):

        @pl.when(pid == k)
        def _(k=k):
            @pl.loop(0, GROUP // 2)
            def _(pair):
                step(2 * pair, 0, k, chunks - k)
                step(2 * pair + 1, 1, k, chunks - k)


def backward_kernel(rows, index_ref, start_ref, field_ref, grad_ref, buf):
    chunks = rows // 8
    pid = pl.program_id(0)
    first, last = lane_masks()

    @pl.when(pid == 0)
    def _():
        buf[...] = jnp.zeros_like(buf)

    def finish(j, parity, c, half, are, aim):
        if half == 0 and chunks // 3 <= c < 2 * chunks // 3:
            own = 8 * (c - chunks // 3)
            fre = field_ref[j, 0, pl.ds(own, 8), :]
            fim = field_ref[j, 1, pl.ds(own, 8), :]
            slab = GROUP // 2
            grad_ref[j // slab, 0, j % slab, pl.ds(own, 8), :] = phase_scale * (aim * fre - are * fim)
        cosine, sine = phase_factor(index_ref[j, half, pl.ds(8 * c, 8), :])
        row = 8 + 8 * c
        buf[parity, half, pl.ds(row, 8), :] = cosine * are + sine * aim
        buf[parity, 2 + half, pl.ds(row, 8), :] = cosine * aim - sine * are

    def step(j, parity, lo, hi):
        for c in range(lo, hi):
            row = 8 + 8 * c
            re, sum_re = neighbours(buf, 1 - parity, 0, row, first, last)
            im, sum_im = neighbours(buf, 1 - parity, 1, row, first, last)
            for half in range(2):
                are = sum_re[half] - (im[half] + im[half])
                aim = sum_im[half] + (re[half] + re[half])
                finish(j, parity, c, half, are, aim)

    for k in range(8):

        @pl.when(pid == k)
        def _(k=k):
            skip = 0
            if k == 0:
                skip = 1
                for c in range(chunks):
                    for half in range(2):
                        finish(
                            GROUP - 1,
                            1,
                            c,
                            half,
                            start_ref[0, half, pl.ds(8 * c, 8), :],
                            start_ref[1, half, pl.ds(8 * c, 8), :],
                        )
                step(GROUP - 2, 0, k, chunks - k)

            @pl.loop(skip, GROUP // 2)
            def _(pair):
                step(GROUP - 1 - 2 * pair, 1, k, chunks - k)
                step(GROUP - 2 - 2 * pair, 0, k, chunks - k)


def ring(count, by):
    return [(i, (i + by) % count) for i in range(count)]


def widen(block, axis_x, axis_y):
    n, rows, cols = block.shape
    half = cols // 2
    nx, ny = lax.axis_size(axis_x), lax.axis_size(axis_y)
    pack = lambda v: jnp.concatenate([v[: n // 2], v[n // 2 :]], axis=2)
    unpack = lambda v: jnp.concatenate([v[:, :, :half], v[:, :, half:]], axis=0)
    left = unpack(lax.ppermute(pack(block[:, :, half:]), axis_x, ring(nx, 1)))
    right = unpack(lax.ppermute(pack(block[:, :, :half]), axis_x, ring(nx, -1)))
    wide = jnp.stack([block, jnp.concatenate([right, left], axis=2)], axis=1)
    above = lax.ppermute(wide, axis_y, ring(ny, 1))
    below = lax.ppermute(wide, axis_y, ring(ny, -1))
    return jnp.concatenate([above, wide, below], axis=2)


def with_halo(block, sides, width):
    for axis, dim in sides:
        count = lax.axis_size(axis)
        low = lax.ppermute(
            lax.slice_in_dim(block, block.shape[dim] - width, None, axis=dim), axis, ring(count, 1)
        )
        high = lax.ppermute(lax.slice_in_dim(block, 0, width, axis=dim), axis, ring(count, -1))
        block = jnp.concatenate([low, block, high], axis=dim)
    return block


def smooth(extended, reach, z_first, nz_total):
    length = extended.shape[0]
    base = extended[:-1, :-1, :-1]
    diff_z = extended[1:, :-1, :-1] - base
    diff_y = extended[:-1, 1:, :-1] - base
    diff_x = extended[:-1, :-1, 1:] - base
    depth_pos = (z_first - reach + jnp.arange(length - 1)) % nz_total
    diff_z = jnp.where(depth_pos[:, None, None] == nz_total - 1, 0.0, diff_z)
    scale = lax.rsqrt(
        diff_z * diff_z + diff_y * diff_y + diff_x * diff_x + tv_smooth * tv_smooth
    )
    flux_z = diff_z * scale
    flux_y = diff_y * scale
    flux_x = diff_x * scale
    divergence = (
        flux_z[1:, 1:, 1:]
        - flux_z[:-1, 1:, 1:]
        + flux_y[1:, 1:, 1:]
        - flux_y[1:, :-1, 1:]
        + flux_x[1:, 1:, 1:]
        - flux_x[1:, 1:, :-1]
    )
    return extended[1:-1, 1:-1, 1:-1] + tv_rate * divergence


def body(index, measured, illum):
    slab, rows, cols = index.shape
    depth = lax.axis_size("angle")
    nz = slab * depth
    nx = cols * lax.axis_size("tx")
    ny = rows * lax.axis_size("ty")
    tall = 3 * rows
    core_groups = [[2 * i, 2 * i + 1] for i in range(depth // 2)]
    chip_groups = [list(range(c, depth, 2)) for c in range(2)]

    half = lax.broadcasted_iota(jnp.int32, (2, tall, cols), 0)
    lane = lax.broadcasted_iota(jnp.int32, (2, tall, cols), 2)
    gx = lax.axis_index("tx") * cols + jnp.where(half == 0, lane, jnp.where(lane < cols // 2, lane + cols, lane - cols))
    gy = lax.axis_index("ty") * rows - rows + lax.broadcasted_iota(jnp.int32, (2, tall, cols), 1)
    turns = (illum[0, 0] * gx * (ny // math.gcd(nx, ny)) + illum[0, 1] * gy * (nx // math.gcd(nx, ny)))
    whole = math.lcm(nx, ny)
    turns = lax.rem(lax.rem(turns, whole) + whole, whole)
    q = (2.0 * math.pi / whole) * turns.astype(jnp.float32)
    start = jnp.stack([jnp.cos(q), jnp.sin(q)])

    column = lax.all_gather(widen(index, "tx", "ty"), "angle", axis=0, tiled=True)

    index_block = (GROUP, 2, tall, cols)
    field_block = (GROUP, 2, rows, cols)
    steps = nz // GROUP
    scratch = [pltpu.VMEM((2, 4, tall + 16, cols), jnp.float32)]
    params = pltpu.CompilerParams(dimension_semantics=("arbitrary",), vmem_limit_bytes=40 * 2**20)
    fields = pl.pallas_call(
        functools.partial(forward_kernel, tall),
        grid=(steps,),
        in_specs=[
            pl.BlockSpec(index_block, lambda i: (i, 0, 0, 0)),
            pl.BlockSpec((2, 2, tall, cols), lambda i: (0, 0, 0, 0)),
        ],
        out_specs=pl.BlockSpec(field_block, lambda i: (i, 0, 0, 0)),
        out_shape=jax.ShapeDtypeStruct((nz, 2, rows, cols), jnp.float32),
        scratch_shapes=scratch,
        compiler_params=params,
        name="forward",
    )(column, start)

    back = (TURN.conjugate() ** nz)
    back = back / abs(back)
    target_re = back.real * measured[0] - back.imag * measured[1]
    target_im = back.real * measured[1] + back.imag * measured[0]
    residual = fields[nz - 1] - jnp.concatenate([target_re, target_im], axis=0)
    adjoint = widen(residual, "tx", "ty")

    grads = pl.pallas_call(
        functools.partial(backward_kernel, tall),
        grid=(steps,),
        in_specs=[
            pl.BlockSpec(index_block, lambda i: (steps - 1 - i, 0, 0, 0)),
            pl.BlockSpec((2, 2, tall, cols), lambda i: (0, 0, 0, 0)),
            pl.BlockSpec(field_block, lambda i: (steps - 1 - i, 0, 0, 0)),
        ],
        out_specs=pl.BlockSpec((2, 1, slab, rows, cols), lambda i: (0, steps - 1 - i, 0, 0, 0)),
        out_shape=jax.ShapeDtypeStruct((2, depth // 2, slab, rows, cols), jnp.float32),
        scratch_shapes=scratch,
        compiler_params=params,
        name="backward",
    )(column, adjoint, fields)

    pair = lax.all_to_all(grads, "angle", 0, 0, tiled=True, axis_index_groups=core_groups)
    both = pair[0] + pair[1]
    parts = lax.all_to_all(both, "angle", 0, 0, tiled=True, axis_index_groups=chip_groups)
    gradient = jnp.sum(parts, axis=0)

    volume = index - step_size * gradient
    z_first = lax.axis_index("angle") * slab
    extended = with_halo(volume, (("angle", 0), ("tx", 2), ("ty", 1)), TV_STEPS)
    for turn in range(TV_STEPS):
        extended = smooth(extended, TV_STEPS - turn, z_first, nz)
    return (gradient, extended)


def solution(mesh):
    in_specs = (P("angle", "ty", "tx"), P(None, "angle", "ty", "tx"), P("angle", None))
    out_specs = (P("angle", "ty", "tx"), P("angle", "ty", "tx"))
    return jax.shard_map(body, mesh=mesh, in_specs=in_specs, out_specs=out_specs, check_vma=False)
```

time: 785 us -> 266 us (0.34)
  starting transfers between devices: 260 us -> 50.1 us
  other arithmetic: 166 us -> 11.7 us
  waiting for transfers between devices: 300 us -> 147 us
  local copies, waits for them, and re-layouts: 33.1 us -> 2.19 us
  Pallas kernels: 0 us -> 28.6 us
  blocking collectives: 0 us -> 8.07 us
    ppermute x43 -> x3, starting transfers between devices: 140 us -> 5.43 us  [with_halo(): lax.ppermute(lax.slice_in_dim(block, block.shape[dim] - width, None, axis...]
    ppermute x43 -> x3, waiting for transfers between devices: 122 us -> 7.84 us  [with_halo(): lax.ppermute(lax.slice_in_dim(block, block.shape[dim] - width, None, axis...]
    reduce_scatter x1 -> x0, waiting for transfers between devices: 97.9 us -> none  [body(): lax.psum_scatter(grad_column, 'angle', scatter_dimension=0, tiled=True)]
    another operation x241 -> x5, other arithmetic: 85.1 us -> 1.16 us  [the longest x4 1.13 us: widen(): wide = jnp.stack([block, jnp.concatenate([right, left], axis=2)], axis=1)]
    ppermute x43 -> x11, starting transfers between devices: 120 us -> 40.8 us  [the longest x2 12 us: widen(): right = unpack(lax.ppermute(pack(block[:, :, :half]), axis_x, ring(nx, -1)))]
    sub x201 -> x4, other arithmetic: 54.3 us -> 0.04 us  [the longest x2 0.02 us: body(): residual = fields[nz - 1] - jnp.concatenate([target_re, target_im], axis=0)]
    all_gather x1, waiting for transfers between devices: 49.3 us -> 83.2 us  [body(): lax.all_gather(widen(index, 'tx', 'ty'), 'angle', axis=0, tiled=True)]
    all_to_all x0 -> x1, waiting for transfers between devices: none -> 29.2 us  [body(): lax.all_to_all(both, 'angle', 0, 0, tiled=True, axis_index_groups=chip_gr...]
  transfers between devices with their start and end apart: 88 -> 16, of which waited for: 54 -> 13; matrix products, arithmetic and copies ran while one was open for 3% -> 1% of each run, Pallas kernels for 0% -> 0%
where the time goes in v1:
time: 266 us; the launch traced here: 262 us
  waiting for transfers between devices  147 us (55%)
  starting transfers between devices  50.1 us (19%)
  Pallas kernels  28.6 us (11%)
  between operations  14.4 us (5%)
  other arithmetic  11.7 us (4%)
  blocking collectives  8.07 us (3%)
    all_gather x1, waiting for transfers between devices, body(): lax.all_gather(widen(index, 'tx', 'ty'), 'angle', axis=0, tiled=True)  83.2 us
    all_to_all x1, waiting for transfers between devices, body(): lax.all_to_all(both, 'angle', 0, 0, tiled=True, axis_index_groups=chip_gr...  29.2 us
    pallas_call x1, Pallas kernels, body(): pl.pallas_call(functools.partial(backward_kernel, tall), grid=(steps,), i...  14.4 us
    pallas_call x1, Pallas kernels, body(): pl.pallas_call(functools.partial(forward_kernel, tall), grid=(steps,), in...  14.2 us
    ppermute x2, starting transfers between devices, widen(): right = unpack(lax.ppermute(pack(block[:, :, :half]), axis_x, ring(nx, -1)))  12 us
    ppermute x3, waiting for transfers between devices, with_halo(): lax.ppermute(lax.slice_in_dim(block, 0, width, axis=dim), axis, ring(coun...  11.6 us
    ppermute x2, waiting for transfers between devices, widen(): left = unpack(lax.ppermute(pack(block[:, :, half:]), axis_x, ring(nx, 1)))  10.2 us
    ppermute x3, starting transfers between devices, with_halo(): lax.ppermute(lax.slice_in_dim(block, 0, width, axis=dim), axis, ring(coun...  10.2 us
  transfers between devices with their start and end apart: 16, of which 13 were waited for; matrix products, arithmetic and copies ran while one was open for 1% of the time, Pallas kernels for 0%

profile of v1, /device:TPU:1, one launch (start us, length us, event | category | flops | bytes accessed | tf_op | source)
XLA Modules:
  0.0 262.3 jit_solution(14566253452026891062)
XLA Ops:
  7.2 0.0 all-gather.2.cloned.1.call-start
  7.2 1.0 fusion.34
  8.3 0.1 pad_maximum_fusion.7
  8.4 6.7 %collective-permute-start = (f32[2,64,128]{2,1,0:T(8,128)S(1)}, f32[2,64,128]{2,1,0:T(8,128)S(1)}, u32[]{:S(2)}, u32[]{:S(2)}) collective-permute-start(f32[2,64,128]{2,1,0:T(8,128)S(1)} %pad_maximum_fusion.7), channel_id=1, source_target_pairs={{0,24},{8,0},{16,8},{24,16},{1,25},{9,1},{17,9},{25,17},{2,26},{10... | collective-permute-start | bytes 196616 | tf_op jit(solution)/shard_map/ppermute | solution.py:178
  15.1 0.1 pad_maximum_fusion.8
  15.2 1.9 collective-permute-start.1
  17.1 0.1 fusion.36
  17.2 5.4 %collective-permute-done.1 = f32[2,64,128]{2,1,0:T(8,128)S(1)} collective-permute-done((f32[2,64,128]{2,1,0:T(8,128)S(1)}, f32[2,64,128]{2,1,0:T(8,128)S(1)}, u32[]{:S(2)}, u32[]{:S(2)}) %collective-permute-start.1) | collective-permute-done | bytes 65568 | tf_op jit(solution)/shard_map/ppermute | solution.py:177
  22.6 0.1 fusion.37
  22.7 0.1 maximum_bitcast_fusion
  22.8 0.9 pad_maximum_fusion.5
  23.7 3.1 %collective-permute-start.2 = (f32[4,2,64,128]{3,2,1,0:T(8,128)S(1)}, f32[4,2,64,128]{3,2,1,0:T(8,128)S(1)}, u32[]{:S(2)}, u32[]{:S(2)}) collective-permute-start(f32[4,2,64,128]{3,2,1,0:T(8,128)S(1)} %pad_maximum_fusion.5), channel_id=1, source_target_pairs={{0,1},{1,2},{2,3},{3,4},{4,5},{5,6},{6,7},{7,0},{8,9},{9,10},{10,1... | collective-permute-start | bytes 786440 | tf_op jit(solution)/shard_map/ppermute | solution.py:180
  26.9 4.3 %collective-permute-start.3 = (f32[4,2,64,128]{3,2,1,0:T(8,128)S(1)}, f32[4,2,64,128]{3,2,1,0:T(8,128)S(1)}, u32[]{:S(2)}, u32[]{:S(2)}) collective-permute-start(f32[4,2,64,128]{3,2,1,0:T(8,128)S(1)} %pad_maximum_fusion.5), channel_id=1, source_target_pairs={{0,7},{1,0},{2,1},{3,2},{4,3},{5,4},{6,5},{7,6},{8,15},{9,8},{10,9... | collective-permute-start | bytes 786440 | tf_op jit(solution)/shard_map/ppermute | solution.py:181
  31.1 1.8 collective-permute-done.2
  32.9 1.5 collective-permute-done.3
  34.4 1.9 pad_maximum_fusion
  36.3 0.0 all-gather.2.cloned.1.call-update
  36.4 0.6 fusion.40
  37.0 0.6 add_multiply_fusion
  37.6 1.5 fusion.22
  39.2 83.2 %all-gather.2.cloned.1.call-done.index_ref = f32[64,2,192,128]{3,2,1,0:T(8,128)} async-done(((f32[4,2,192,128]{3,2,1,0:T(8,128)}), f32[64,2,192,128]{3,2,1,0:T(8,128)}) %all-gather.2.cloned.1.call-update) | async-done | bytes 12582928 | tf_op jit(solution)/shard_map/all_gather | solution.py:241
  122.3 14.2 %forward.1.field_ref = f32[64,2,64,128]{3,2,1,0:T(8,128)S(1)} custom-call(f32[64,2,192,128]{3,2,1,0:T(8,128)} %all-gather.2.cloned.1.call-done.index_ref, f32[2,2,192,128]{3,2,1,0:T(8,128)S(1)} %pad_maximum_fusion.2.start_ref), custom_call_target="tpu_custom_call" | custom-call | tf_op jit(solution)/shard_map/forward/pallas_call | solution.py:248
  136.6 0.1 fusion.35
  136.7 0.1 pad_maximum_fusion.14
  136.7 5.3 %collective-permute-start.4 = (f32[1,64,128]{2,1,0:T(8,128)S(1)}, f32[1,64,128]{2,1,0:T(8,128)S(1)}, u32[]{:S(2)}, u32[]{:S(2)}) collective-permute-start(f32[1,64,128]{2,1,0:T(8,128)S(1)} %pad_maximum_fusion.14), channel_id=1, source_target_pairs={{0,24},{8,0},{16,8},{24,16},{1,25},{9,1},{17,9},{25,17},{2,26},{10... | collective-permute-start | bytes 98312 | tf_op jit(solution)/shard_map/ppermute | solution.py:178
  142.1 0.1 pad_maximum_fusion.15
  142.2 1.9 collective-permute-start.5
  144.1 0.1 fusion.38
  144.2 4.8 %collective-permute-done.5 = f32[1,64,128]{2,1,0:T(8,128)S(1)} collective-permute-done((f32[1,64,128]{2,1,0:T(8,128)S(1)}, f32[1,64,128]{2,1,0:T(8,128)S(1)}, u32[]{:S(2)}, u32[]{:S(2)}) %collective-permute-start.5) | collective-permute-done | bytes 32800 | tf_op jit(solution)/shard_map/ppermute | solution.py:177
  149.0 0.1 fusion.39
  149.0 0.1 maximum_bitcast_fusion.1
  149.2 3.1 %collective-permute-start.6 = (f32[2,2,64,128]{3,2,1,0:T(8,128)S(1)}, f32[2,2,64,128]{3,2,1,0:T(8,128)S(1)}, u32[]{:S(2)}, u32[]{:S(2)}) collective-permute-start(f32[2,2,64,128]{3,2,1,0:T(8,128)S(1)} %pad_maximum_fusion.6), channel_id=1, source_target_pairs={{0,1},{1,2},{2,3},{3,4},{4,5},{5,6},{6,7},{7,0},{8,9},{9,10},{10,1... | collective-permute-start | bytes 393224 | tf_op jit(solution)/shard_map/ppermute | solution.py:180
  152.3 4.3 %collective-permute-start.7 = (f32[2,2,64,128]{3,2,1,0:T(8,128)S(1)}, f32[2,2,64,128]{3,2,1,0:T(8,128)S(1)}, u32[]{:S(2)}, u32[]{:S(2)}) collective-permute-start(f32[2,2,64,128]{3,2,1,0:T(8,128)S(1)} %pad_maximum_fusion.6), channel_id=1, source_target_pairs={{0,7},{1,0},{2,1},{3,2},{4,3},{5,4},{6,5},{7,6},{8,15},{9,8},{10,9... | collective-permute-start | bytes 393224 | tf_op jit(solution)/shard_map/ppermute | solution.py:181
  156.6 0.4 collective-permute-done.6
  157.0 1.5 collective-permute-done.7
  158.5 14.4 %backward.1 = f32[2,8,4,64,128]{4,3,2,1,0:T(8,128)S(1)} custom-call(f32[64,2,192,128]{3,2,1,0:T(8,128)} %all-gather.2.cloned.1.call-done.index_ref, f32[2,2,192,128]{3,2,1,0:T(8,128)S(1)} %pad_maximum_fusion.3.start_ref, f32[64,2,64,128]{3,2,1,0:T(8,128)S(1)} %forward.1.field_ref), custom_call_target="tpu_custom_call" | custom-call | tf_op jit(solution)/shard_map/backward/pallas_call | solution.py:269
  172.9 8.1 %all_to_all.10 = f32[2,8,4,64,128]{4,3,2,1,0:T(8,128)S(1)} all-to-all(f32[2,8,4,64,128]{4,3,2,1,0:T(8,128)S(1)} %backward.1), channel_id=1, replica_groups={{0,32},{64,96},{128,160},{192,224},{256,288},{320,352},{384,416},{448,4..., dimensions={0} | all-to-all | bytes 4194304 | tf_op jit(solution)/shard_map/all_to_all | solution.py:284
  181.0 1.1 fusion
  182.1 3.8 %all-to-all-start.1 = ((f32[8,4,64,128]{3,2,1,0:T(8,128)}), f32[8,4,64,128]{3,2,1,0:T(8,128)S(1)}, u32[]{:S(2)}, u32[]{:S(2)}) async-start(f32[8,4,64,128]{3,2,1,0:T(8,128)} %fusion), calls=%async_computation.1 | async-start | bytes 2097152 | tf_op jit(solution)/shard_map/all_to_all | solution.py:286
  185.8 29.2 %all-to-all-done.1 = f32[8,4,64,128]{3,2,1,0:T(8,128)S(1)} async-done(((f32[8,4,64,128]{3,2,1,0:T(8,128)}), f32[8,4,64,128]{3,2,1,0:T(8,128)S(1)}, u32[]{:S(2)}, u32[]{:S(2)}) %all-to-all-start.1) | async-done | bytes 1048608 | tf_op jit(solution)/shard_map/all_to_all | solution.py:286
  215.1 0.1 reduce_sum.9
  215.2 0.0 copy-start.1
  215.2 0.6 collective-permute-start.8
  215.9 1.6 collective-permute-done.8
  217.5 2.7 %collective-permute-done.9 = f32[3,64,128]{2,1,0:T(8,128)S(1)} collective-permute-done((f32[3,64,128]{2,1,0:T(8,128)S(1)}, f32[3,64,128]{2,1,0:T(8,128)S(1)}, u32[]{:S(2)}, u32[]{:S(2)}) %collective-permute-start.9) | collective-permute-done | bytes 98336 | tf_op jit(solution)/shard_map/ppermute | solution.py:191
  220.2 0.2 fusion.32
  220.4 1.9 collective-permute-start.10
  222.3 5.5 %collective-permute-start.11 = (f32[10,64,3]{2,1,0:T(8,128)S(1)}, f32[10,64,3]{2,1,0:T(8,128)S(1)}, u32[]{:S(2)}, u32[]{:S(2)}) collective-permute-start(f32[10,64,3]{2,1,0:T(8,128)S(1)} %get-tuple-element.17), channel_id=1, source_target_pairs={{0,24},{8,0},{16,8},{24,16},{1,25},{9,1},{17,9},{25,17},{2,26},{10... | collective-permute-start | bytes 23048 | tf_op jit(solution)/shard_map/ppermute | solution.py:191
  227.8 6.2 %collective-permute-done.10 = f32[10,64,3]{2,1,0:T(8,128)S(1)} collective-permute-done((f32[10,64,3]{2,1,0:T(8,128)S(1)}, f32[10,64,3]{2,1,0:T(8,128)S(1)}, u32[]{:S(2)}, u32[]{:S(2)}) %collective-permute-start.10) | collective-permute-done | bytes 7712 | tf_op jit(solution)/shard_map/ppermute | solution.py:188
  234.0 8.0 %collective-permute-done.11 = f32[10,64,3]{2,1,0:T(8,128)S(1)} collective-permute-done((f32[10,64,3]{2,1,0:T(8,128)S(1)}, f32[10,64,3]{2,1,0:T(8,128)S(1)}, u32[]{:S(2)}, u32[]{:S(2)}) %collective-permute-start.11) | collective-permute-done | bytes 7712 | tf_op jit(solution)/shard_map/ppermute | solution.py:191
  242.0 0.1 pad_maximum_fusion.13
  242.2 2.9 %collective-permute-start.12 = (f32[10,3,134]{2,1,0:T(4,128)S(1)}, f32[10,3,134]{2,1,0:T(4,128)S(1)}, u32[]{:S(2)}, u32[]{:S(2)}) collective-permute-start(f32[10,3,134]{2,1,0:T(4,128)S(1)} %get-tuple-element.12), channel_id=1, source_target_pairs={{0,1},{1,2},{2,3},{3,4},{4,5},{5,6},{6,7},{7,0},{8,9},{9,10},{10,1... | collective-permute-start | bytes 48248 | tf_op jit(solution)/shard_map/ppermute | solution.py:188
  245.1 4.7 %collective-permute-start.13 = (f32[10,3,134]{2,1,0:T(4,128)S(1)}, f32[10,3,134]{2,1,0:T(4,128)S(1)}, u32[]{:S(2)}, u32[]{:S(2)}) collective-permute-start(f32[10,3,134]{2,1,0:T(4,128)S(1)} %get-tuple-element.13), channel_id=1, source_target_pairs={{0,7},{1,0},{2,1},{3,2},{4,3},{5,4},{6,5},{7,6},{8,15},{9,8},{10,9... | collective-permute-start | bytes 48248 | tf_op jit(solution)/shard_map/ppermute | solution.py:191
  249.8 0.9 collective-permute-done.13
  250.7 0.4 pad_maximum_fusion.1
  251.0 0.4 fusion.23
  251.4 0.3 fusion.8
  251.7 1.0 fusion.3
  252.7 0.3 fusion.24
  253.1 0.2 fusion.15
  253.3 0.8 fusion.6
  254.1 0.2 fusion.25
  254.3 0.2 fusion.19
  254.5 0.9 fusion.18
  (26 shorter events, 0.2 us)
Async XLA Ops:
  7.2 29.2 %copy-start.3 = (s32[1,2]{1,0:T(1,128)S(1)}, s32[1,2]{1,0:T(1,128)}, u32[]{:S(2)}) copy-start(s32[1,2]{1,0:T(1,128)} %param.5) | copy-start | bytes 28
  7.2 32.0 %copy-start.2 = (f32[2,1,64,128]{3,2,1,0:T(8,128)S(1)}, f32[2,1,64,128]{3,2,1,0:T(8,128)}, u32[]{:S(2)}) copy-start(f32[2,1,64,128]{3,2,1,0:T(8,128)} %param.4) | copy-start | bytes 196612
  7.2 115.2 %all-gather.2.cloned.1.call-start = ((), (), s32[]{:S(2)}) async-start(), calls=%async_computation.2 | async-start | bytes 13369344 | tf_op jit(solution)/shard_map/all_gather | solution.py:241
  8.4 8.7 %collective-permute-start = (f32[2,64,128]{2,1,0:T(8,128)S(1)}, f32[2,64,128]{2,1,0:T(8,128)S(1)}, u32[]{:S(2)}, u32[]{:S(2)}) collective-permute-start(f32[2,64,128]{2,1,0:T(8,128)S(1)} %pad_maximum_fusion.7), channel_id=1, source_target_pairs={{0,24},{8,0},{16,8},{24,16},{1,25},{9,1},{17,9},{25,17},{2,26},{10... | collective-permute-start | bytes 196616 | tf_op jit(solution)/shard_map/ppermute | solution.py:178
  15.2 7.4 %collective-permute-start.1 = (f32[2,64,128]{2,1,0:T(8,128)S(1)}, f32[2,64,128]{2,1,0:T(8,128)S(1)}, u32[]{:S(2)}, u32[]{:S(2)}) collective-permute-start(f32[2,64,128]{2,1,0:T(8,128)S(1)} %pad_maximum_fusion.8), channel_id=1, source_target_pairs={{0,8},{8,16},{16,24},{24,0},{1,9},{9,17},{17,25},{25,1},{2,10},{10... | collective-permute-start | bytes 196616 | tf_op jit(solution)/shard_map/ppermute | solution.py:177
  23.7 9.2 %collective-permute-start.2 = (f32[4,2,64,128]{3,2,1,0:T(8,128)S(1)}, f32[4,2,64,128]{3,2,1,0:T(8,128)S(1)}, u32[]{:S(2)}, u32[]{:S(2)}) collective-permute-start(f32[4,2,64,128]{3,2,1,0:T(8,128)S(1)} %pad_maximum_fusion.5), channel_id=1, source_target_pairs={{0,1},{1,2},{2,3},{3,4},{4,5},{5,6},{6,7},{7,0},{8,9},{9,10},{10,1... | collective-permute-start | bytes 786440 | tf_op jit(solution)/shard_map/ppermute | solution.py:180
  26.9 7.6 %collective-permute-start.3 = (f32[4,2,64,128]{3,2,1,0:T(8,128)S(1)}, f32[4,2,64,128]{3,2,1,0:T(8,128)S(1)}, u32[]{:S(2)}, u32[]{:S(2)}) collective-permute-start(f32[4,2,64,128]{3,2,1,0:T(8,128)S(1)} %pad_maximum_fusion.5), channel_id=1, source_target_pairs={{0,7},{1,0},{2,1},{3,2},{4,3},{5,4},{6,5},{7,6},{8,15},{9,8},{10,9... | collective-permute-start | bytes 786440 | tf_op jit(solution)/shard_map/ppermute | solution.py:181
  136.7 7.3 %collective-permute-start.4 = (f32[1,64,128]{2,1,0:T(8,128)S(1)}, f32[1,64,128]{2,1,0:T(8,128)S(1)}, u32[]{:S(2)}, u32[]{:S(2)}) collective-permute-start(f32[1,64,128]{2,1,0:T(8,128)S(1)} %pad_maximum_fusion.14), channel_id=1, source_target_pairs={{0,24},{8,0},{16,8},{24,16},{1,25},{9,1},{17,9},{25,17},{2,26},{10... | collective-permute-start | bytes 98312 | tf_op jit(solution)/shard_map/ppermute | solution.py:178
  142.2 6.8 %collective-permute-start.5 = (f32[1,64,128]{2,1,0:T(8,128)S(1)}, f32[1,64,128]{2,1,0:T(8,128)S(1)}, u32[]{:S(2)}, u32[]{:S(2)}) collective-permute-start(f32[1,64,128]{2,1,0:T(8,128)S(1)} %pad_maximum_fusion.15), channel_id=1, source_target_pairs={{0,8},{8,16},{16,24},{24,0},{1,9},{9,17},{17,25},{25,1},{2,10},{10... | collective-permute-start | bytes 98312 | tf_op jit(solution)/shard_map/ppermute | solution.py:177
  149.2 7.8 %collective-permute-start.6 = (f32[2,2,64,128]{3,2,1,0:T(8,128)S(1)}, f32[2,2,64,128]{3,2,1,0:T(8,128)S(1)}, u32[]{:S(2)}, u32[]{:S(2)}) collective-permute-start(f32[2,2,64,128]{3,2,1,0:T(8,128)S(1)} %pad_maximum_fusion.6), channel_id=1, source_target_pairs={{0,1},{1,2},{2,3},{3,4},{4,5},{5,6},{6,7},{7,0},{8,9},{9,10},{10,1... | collective-permute-start | bytes 393224 | tf_op jit(solution)/shard_map/ppermute | solution.py:180
  152.3 6.2 %collective-permute-start.7 = (f32[2,2,64,128]{3,2,1,0:T(8,128)S(1)}, f32[2,2,64,128]{3,2,1,0:T(8,128)S(1)}, u32[]{:S(2)}, u32[]{:S(2)}) collective-permute-start(f32[2,2,64,128]{3,2,1,0:T(8,128)S(1)} %pad_maximum_fusion.6), channel_id=1, source_target_pairs={{0,7},{1,0},{2,1},{3,2},{4,3},{5,4},{6,5},{7,6},{8,15},{9,8},{10,9... | collective-permute-start | bytes 393224 | tf_op jit(solution)/shard_map/ppermute | solution.py:181
  181.0 34.2 %copy-start = (f32[4,64,128]{2,1,0:T(8,128)S(1)}, f32[4,64,128]{2,1,0:T(8,128)}, u32[]{:S(2)}) copy-start(f32[4,64,128]{2,1,0:T(8,128)} %param.3) | copy-start | bytes 393220
  182.1 33.0 %all-to-all-start.1 = ((f32[8,4,64,128]{3,2,1,0:T(8,128)}), f32[8,4,64,128]{3,2,1,0:T(8,128)S(1)}, u32[]{:S(2)}, u32[]{:S(2)}) async-start(f32[8,4,64,128]{3,2,1,0:T(8,128)} %fusion), calls=%async_computation.1 | async-start | bytes 2097152 | tf_op jit(solution)/shard_map/all_to_all | solution.py:286
  215.2 36.3 %copy-start.1 = (f32[4,64,128]{2,1,0:T(8,128)}, f32[4,64,128]{2,1,0:T(8,128)S(1)}, u32[]{:S(2)}) copy-start(f32[4,64,128]{2,1,0:T(8,128)S(1)} %reduce_sum.9) | copy-start | bytes 393220
  215.2 2.3 collective-permute-start.8
  215.8 4.3 %collective-permute-start.9 = (f32[3,64,128]{2,1,0:T(8,128)S(1)}, f32[3,64,128]{2,1,0:T(8,128)S(1)}, u32[]{:S(2)}, u32[]{:S(2)}) collective-permute-start(f32[3,64,128]{2,1,0:T(8,128)S(1)} %get-tuple-element.19), channel_id=1, source_target_pairs={{0,480},{32,0},{64,32},{96,64},{128,96},{160,128},{192,160},{224,1... | collective-permute-start | bytes 294920 | tf_op jit(solution)/shard_map/ppermute | solution.py:191
  220.4 13.6 %collective-permute-start.10 = (f32[10,64,3]{2,1,0:T(8,128)S(1)}, f32[10,64,3]{2,1,0:T(8,128)S(1)}, u32[]{:S(2)}, u32[]{:S(2)}) collective-permute-start(f32[10,64,3]{2,1,0:T(8,128)S(1)} %get-tuple-element.16), channel_id=1, source_target_pairs={{0,8},{8,16},{16,24},{24,0},{1,9},{9,17},{17,25},{25,1},{2,10},{10... | collective-permute-start | bytes 23048 | tf_op jit(solution)/shard_map/ppermute | solution.py:188
  222.3 19.7 %collective-permute-start.11 = (f32[10,64,3]{2,1,0:T(8,128)S(1)}, f32[10,64,3]{2,1,0:T(8,128)S(1)}, u32[]{:S(2)}, u32[]{:S(2)}) collective-permute-start(f32[10,64,3]{2,1,0:T(8,128)S(1)} %get-tuple-element.17), channel_id=1, source_target_pairs={{0,24},{8,0},{16,8},{24,16},{1,25},{9,1},{17,9},{25,17},{2,26},{10... | collective-permute-start | bytes 23048 | tf_op jit(solution)/shard_map/ppermute | solution.py:191
  242.2 7.6 %collective-permute-start.12 = (f32[10,3,134]{2,1,0:T(4,128)S(1)}, f32[10,3,134]{2,1,0:T(4,128)S(1)}, u32[]{:S(2)}, u32[]{:S(2)}) collective-permute-start(f32[10,3,134]{2,1,0:T(4,128)S(1)} %get-tuple-element.12), channel_id=1, source_target_pairs={{0,1},{1,2},{2,3},{3,4},{4,5},{5,6},{6,7},{7,0},{8,9},{9,10},{10,1... | collective-permute-start | bytes 48248 | tf_op jit(solution)/shard_map/ppermute | solution.py:188
  245.1 5.6 %collective-permute-start.13 = (f32[10,3,134]{2,1,0:T(4,128)S(1)}, f32[10,3,134]{2,1,0:T(4,128)S(1)}, u32[]{:S(2)}, u32[]{:S(2)}) collective-permute-start(f32[10,3,134]{2,1,0:T(4,128)S(1)} %get-tuple-element.13), channel_id=1, source_target_pairs={{0,7},{1,0},{2,1},{3,2},{4,3},{5,4},{6,5},{7,6},{8,15},{9,8},{10,9... | collective-permute-start | bytes 48248 | tf_op jit(solution)/shard_map/ppermute | solution.py:191
Sparse Core Ops, SparseCore 0:
  36.4 85.8 all-gather.1

commit v2 on v1

--- a/solution.py
+++ b/solution.py
@@ -30,9 +30,9 @@
     t = 3.05 * (nodes + 1.0)
     z = t * t
     scaled = z / z.max()
-    even = np.linalg.lstsq(scaled[:, None] ** np.arange(5), GAIN * np.cos(phase_scale * t), rcond=None)[0]
-    odd = np.linalg.lstsq(scaled[:, None] ** np.arange(5), GAIN * np.sin(phase_scale * t) / t, rcond=None)[0]
-    powers = z.max() ** np.arange(5)
+    even = np.linalg.lstsq(scaled[:, None] ** np.arange(4), GAIN * np.cos(phase_scale * t), rcond=None)[0]
+    odd = np.linalg.lstsq(scaled[:, None] ** np.arange(4), GAIN * np.sin(phase_scale * t) / t, rcond=None)[0]
+    powers = z.max() ** np.arange(4)
     return [float(v) for v in even / powers], [float(v) for v in odd / powers]
 
 
@@ -41,11 +41,11 @@
 
 def phase_factor(t):
     z = t * t
-    cosine = EVEN[4]
-    for coef in EVEN[3::-1]:
+    cosine = EVEN[3]
+    for coef in EVEN[2::-1]:
         cosine = cosine * z + coef
-    sine = ODD[4]
-    for coef in ODD[3::-1]:
+    sine = ODD[3]
+    for coef in ODD[2::-1]:
         sine = sine * z + coef
     return cosine, sine * t
 
@@ -64,6 +64,17 @@
     return mid, out
 
 
+def index_rows(index_ref, j, half, c, chunks):
+    third = chunks // 3
+    if half == 0:
+        return index_ref[j, pl.ds(8 * c, 8), :]
+    if c < third:
+        return index_ref[j, pl.ds(8 * (4 * third + c), 8), :]
+    if c < 2 * third:
+        return index_ref[j, pl.ds(8 * (2 * third + c), 8), :]
+    return pltpu.roll(index_ref[j, pl.ds(8 * (2 * third + c), 8), :], 64, 1)
+
+
 def lane_masks():
     lane = lax.broadcasted_iota(jnp.int32, (8, 128), 1)
     return lane == 0, lane == 127
@@ -86,7 +97,7 @@
             re, sum_re = neighbours(buf, parity, 0, row, first, last)
             im, sum_im = neighbours(buf, parity, 1, row, first, last)
             for half in range(2):
-                cosine, sine = phase_factor(index_ref[j, half, pl.ds(8 * c, 8), :])
+                cosine, sine = phase_factor(index_rows(index_ref, j, half, c, chunks))
                 wre = sum_re[half] + (im[half] + im[half])
                 wim = sum_im[half] - (re[half] + re[half])
                 nre = cosine * wre - sine * wim
@@ -124,7 +135,7 @@
             fim = field_ref[j, 1, pl.ds(own, 8), :]
             slab = GROUP // 2
             grad_ref[j // slab, 0, j % slab, pl.ds(own, 8), :] = phase_scale * (aim * fre - are * fim)
-        cosine, sine = phase_factor(index_ref[j, half, pl.ds(8 * c, 8), :])
+        cosine, sine = phase_factor(index_rows(index_ref, j, half, c, chunks))
         row = 8 + 8 * c
         buf[parity, half, pl.ds(row, 8), :] = cosine * are + sine * aim
         buf[parity, 2 + half, pl.ds(row, 8), :] = cosine * aim - sine * are
@@ -179,7 +190,16 @@
     wide = jnp.stack([block, jnp.concatenate([right, left], axis=2)], axis=1)
     above = lax.ppermute(wide, axis_y, ring(ny, 1))
     below = lax.ppermute(wide, axis_y, ring(ny, -1))
-    return jnp.concatenate([above, wide, below], axis=2)
+    return above, wide, below
+
+
+def pack_corners(above, wide, below):
+    _, _, rows, cols = wide.shape
+    lane = lax.broadcasted_iota(jnp.int32, (rows, cols), 1)
+    away = jnp.where(lane < cols // 2, lane + 1, cols - lane)
+    from_above = away <= lax.broadcasted_iota(jnp.int32, (rows, cols), 0)
+    corners = jnp.where(from_above, above[:, 1], jnp.roll(below[:, 1], cols // 2, axis=2))
+    return jnp.concatenate([above[:, 0], wide[:, 0], below[:, 0], wide[:, 1], corners], axis=1)
 
 
 def with_halo(block, sides, width):
@@ -238,9 +258,9 @@
     q = (2.0 * math.pi / whole) * turns.astype(jnp.float32)
     start = jnp.stack([jnp.cos(q), jnp.sin(q)])
 
-    column = lax.all_gather(widen(index, "tx", "ty"), "angle", axis=0, tiled=True)
-
-    index_block = (GROUP, 2, tall, cols)
+    column = lax.all_gather(pack_corners(*widen(index, "tx", "ty")), "angle", axis=0, tiled=True)
+
+    index_block = (GROUP, 5 * rows, cols)
     field_block = (GROUP, 2, rows, cols)
     steps = nz // GROUP
     scratch = [pltpu.VMEM((2, 4, tall + 16, cols), jnp.float32)]
@@ -249,7 +269,7 @@
         functools.partial(forward_kernel, tall),
         grid=(steps,),
         in_specs=[
-            pl.BlockSpec(index_block, lambda i: (i, 0, 0, 0)),
+            pl.BlockSpec(index_block, lambda i: (i, 0, 0)),
             pl.BlockSpec((2, 2, tall, cols), lambda i: (0, 0, 0, 0)),
         ],
         out_specs=pl.BlockSpec(field_block, lambda i: (i, 0, 0, 0)),
@@ -264,13 +284,13 @@
     target_re = back.real * measured[0] - back.imag * measured[1]
     target_im = back.real * measured[1] + back.imag * measured[0]
     residual = fields[nz - 1] - jnp.concatenate([target_re, target_im], axis=0)
-    adjoint = widen(residual, "tx", "ty")
+    adjoint = jnp.concatenate(widen(residual, "tx", "ty"), axis=2)
 
     grads = pl.pallas_call(
         functools.partial(backward_kernel, tall),
         grid=(steps,),
         in_specs=[
-            pl.BlockSpec(index_block, lambda i: (steps - 1 - i, 0, 0, 0)),
+            pl.BlockSpec(index_block, lambda i: (steps - 1 - i, 0, 0)),
             pl.BlockSpec((2, 2, tall, cols), lambda i: (0, 0, 0, 0)),
             pl.BlockSpec(field_block, lambda i: (steps - 1 - i, 0, 0, 0)),
         ],

time: 266 us -> 255 us (0.959)
  waiting for transfers between devices: 147 us -> 136 us
    all_gather x1, waiting for transfers between devices: 83.2 us -> 73.3 us  [body(): lax.all_gather(pack_corners(*widen(index, 'tx', 'ty')), 'angle', axis=0,...]
  transfers between devices with their start and end apart: 16 -> 16, of which waited for: 13 -> 13; matrix products, arithmetic and copies ran while one was open for 1% -> 2% of each run, Pallas kernels for 0% -> 0%
where the time goes in v2:
time: 255 us; the launch traced here: 251 us
  waiting for transfers between devices  136 us (53%)
  starting transfers between devices  50.1 us (20%)
  Pallas kernels  27.7 us (11%)
  between operations  14.5 us (6%)
  other arithmetic  10.1 us (4%)
  blocking collectives  8.07 us (3%)
  local copies, waits for them, and re-layouts  4.06 us (2%)
    all_gather x1, waiting for transfers between devices, body(): lax.all_gather(pack_corners(*widen(index, 'tx', 'ty')), 'angle', axis=0,...  73.3 us
    all_to_all x1, waiting for transfers between devices, body(): lax.all_to_all(both, 'angle', 0, 0, tiled=True, axis_index_groups=chip_gr...  29.2 us
    pallas_call x1, Pallas kernels, body(): pl.pallas_call(functools.partial(backward_kernel, tall), grid=(steps,), i...  13.9 us
    pallas_call x1, Pallas kernels, body(): pl.pallas_call(functools.partial(forward_kernel, tall), grid=(steps,), in...  13.8 us
    ppermute x2, starting transfers between devices, widen(): right = unpack(lax.ppermute(pack(block[:, :, :half]), axis_x, ring(nx, -1)))  12 us
    ppermute x3, waiting for transfers between devices, with_halo(): lax.ppermute(lax.slice_in_dim(block, 0, width, axis=dim), axis, ring(coun...  11.6 us
    ppermute x2, waiting for transfers between devices, widen(): left = unpack(lax.ppermute(pack(block[:, :, half:]), axis_x, ring(nx, 1)))  10.2 us
    ppermute x3, starting transfers between devices, with_halo(): lax.ppermute(lax.slice_in_dim(block, 0, width, axis=dim), axis, ring(coun...  10.2 us
  transfers between devices with their start and end apart: 16, of which 13 were waited for; matrix products, arithmetic and copies ran while one was open for 2% of the time, Pallas kernels for 0%

profile of v2, /device:TPU:1, one launch (start us, length us, event | category | flops | bytes accessed | tf_op | source)
XLA Modules:
  0.0 250.9 jit_solution(10737113071901598401)
XLA Ops:
  7.2 1.0 fusion.40
  8.3 0.1 pad_maximum_fusion.6
  8.4 6.7 %collective-permute-start = (f32[2,64,128]{2,1,0:T(8,128)S(1)}, f32[2,64,128]{2,1,0:T(8,128)S(1)}, u32[]{:S(2)}, u32[]{:S(2)}) collective-permute-start(f32[2,64,128]{2,1,0:T(8,128)S(1)} %pad_maximum_fusion.6), channel_id=1, source_target_pairs={{0,24},{8,0},{16,8},{24,16},{1,25},{9,1},{17,9},{25,17},{2,26},{10... | collective-permute-start | bytes 196616 | tf_op jit(solution)/shard_map/ppermute | solution.py:189
  15.1 0.1 pad_maximum_fusion.7
  15.2 1.9 collective-permute-start.1
  17.1 0.1 fusion.42
  17.2 5.4 %collective-permute-done.1 = f32[2,64,128]{2,1,0:T(8,128)S(1)} collective-permute-done((f32[2,64,128]{2,1,0:T(8,128)S(1)}, f32[2,64,128]{2,1,0:T(8,128)S(1)}, u32[]{:S(2)}, u32[]{:S(2)}) %collective-permute-start.1) | collective-permute-done | bytes 65568 | tf_op jit(solution)/shard_map/ppermute | solution.py:188
  22.6 0.1 fusion.43
  22.7 0.1 fusion.29
  22.8 0.9 pad_maximum_fusion.4
  23.7 3.1 %collective-permute-start.2 = (f32[4,2,64,128]{3,2,0,1:T(8,128)S(1)}, f32[4,2,64,128]{3,2,0,1:T(8,128)S(1)}, u32[]{:S(2)}, u32[]{:S(2)}) collective-permute-start(f32[4,2,64,128]{3,2,0,1:T(8,128)S(1)} %pad_maximum_fusion.4), channel_id=1, source_target_pairs={{0,1},{1,2},{2,3},{3,4},{4,5},{5,6},{6,7},{7,0},{8,9},{9,10},{10,1... | collective-permute-start | bytes 786440 | tf_op jit(solution)/shard_map/ppermute | solution.py:191
  26.9 4.3 %collective-permute-start.3 = (f32[4,2,64,128]{3,2,0,1:T(8,128)S(1)}, f32[4,2,64,128]{3,2,0,1:T(8,128)S(1)}, u32[]{:S(2)}, u32[]{:S(2)}) collective-permute-start(f32[4,2,64,128]{3,2,0,1:T(8,128)S(1)} %pad_maximum_fusion.4), channel_id=1, source_target_pairs={{0,7},{1,0},{2,1},{3,2},{4,3},{5,4},{6,5},{7,6},{8,15},{9,8},{10,9... | collective-permute-start | bytes 786440 | tf_op jit(solution)/shard_map/ppermute | solution.py:192
  31.2 1.8 collective-permute-done.2
  33.0 0.9 constant_dynamic-update-slice_fusion.1
  33.9 0.6 collective-permute-done.3
  34.5 0.1 constant_dynamic-update-slice_fusion
  34.6 0.1 fusion.39
  34.7 0.1 fusion.20
  34.8 0.8 copy-done.1
  35.7 0.6 fusion.46
  36.3 0.6 add_multiply_fusion
  37.0 1.5 fusion.26
  38.5 73.3 %all-gather.2.cloned.1.call-done.index_ref = f32[64,320,128]{2,1,0:T(8,128)} async-done(((f32[4,320,128]{2,1,0:T(8,128)}), f32[64,320,128]{2,1,0:T(8,128)}) %all-gather.2.cloned.1.call-update) | async-done | bytes 10485776 | tf_op jit(solution)/shard_map/all_gather | solution.py:261
  111.8 13.8 %forward.1.field_ref = f32[64,2,64,128]{3,2,1,0:T(8,128)S(1)} custom-call(f32[64,320,128]{2,1,0:T(8,128)} %all-gather.2.cloned.1.call-done.index_ref, f32[2,2,192,128]{3,2,1,0:T(8,128)S(1)} %pad_maximum_fusion.1.start_ref), custom_call_target="tpu_custom_call" | custom-call | tf_op jit(solution)/shard_map/forward/pallas_call | solution.py:268
  125.7 0.1 fusion.41
  125.7 0.1 pad_maximum_fusion.13
  125.8 5.3 %collective-permute-start.4 = (f32[1,64,128]{2,1,0:T(8,128)S(1)}, f32[1,64,128]{2,1,0:T(8,128)S(1)}, u32[]{:S(2)}, u32[]{:S(2)}) collective-permute-start(f32[1,64,128]{2,1,0:T(8,128)S(1)} %pad_maximum_fusion.13), channel_id=1, source_target_pairs={{0,24},{8,0},{16,8},{24,16},{1,25},{9,1},{17,9},{25,17},{2,26},{10... | collective-permute-start | bytes 98312 | tf_op jit(solution)/shard_map/ppermute | solution.py:189
  131.2 0.1 pad_maximum_fusion.14
  131.2 1.9 collective-permute-start.5
  133.2 0.1 fusion.44
  133.3 4.8 %collective-permute-done.5 = f32[1,64,128]{2,1,0:T(8,128)S(1)} collective-permute-done((f32[1,64,128]{2,1,0:T(8,128)S(1)}, f32[1,64,128]{2,1,0:T(8,128)S(1)}, u32[]{:S(2)}, u32[]{:S(2)}) %collective-permute-start.5) | collective-permute-done | bytes 32800 | tf_op jit(solution)/shard_map/ppermute | solution.py:188
  138.0 0.1 fusion.45
  138.1 0.1 maximum_bitcast_fusion
  138.2 3.1 %collective-permute-start.6 = (f32[2,2,64,128]{3,2,1,0:T(8,128)S(1)}, f32[2,2,64,128]{3,2,1,0:T(8,128)S(1)}, u32[]{:S(2)}, u32[]{:S(2)}) collective-permute-start(f32[2,2,64,128]{3,2,1,0:T(8,128)S(1)} %pad_maximum_fusion.5), channel_id=1, source_target_pairs={{0,1},{1,2},{2,3},{3,4},{4,5},{5,6},{6,7},{7,0},{8,9},{9,10},{10,1... | collective-permute-start | bytes 393224 | tf_op jit(solution)/shard_map/ppermute | solution.py:191
  141.3 4.3 %collective-permute-start.7 = (f32[2,2,64,128]{3,2,1,0:T(8,128)S(1)}, f32[2,2,64,128]{3,2,1,0:T(8,128)S(1)}, u32[]{:S(2)}, u32[]{:S(2)}) collective-permute-start(f32[2,2,64,128]{3,2,1,0:T(8,128)S(1)} %pad_maximum_fusion.5), channel_id=1, source_target_pairs={{0,7},{1,0},{2,1},{3,2},{4,3},{5,4},{6,5},{7,6},{8,15},{9,8},{10,9... | collective-permute-start | bytes 393224 | tf_op jit(solution)/shard_map/ppermute | solution.py:192
  145.6 0.4 collective-permute-done.6
  146.1 1.5 collective-permute-done.7
  147.6 13.9 %backward.1 = f32[2,8,4,64,128]{4,3,2,1,0:T(8,128)S(1)} custom-call(f32[64,320,128]{2,1,0:T(8,128)} %all-gather.2.cloned.1.call-done.index_ref, f32[2,2,192,128]{3,2,1,0:T(8,128)S(1)} %pad_maximum_fusion.2.start_ref, f32[64,2,64,128]{3,2,1,0:T(8,128)S(1)} %forward.1.field_ref), custom_call_target="tpu_custom_call" | custom-call | tf_op jit(solution)/shard_map/backward/pallas_call | solution.py:289
  161.5 8.1 %all_to_all.10 = f32[2,8,4,64,128]{4,3,2,1,0:T(8,128)S(1)} all-to-all(f32[2,8,4,64,128]{4,3,2,1,0:T(8,128)S(1)} %backward.1), channel_id=1, replica_groups={{0,32},{64,96},{128,160},{192,224},{256,288},{320,352},{384,416},{448,4..., dimensions={0} | all-to-all | bytes 4194304 | tf_op jit(solution)/shard_map/all_to_all | solution.py:304
  169.6 1.1 fusion
  170.7 3.8 %all-to-all-start.1 = ((f32[8,4,64,128]{3,2,1,0:T(8,128)}), f32[8,4,64,128]{3,2,1,0:T(8,128)S(1)}, u32[]{:S(2)}, u32[]{:S(2)}) async-start(f32[8,4,64,128]{3,2,1,0:T(8,128)} %fusion), calls=%async_computation.1 | async-start | bytes 2097152 | tf_op jit(solution)/shard_map/all_to_all | solution.py:306
  174.5 29.2 %all-to-all-done.1 = f32[8,4,64,128]{3,2,1,0:T(8,128)S(1)} async-done(((f32[8,4,64,128]{3,2,1,0:T(8,128)}), f32[8,4,64,128]{3,2,1,0:T(8,128)S(1)}, u32[]{:S(2)}, u32[]{:S(2)}) %all-to-all-start.1) | async-done | bytes 1048608 | tf_op jit(solution)/shard_map/all_to_all | solution.py:306
  203.8 0.6 collective-permute-start.8
  204.5 1.6 collective-permute-done.8
  206.1 2.7 %collective-permute-done.9 = f32[3,64,128]{2,1,0:T(8,128)S(1)} collective-permute-done((f32[3,64,128]{2,1,0:T(8,128)S(1)}, f32[3,64,128]{2,1,0:T(8,128)S(1)}, u32[]{:S(2)}, u32[]{:S(2)}) %collective-permute-start.9) | collective-permute-done | bytes 98336 | tf_op jit(solution)/shard_map/ppermute | solution.py:211
  208.8 0.2 fusion.37
  209.0 1.9 collective-permute-start.10
  210.9 5.5 %collective-permute-start.11 = (f32[10,64,3]{2,1,0:T(8,128)S(1)}, f32[10,64,3]{2,1,0:T(8,128)S(1)}, u32[]{:S(2)}, u32[]{:S(2)}) collective-permute-start(f32[10,64,3]{2,1,0:T(8,128)S(1)} %get-tuple-element.17), channel_id=1, source_target_pairs={{0,24},{8,0},{16,8},{24,16},{1,25},{9,1},{17,9},{25,17},{2,26},{10... | collective-permute-start | bytes 23048 | tf_op jit(solution)/shard_map/ppermute | solution.py:211
  216.4 6.2 %collective-permute-done.10 = f32[10,64,3]{2,1,0:T(8,128)S(1)} collective-permute-done((f32[10,64,3]{2,1,0:T(8,128)S(1)}, f32[10,64,3]{2,1,0:T(8,128)S(1)}, u32[]{:S(2)}, u32[]{:S(2)}) %collective-permute-start.10) | collective-permute-done | bytes 7712 | tf_op jit(solution)/shard_map/ppermute | solution.py:208
  222.6 8.0 %collective-permute-done.11 = f32[10,64,3]{2,1,0:T(8,128)S(1)} collective-permute-done((f32[10,64,3]{2,1,0:T(8,128)S(1)}, f32[10,64,3]{2,1,0:T(8,128)S(1)}, u32[]{:S(2)}, u32[]{:S(2)}) %collective-permute-start.11) | collective-permute-done | bytes 7712 | tf_op jit(solution)/shard_map/ppermute | solution.py:211
  230.7 0.1 pad_maximum_fusion.12
  230.8 2.9 %collective-permute-start.12 = (f32[10,3,134]{2,1,0:T(4,128)S(1)}, f32[10,3,134]{2,1,0:T(4,128)S(1)}, u32[]{:S(2)}, u32[]{:S(2)}) collective-permute-start(f32[10,3,134]{2,1,0:T(4,128)S(1)} %get-tuple-element.12), channel_id=1, source_target_pairs={{0,1},{1,2},{2,3},{3,4},{4,5},{5,6},{6,7},{7,0},{8,9},{9,10},{10,1... | collective-permute-start | bytes 48248 | tf_op jit(solution)/shard_map/ppermute | solution.py:208
  233.7 4.7 %collective-permute-start.13 = (f32[10,3,134]{2,1,0:T(4,128)S(1)}, f32[10,3,134]{2,1,0:T(4,128)S(1)}, u32[]{:S(2)}, u32[]{:S(2)}) collective-permute-start(f32[10,3,134]{2,1,0:T(4,128)S(1)} %get-tuple-element.13), channel_id=1, source_target_pairs={{0,7},{1,0},{2,1},{3,2},{4,3},{5,4},{6,5},{7,6},{8,15},{9,8},{10,9... | collective-permute-start | bytes 48248 | tf_op jit(solution)/shard_map/ppermute | solution.py:211
  238.4 0.9 collective-permute-done.13
  239.3 0.4 pad_maximum_fusion
  239.6 0.4 fusion.27
  240.0 0.3 fusion.8
  240.3 1.0 fusion.3
  241.4 0.3 fusion.28
  241.7 0.2 fusion.15
  241.9 0.8 fusion.6
  242.7 0.2 fusion.30
  242.9 0.2 fusion.23
  243.1 0.9 fusion.18
  (36 shorter events, 0.4 us)
Async XLA Ops:
  7.2 28.5 %copy-start.4 = (s32[1,2]{1,0:T(1,128)S(1)}, s32[1,2]{1,0:T(1,128)}, u32[]{:S(2)}) copy-start(s32[1,2]{1,0:T(1,128)} %param.5) | copy-start | bytes 28
  7.2 31.3 %copy-start.3 = (f32[2,1,64,128]{3,2,1,0:T(8,128)S(1)}, f32[2,1,64,128]{3,2,1,0:T(8,128)}, u32[]{:S(2)}) copy-start(f32[2,1,64,128]{3,2,1,0:T(8,128)} %param.4) | copy-start | bytes 196612
  7.2 104.6 %all-gather.2.cloned.1.call-start = ((), (), s32[]{:S(2)}) async-start(), calls=%async_computation.2 | async-start | bytes 11141120 | tf_op jit(solution)/shard_map/all_gather | solution.py:261
  8.4 8.8 %collective-permute-start = (f32[2,64,128]{2,1,0:T(8,128)S(1)}, f32[2,64,128]{2,1,0:T(8,128)S(1)}, u32[]{:S(2)}, u32[]{:S(2)}) collective-permute-start(f32[2,64,128]{2,1,0:T(8,128)S(1)} %pad_maximum_fusion.6), channel_id=1, source_target_pairs={{0,24},{8,0},{16,8},{24,16},{1,25},{9,1},{17,9},{25,17},{2,26},{10... | collective-permute-start | bytes 196616 | tf_op jit(solution)/shard_map/ppermute | solution.py:189
  15.2 7.4 %collective-permute-start.1 = (f32[2,64,128]{2,1,0:T(8,128)S(1)}, f32[2,64,128]{2,1,0:T(8,128)S(1)}, u32[]{:S(2)}, u32[]{:S(2)}) collective-permute-start(f32[2,64,128]{2,1,0:T(8,128)S(1)} %pad_maximum_fusion.7), channel_id=1, source_target_pairs={{0,8},{8,16},{16,24},{24,0},{1,9},{9,17},{17,25},{25,1},{2,10},{10... | collective-permute-start | bytes 196616 | tf_op jit(solution)/shard_map/ppermute | solution.py:188
  23.7 9.2 %collective-permute-start.2 = (f32[4,2,64,128]{3,2,0,1:T(8,128)S(1)}, f32[4,2,64,128]{3,2,0,1:T(8,128)S(1)}, u32[]{:S(2)}, u32[]{:S(2)}) collective-permute-start(f32[4,2,64,128]{3,2,0,1:T(8,128)S(1)} %pad_maximum_fusion.4), channel_id=1, source_target_pairs={{0,1},{1,2},{2,3},{3,4},{4,5},{5,6},{6,7},{7,0},{8,9},{9,10},{10,1... | collective-permute-start | bytes 786440 | tf_op jit(solution)/shard_map/ppermute | solution.py:191
  26.9 7.6 %collective-permute-start.3 = (f32[4,2,64,128]{3,2,0,1:T(8,128)S(1)}, f32[4,2,64,128]{3,2,0,1:T(8,128)S(1)}, u32[]{:S(2)}, u32[]{:S(2)}) collective-permute-start(f32[4,2,64,128]{3,2,0,1:T(8,128)S(1)} %pad_maximum_fusion.4), channel_id=1, source_target_pairs={{0,7},{1,0},{2,1},{3,2},{4,3},{5,4},{6,5},{7,6},{8,15},{9,8},{10,9... | collective-permute-start | bytes 786440 | tf_op jit(solution)/shard_map/ppermute | solution.py:192
  34.8 0.8 copy-start.1
  125.8 7.3 %collective-permute-start.4 = (f32[1,64,128]{2,1,0:T(8,128)S(1)}, f32[1,64,128]{2,1,0:T(8,128)S(1)}, u32[]{:S(2)}, u32[]{:S(2)}) collective-permute-start(f32[1,64,128]{2,1,0:T(8,128)S(1)} %pad_maximum_fusion.13), channel_id=1, source_target_pairs={{0,24},{8,0},{16,8},{24,16},{1,25},{9,1},{17,9},{25,17},{2,26},{10... | collective-permute-start | bytes 98312 | tf_op jit(solution)/shard_map/ppermute | solution.py:189
  131.2 6.8 %collective-permute-start.5 = (f32[1,64,128]{2,1,0:T(8,128)S(1)}, f32[1,64,128]{2,1,0:T(8,128)S(1)}, u32[]{:S(2)}, u32[]{:S(2)}) collective-permute-start(f32[1,64,128]{2,1,0:T(8,128)S(1)} %pad_maximum_fusion.14), channel_id=1, source_target_pairs={{0,8},{8,16},{16,24},{24,0},{1,9},{9,17},{17,25},{25,1},{2,10},{10... | collective-permute-start | bytes 98312 | tf_op jit(solution)/shard_map/ppermute | solution.py:188
  138.2 7.8 %collective-permute-start.6 = (f32[2,2,64,128]{3,2,1,0:T(8,128)S(1)}, f32[2,2,64,128]{3,2,1,0:T(8,128)S(1)}, u32[]{:S(2)}, u32[]{:S(2)}) collective-permute-start(f32[2,2,64,128]{3,2,1,0:T(8,128)S(1)} %pad_maximum_fusion.5), channel_id=1, source_target_pairs={{0,1},{1,2},{2,3},{3,4},{4,5},{5,6},{6,7},{7,0},{8,9},{9,10},{10,1... | collective-permute-start | bytes 393224 | tf_op jit(solution)/shard_map/ppermute | solution.py:191
  141.3 6.2 %collective-permute-start.7 = (f32[2,2,64,128]{3,2,1,0:T(8,128)S(1)}, f32[2,2,64,128]{3,2,1,0:T(8,128)S(1)}, u32[]{:S(2)}, u32[]{:S(2)}) collective-permute-start(f32[2,2,64,128]{3,2,1,0:T(8,128)S(1)} %pad_maximum_fusion.5), channel_id=1, source_target_pairs={{0,7},{1,0},{2,1},{3,2},{4,3},{5,4},{6,5},{7,6},{8,15},{9,8},{10,9... | collective-permute-start | bytes 393224 | tf_op jit(solution)/shard_map/ppermute | solution.py:192
  169.5 34.2 %copy-start = (f32[4,64,128]{2,1,0:T(8,128)S(1)}, f32[4,64,128]{2,1,0:T(8,128)}, u32[]{:S(2)}) copy-start(f32[4,64,128]{2,1,0:T(8,128)} %param.3) | copy-start | bytes 393220
  170.7 33.0 %all-to-all-start.1 = ((f32[8,4,64,128]{3,2,1,0:T(8,128)}), f32[8,4,64,128]{3,2,1,0:T(8,128)S(1)}, u32[]{:S(2)}, u32[]{:S(2)}) async-start(f32[8,4,64,128]{3,2,1,0:T(8,128)} %fusion), calls=%async_computation.1 | async-start | bytes 2097152 | tf_op jit(solution)/shard_map/all_to_all | solution.py:306
  203.8 36.3 %copy-start.2 = (f32[4,64,128]{2,1,0:T(8,128)}, f32[4,64,128]{2,1,0:T(8,128)S(1)}, u32[]{:S(2)}) copy-start(f32[4,64,128]{2,1,0:T(8,128)S(1)} %reduce_sum.9) | copy-start | bytes 393220
  203.8 2.3 collective-permute-start.8
  204.5 4.3 %collective-permute-start.9 = (f32[3,64,128]{2,1,0:T(8,128)S(1)}, f32[3,64,128]{2,1,0:T(8,128)S(1)}, u32[]{:S(2)}, u32[]{:S(2)}) collective-permute-start(f32[3,64,128]{2,1,0:T(8,128)S(1)} %get-tuple-element.19), channel_id=1, source_target_pairs={{0,480},{32,0},{64,32},{96,64},{128,96},{160,128},{192,160},{224,1... | collective-permute-start | bytes 294920 | tf_op jit(solution)/shard_map/ppermute | solution.py:211
  209.0 13.6 %collective-permute-start.10 = (f32[10,64,3]{2,1,0:T(8,128)S(1)}, f32[10,64,3]{2,1,0:T(8,128)S(1)}, u32[]{:S(2)}, u32[]{:S(2)}) collective-permute-start(f32[10,64,3]{2,1,0:T(8,128)S(1)} %get-tuple-element.16), channel_id=1, source_target_pairs={{0,8},{8,16},{16,24},{24,0},{1,9},{9,17},{17,25},{25,1},{2,10},{10... | collective-permute-start | bytes 23048 | tf_op jit(solution)/shard_map/ppermute | solution.py:208
  210.9 19.7 %collective-permute-start.11 = (f32[10,64,3]{2,1,0:T(8,128)S(1)}, f32[10,64,3]{2,1,0:T(8,128)S(1)}, u32[]{:S(2)}, u32[]{:S(2)}) collective-permute-start(f32[10,64,3]{2,1,0:T(8,128)S(1)} %get-tuple-element.17), channel_id=1, source_target_pairs={{0,24},{8,0},{16,8},{24,16},{1,25},{9,1},{17,9},{25,17},{2,26},{10... | collective-permute-start | bytes 23048 | tf_op jit(solution)/shard_map/ppermute | solution.py:211
  230.8 7.6 %collective-permute-start.12 = (f32[10,3,134]{2,1,0:T(4,128)S(1)}, f32[10,3,134]{2,1,0:T(4,128)S(1)}, u32[]{:S(2)}, u32[]{:S(2)}) collective-permute-start(f32[10,3,134]{2,1,0:T(4,128)S(1)} %get-tuple-element.12), channel_id=1, source_target_pairs={{0,1},{1,2},{2,3},{3,4},{4,5},{5,6},{6,7},{7,0},{8,9},{9,10},{10,1... | collective-permute-start | bytes 48248 | tf_op jit(solution)/shard_map/ppermute | solution.py:208
  233.7 5.6 %collective-permute-start.13 = (f32[10,3,134]{2,1,0:T(4,128)S(1)}, f32[10,3,134]{2,1,0:T(4,128)S(1)}, u32[]{:S(2)}, u32[]{:S(2)}) collective-permute-start(f32[10,3,134]{2,1,0:T(4,128)S(1)} %get-tuple-element.13), channel_id=1, source_target_pairs={{0,7},{1,0},{2,1},{3,2},{4,3},{5,4},{6,5},{7,6},{8,15},{9,8},{10,9... | collective-permute-start | bytes 48248 | tf_op jit(solution)/shard_map/ppermute | solution.py:211
Sparse Core Ops, SparseCore 0:
  35.8 75.9 all-gather.1

commit v3 on v2

--- a/solution.py
+++ b/solution.py
@@ -202,40 +202,153 @@
     return jnp.concatenate([above[:, 0], wide[:, 0], below[:, 0], wide[:, 1], corners], axis=1)
 
 
-def with_halo(block, sides, width):
-    for axis, dim in sides:
-        count = lax.axis_size(axis)
-        low = lax.ppermute(
-            lax.slice_in_dim(block, block.shape[dim] - width, None, axis=dim), axis, ring(count, 1)
-        )
-        high = lax.ppermute(lax.slice_in_dim(block, 0, width, axis=dim), axis, ring(count, -1))
-        block = jnp.concatenate([low, block, high], axis=dim)
-    return block
-
-
-def smooth(extended, reach, z_first, nz_total):
-    length = extended.shape[0]
-    base = extended[:-1, :-1, :-1]
-    diff_z = extended[1:, :-1, :-1] - base
-    diff_y = extended[:-1, 1:, :-1] - base
-    diff_x = extended[:-1, :-1, 1:] - base
-    depth_pos = (z_first - reach + jnp.arange(length - 1)) % nz_total
-    diff_z = jnp.where(depth_pos[:, None, None] == nz_total - 1, 0.0, diff_z)
-    scale = lax.rsqrt(
-        diff_z * diff_z + diff_y * diff_y + diff_x * diff_x + tv_smooth * tv_smooth
-    )
-    flux_z = diff_z * scale
-    flux_y = diff_y * scale
-    flux_x = diff_x * scale
-    divergence = (
-        flux_z[1:, 1:, 1:]
-        - flux_z[:-1, 1:, 1:]
-        + flux_y[1:, 1:, 1:]
-        - flux_y[1:, :-1, 1:]
-        + flux_x[1:, 1:, 1:]
-        - flux_x[1:, 1:, :-1]
-    )
-    return extended[1:-1, 1:-1, 1:-1] + tv_rate * divergence
+AROUND = [(0, -1), (0, 1), (1, -1), (1, 0), (1, 1), (-1, -1), (-1, 0), (-1, 1)]
+STRIDE = 4
+
+
+def tile_at(nx, ny, dx, dy):
+    tx, ty = lax.axis_index("tx"), lax.axis_index("ty")
+    return lax.rem(tx + dx + nx, nx) * ny + lax.rem(ty + dy + ny, ny)
+
+
+def share_kernel(nx, ny, parts_ref, index_ref, grad_ref, vol_ref, out_ref):
+    slab, rows, cols = index_ref.shape
+    out_ref[...] = jnp.zeros_like(out_ref)
+    for s in range(slab):
+        grad = parts_ref[0, s]
+        for p in range(1, parts_ref.shape[0]):
+            grad = grad + parts_ref[p, s]
+        vol = index_ref[s] - step_size * grad
+        grad_ref[s] = grad
+        vol_ref[s] = vol
+        turned = vol.T
+        keep = pl.ds(STRIDE * s, TV_STEPS)
+        for dx, dy in AROUND:
+            spot = tile_at(nx, ny, dx, dy)
+            if dx == 0:
+                out_ref[spot, keep, :] = vol[rows - TV_STEPS :] if dy > 0 else vol[:TV_STEPS]
+            else:
+                out_ref[spot, keep, :rows] = turned[cols - TV_STEPS :] if dx > 0 else turned[:TV_STEPS]
+
+
+def sort_kernel(nx, ny, strips_ref, vol_ref, near_ref, up_ref, down_ref):
+    slab, rows, cols = vol_ref.shape
+    body_rows = TV_STEPS * rows
+    part = STRIDE * TV_STEPS
+    for s in range(TV_STEPS):
+        down_ref[pl.ds(rows * s, rows), :] = vol_ref[s]
+        up_ref[pl.ds(rows * s, rows), :] = vol_ref[slab - TV_STEPS + s]
+    for i, (dx, dy) in enumerate(AROUND):
+        strip = strips_ref[tile_at(nx, ny, dx, dy)]
+        near_ref[i] = strip
+        down_ref[pl.ds(body_rows + part * i, part), :] = strip[:part]
+        up_ref[pl.ds(body_rows + part * i, part), :] = strip[STRIDE * (slab - TV_STEPS) :]
+
+
+def smooth_kernel(nz, vol_ref, near_ref, low_ref, high_ref, out_ref, v, fz, fy, fx, turn):
+    slab, rows, cols = vol_ref.shape
+    body_rows = TV_STEPS * rows
+    part = STRIDE * TV_STEPS
+    depth = slab + 2 * TV_STEPS
+    base = 16
+    lane3 = lax.broadcasted_iota(jnp.int32, (TV_STEPS, cols), 1)
+    first, last = lane_masks()
+    turn[...] = jnp.zeros_like(turn)
+    for z in range(depth):
+        s = z - TV_STEPS
+        if 0 <= s < slab:
+            tile = vol_ref[s]
+            near = [near_ref[i, pl.ds(STRIDE * s, TV_STEPS), :] for i in range(8)]
+        else:
+            src, k = (low_ref, z) if s < 0 else (high_ref, s - slab)
+            tile = src[pl.ds(rows * k, rows), :]
+            near = [src[pl.ds(body_rows + part * i + STRIDE * k, TV_STEPS), :] for i in range(8)]
+        for half in range(2):
+            v[z, half, pl.ds(0, base), :] = jnp.zeros((base, cols), jnp.float32)
+            v[z, half, pl.ds(base + rows, 16), :] = jnp.zeros((16, cols), jnp.float32)
+        v[z, 0, pl.ds(base, rows), :] = tile
+        v[z, 0, pl.ds(base - TV_STEPS, TV_STEPS), :] = near[0]
+        v[z, 0, pl.ds(base + rows, TV_STEPS), :] = near[1]
+        for row, k in ((0, 2), (cols - TV_STEPS, 5)):
+            above, beside, below = near[k : k + 3]
+            ends = jnp.where(lane3 < 3 * cols // 4, pltpu.roll(below, rows, 1), pltpu.roll(above, rows, 1))
+            turn[pl.ds(row, TV_STEPS), :] = jnp.where(lane3 < rows, beside, ends)
+        sides = turn[...].T
+        v[z, 1, pl.ds(base, rows), :] = sides[:rows]
+        v[z, 1, pl.ds(base + rows, TV_STEPS), :] = sides[rows : rows + TV_STEPS]
+        v[z, 1, pl.ds(base - TV_STEPS, TV_STEPS), :] = sides[cols - TV_STEPS :]
+
+    z_first = lax.axis_index("angle") * slab - TV_STEPS + nz
+    chunks = rows // 8 + 2
+    for t in range(TV_STEPS):
+
+        @pl.loop(t, depth - 1 - t)
+        def _(z):
+            inner = jnp.where(lax.rem(z_first + z, nz) == nz - 1, 0.0, 1.0)
+            for c in range(chunks):
+                row = base - 8 + 8 * c
+                mid = [v[z, half, pl.ds(row, 8), :] for half in range(2)]
+                ahead = [pltpu.roll(m, cols - 1, 1) for m in mid]
+                for half in range(2):
+                    dz = (v[z + 1, half, pl.ds(row, 8), :] - mid[half]) * inner
+                    dy = v[z, half, pl.ds(row + 1, 8), :] - mid[half]
+                    dx = jnp.where(last, ahead[1 - half], ahead[half]) - mid[half]
+                    scale = lax.rsqrt(dz * dz + dy * dy + dx * dx + tv_smooth * tv_smooth)
+                    fz[z, half, pl.ds(row, 8), :] = dz * scale
+                    fy[z, half, pl.ds(row, 8), :] = dy * scale
+                    fx[z, half, pl.ds(row, 8), :] = dx * scale
+
+        @pl.loop(t + 1, depth - 1 - t)
+        def _(z):
+            final = t == TV_STEPS - 1
+            for c in range(1, chunks - 1) if final else range(chunks):
+                row = base - 8 + 8 * c
+                mid = [fx[z, half, pl.ds(row, 8), :] for half in range(2)]
+                behind = [pltpu.roll(m, 1, 1) for m in mid]
+                for half in range(1 if final else 2):
+                    here = pl.ds(row, 8)
+                    div = fz[z, half, here, :] - fz[z - 1, half, here, :]
+                    div = div + (fy[z, half, here, :] - fy[z, half, pl.ds(row - 1, 8), :])
+                    div = div + (mid[half] - jnp.where(first, behind[1 - half], behind[half]))
+                    new = v[z, half, here, :] + tv_rate * div
+                    if final:
+                        out_ref[z - TV_STEPS, pl.ds(row - base, 8), :] = new
+                    else:
+                        v[z, half, here, :] = new
+
+
+def step_and_smooth(parts, index, nz):
+    slab, rows, cols = index.shape
+    nx, ny = lax.axis_size("tx"), lax.axis_size("ty")
+    block = jax.ShapeDtypeStruct(index.shape, jnp.float32)
+    params = pltpu.CompilerParams(vmem_limit_bytes=40 * 2**20)
+    strip_rows = STRIDE * slab
+    gradient, volume, strips = pl.pallas_call(
+        functools.partial(share_kernel, nx, ny),
+        out_shape=(block, block, jax.ShapeDtypeStruct((nx * ny, strip_rows, cols), jnp.float32)),
+        compiler_params=params,
+        name="share",
+    )(parts, index)
+    strips = lax.all_to_all(strips, ("tx", "ty"), 0, 0, tiled=True)
+    outward = jax.ShapeDtypeStruct((TV_STEPS * (rows + 8 * STRIDE), cols), jnp.float32)
+    near, up, down = pl.pallas_call(
+        functools.partial(sort_kernel, nx, ny),
+        out_shape=(jax.ShapeDtypeStruct((8, strip_rows, cols), jnp.float32), outward, outward),
+        compiler_params=params,
+        name="sort",
+    )(strips, volume)
+    depth = lax.axis_size("angle")
+    low = lax.ppermute(up, "angle", ring(depth, 1))
+    high = lax.ppermute(down, "angle", ring(depth, -1))
+    whole = pltpu.VMEM((slab + 2 * TV_STEPS, 2, rows + 32, cols), jnp.float32)
+    smoothed = pl.pallas_call(
+        functools.partial(smooth_kernel, nz),
+        out_shape=block,
+        scratch_shapes=[whole, whole, whole, whole, pltpu.VMEM((cols, cols), jnp.float32)],
+        compiler_params=params,
+        name="smooth",
+    )(volume, near, low, high)
+    return gradient, smoothed
 
 
 def body(index, measured, illum):
@@ -304,14 +417,7 @@
     pair = lax.all_to_all(grads, "angle", 0, 0, tiled=True, axis_index_groups=core_groups)
     both = pair[0] + pair[1]
     parts = lax.all_to_all(both, "angle", 0, 0, tiled=True, axis_index_groups=chip_groups)
-    gradient = jnp.sum(parts, axis=0)
-
-    volume = index - step_size * gradient
-    z_first = lax.axis_index("angle") * slab
-    extended = with_halo(volume, (("angle", 0), ("tx", 2), ("ty", 1)), TV_STEPS)
-    for turn in range(TV_STEPS):
-        extended = smooth(extended, TV_STEPS - turn, z_first, nz)
-    return (gradient, extended)
+    return step_and_smooth(parts, index, nz)
 
 
 def solution(mesh):

time: 255 us -> 241 us (0.945); the launches traced: 251 us -> 240 us
  blocking collectives: 8.07 us -> 56.4 us
  waiting for transfers between devices: 136 us -> 97 us
  starting transfers between devices: 50.1 us -> 31.4 us
  other arithmetic: 10.1 us -> 4.08 us
  Pallas kernels: 27.7 us -> 33.2 us
    all_to_all x0 -> x2, blocking collectives: none -> 48.2 us  [the longest x1 31.5 us: body(): lax.all_to_all(both, 'angle', 0, 0, tiled=True, axis_index_groups=chip_gr...]
    all_to_all x1 -> x0, waiting for transfers between devices: 29.2 us -> none  [body(): lax.all_to_all(both, 'angle', 0, 0, tiled=True, axis_index_groups=chip_gr...]
    ppermute x6 -> x2, waiting for transfers between devices: 19.4 us -> 4.69 us  [the longest x1 2.76 us: step_and_smooth(): high = lax.ppermute(down, 'angle', ring(depth, -1))]
    ppermute x6 -> x2, starting transfers between devices: 15.6 us -> 3.8 us  [the longest x1 3.63 us: step_and_smooth(): low = lax.ppermute(up, 'angle', ring(depth, 1))]
    ppermute x2, waiting for transfers between devices: 10.2 us -> 0.01 us  [widen(): left = unpack(lax.ppermute(pack(block[:, :, half:]), axis_x, ring(nx, 1)))]
    ppermute x2, waiting for transfers between devices: 2.2 us -> 11.4 us  [widen(): above = lax.ppermute(wide, axis_y, ring(ny, 1))]
    ppermute x2, waiting for transfers between devices: 0.01 us -> 8.33 us  [widen(): right = unpack(lax.ppermute(pack(block[:, :, :half]), axis_x, ring(nx, -1)))]
    pallas_call x0 -> x3, Pallas kernels: none -> 5.56 us  [the longest x1 4.82 us: step_and_smooth(): pl.pallas_call(functools.partial(smooth_kernel, nz), out_shape=block, scr...]
  transfers between devices with their start and end apart: 16 -> 11, of which waited for: 13 -> 8; matrix products, arithmetic and copies ran while one was open for 2% -> 1% of each run, Pallas kernels for 0% -> 0%
where the time goes in v3:
time: 241 us; the launch traced here: 240 us
  waiting for transfers between devices  97 us (40%)
  blocking collectives  56.4 us (23%)
  Pallas kernels  33.2 us (14%)
  starting transfers between devices  31.4 us (13%)
  between operations  14.4 us (6%)
  other arithmetic  4.08 us (2%)
  local copies, waits for them, and re-layouts  3.9 us (2%)
    all_gather x1, waiting for transfers between devices, body(): lax.all_gather(pack_corners(*widen(index, 'tx', 'ty')), 'angle', axis=0,...  70.8 us
    all_to_all x1, blocking collectives, body(): lax.all_to_all(both, 'angle', 0, 0, tiled=True, axis_index_groups=chip_gr...  31.5 us
    all_to_all x1, blocking collectives, step_and_smooth(): strips = lax.all_to_all(strips, ('tx', 'ty'), 0, 0, tiled=True)  16.6 us
    pallas_call x1, Pallas kernels, body(): pl.pallas_call(functools.partial(backward_kernel, tall), grid=(steps,), i...  13.9 us
    pallas_call x1, Pallas kernels, body(): pl.pallas_call(functools.partial(forward_kernel, tall), grid=(steps,), in...  13.8 us
    ppermute x2, waiting for transfers between devices, widen(): above = lax.ppermute(wide, axis_y, ring(ny, 1))  11.4 us
    ppermute x2, starting transfers between devices, widen(): left = unpack(lax.ppermute(pack(block[:, :, half:]), axis_x, ring(nx, 1)))  9.08 us
    ppermute x2, waiting for transfers between devices, widen(): right = unpack(lax.ppermute(pack(block[:, :, :half]), axis_x, ring(nx, -1)))  8.33 us
  transfers between devices with their start and end apart: 11, of which 8 were waited for; matrix products, arithmetic and copies ran while one was open for 1% of the time, Pallas kernels for 0%

profile of v3, /device:TPU:1, one launch (start us, length us, event | category | flops | bytes accessed | tf_op | source)
XLA Modules:
  0.0 240.3 jit_solution(3997880318776095482)
XLA Ops:
  7.2 0.0 copy-start.3
  7.2 0.0 copy-start.2
  7.2 0.0 all-gather.2.cloned.1.call-start
  7.2 1.0 fusion.14
  8.3 0.1 pad_maximum_fusion.5
  8.4 5.0 %collective-permute-start.1 = (f32[2,64,128]{2,1,0:T(8,128)S(1)}, f32[2,64,128]{2,1,0:T(8,128)S(1)}, u32[]{:S(2)}, u32[]{:S(2)}) collective-permute-start(f32[2,64,128]{2,1,0:T(8,128)S(1)} %pad_maximum_fusion.5), channel_id=1, source_target_pairs={{0,8},{8,16},{16,24},{24,0},{1,9},{9,17},{17,25},{25,1},{2,10},{10... | collective-permute-start | bytes 196616 | tf_op jit(solution)/shard_map/ppermute | solution.py:188
  13.4 0.1 pad_maximum_fusion.4
  13.5 3.6 %collective-permute-start = (f32[2,64,128]{2,1,0:T(8,128)S(1)}, f32[2,64,128]{2,1,0:T(8,128)S(1)}, u32[]{:S(2)}, u32[]{:S(2)}) collective-permute-start(f32[2,64,128]{2,1,0:T(8,128)S(1)} %pad_maximum_fusion.4), channel_id=1, source_target_pairs={{0,24},{8,0},{16,8},{24,16},{1,25},{9,1},{17,9},{25,17},{2,26},{10... | collective-permute-start | bytes 196616 | tf_op jit(solution)/shard_map/ppermute | solution.py:189
  17.1 0.0 collective-permute-done.1
  17.1 0.1 fusion.17
  17.2 4.8 %collective-permute-done = f32[2,64,128]{2,1,0:T(8,128)S(1)} collective-permute-done((f32[2,64,128]{2,1,0:T(8,128)S(1)}, f32[2,64,128]{2,1,0:T(8,128)S(1)}, u32[]{:S(2)}, u32[]{:S(2)}) %collective-permute-start) | collective-permute-done | bytes 65568 | tf_op jit(solution)/shard_map/ppermute | solution.py:189
  22.0 0.1 fusion.16
  22.1 0.1 fusion.12
  22.2 0.9 pad_maximum_fusion.2
  23.1 3.2 %collective-permute-start.3 = (f32[4,2,64,128]{3,2,0,1:T(8,128)S(1)}, f32[4,2,64,128]{3,2,0,1:T(8,128)S(1)}, u32[]{:S(2)}, u32[]{:S(2)}) collective-permute-start(f32[4,2,64,128]{3,2,0,1:T(8,128)S(1)} %pad_maximum_fusion.2), channel_id=1, source_target_pairs={{0,7},{1,0},{2,1},{3,2},{4,3},{5,4},{6,5},{7,6},{8,15},{9,8},{10,9... | collective-permute-start | bytes 786440 | tf_op jit(solution)/shard_map/ppermute | solution.py:192
  26.3 2.4 collective-permute-start.2
  28.7 1.8 collective-permute-done.3
  30.5 0.1 fusion.13
  30.6 5.5 %collective-permute-done.2 = f32[4,2,64,128]{3,2,0,1:T(8,128)S(1)} collective-permute-done((f32[4,2,64,128]{3,2,0,1:T(8,128)S(1)}, f32[4,2,64,128]{3,2,0,1:T(8,128)S(1)}, u32[]{:S(2)}, u32[]{:S(2)}) %collective-permute-start.2) | collective-permute-done | bytes 262176 | tf_op jit(solution)/shard_map/ppermute | solution.py:191
  36.1 0.9 constant_dynamic-update-slice_fusion.1
  37.1 0.1 constant_dynamic-update-slice_fusion
  37.2 0.1 fusion.7
  37.3 0.0 copy-start.1
  37.3 0.8 copy-done.1
  38.2 0.0 all-gather.2.cloned.1.call-update
  38.2 0.0 copy-done.3
  38.2 0.6 fusion.20
  38.8 0.6 add_multiply_fusion
  39.5 1.5 fusion.11
  41.0 0.0 copy-done.2
  41.0 70.8 %all-gather.2.cloned.1.call-done.index_ref = f32[64,320,128]{2,1,0:T(8,128)} async-done(((f32[4,320,128]{2,1,0:T(8,128)}), f32[64,320,128]{2,1,0:T(8,128)}) %all-gather.2.cloned.1.call-update) | async-done | bytes 10485776 | tf_op jit(solution)/shard_map/all_gather | solution.py:374
  111.9 13.8 %forward.1.field_ref = f32[64,2,64,128]{3,2,1,0:T(8,128)S(1)} custom-call(f32[64,320,128]{2,1,0:T(8,128)} %all-gather.2.cloned.1.call-done.index_ref, f32[2,2,192,128]{3,2,1,0:T(8,128)S(1)} %pad_maximum_fusion.start_ref), custom_call_target="tpu_custom_call" | custom-call | tf_op jit(solution)/shard_map/forward/pallas_call | solution.py:381
  125.7 0.1 fusion.15
  125.8 0.1 pad_maximum_fusion.7
  125.9 4.0 %collective-permute-start.5 = (f32[1,64,128]{2,1,0:T(8,128)S(1)}, f32[1,64,128]{2,1,0:T(8,128)S(1)}, u32[]{:S(2)}, u32[]{:S(2)}) collective-permute-start(f32[1,64,128]{2,1,0:T(8,128)S(1)} %pad_maximum_fusion.7), channel_id=1, source_target_pairs={{0,8},{8,16},{16,24},{24,0},{1,9},{9,17},{17,25},{25,1},{2,10},{10... | collective-permute-start | bytes 98312 | tf_op jit(solution)/shard_map/ppermute | solution.py:188
  129.9 0.1 pad_maximum_fusion.6
  130.0 3.3 %collective-permute-start.4 = (f32[1,64,128]{2,1,0:T(8,128)S(1)}, f32[1,64,128]{2,1,0:T(8,128)S(1)}, u32[]{:S(2)}, u32[]{:S(2)}) collective-permute-start(f32[1,64,128]{2,1,0:T(8,128)S(1)} %pad_maximum_fusion.6), channel_id=1, source_target_pairs={{0,24},{8,0},{16,8},{24,16},{1,25},{9,1},{17,9},{25,17},{2,26},{10... | collective-permute-start | bytes 98312 | tf_op jit(solution)/shard_map/ppermute | solution.py:189
  133.4 0.0 collective-permute-done.5
  133.4 0.1 fusion.19
  133.4 3.5 %collective-permute-done.4 = f32[1,64,128]{2,1,0:T(8,128)S(1)} collective-permute-done((f32[1,64,128]{2,1,0:T(8,128)S(1)}, f32[1,64,128]{2,1,0:T(8,128)S(1)}, u32[]{:S(2)}, u32[]{:S(2)}) %collective-permute-start.4) | collective-permute-done | bytes 32800 | tf_op jit(solution)/shard_map/ppermute | solution.py:189
  137.0 0.1 fusion.18
  137.1 0.1 maximum_bitcast_fusion
  137.2 4.0 %collective-permute-start.7 = (f32[2,2,64,128]{3,2,1,0:T(8,128)S(1)}, f32[2,2,64,128]{3,2,1,0:T(8,128)S(1)}, u32[]{:S(2)}, u32[]{:S(2)}) collective-permute-start(f32[2,2,64,128]{3,2,1,0:T(8,128)S(1)} %pad_maximum_fusion.3), channel_id=1, source_target_pairs={{0,7},{1,0},{2,1},{3,2},{4,3},{5,4},{6,5},{7,6},{8,15},{9,8},{10,9... | collective-permute-start | bytes 393224 | tf_op jit(solution)/shard_map/ppermute | solution.py:192
  141.2 1.9 collective-permute-start.6
  143.1 0.0 collective-permute-done.7
  143.1 5.9 %collective-permute-done.6 = f32[2,2,64,128]{3,2,1,0:T(8,128)S(1)} collective-permute-done((f32[2,2,64,128]{3,2,1,0:T(8,128)S(1)}, f32[2,2,64,128]{3,2,1,0:T(8,128)S(1)}, u32[]{:S(2)}, u32[]{:S(2)}) %collective-permute-start.6) | collective-permute-done | bytes 131104 | tf_op jit(solution)/shard_map/ppermute | solution.py:191
  149.0 13.9 %backward.1 = f32[2,8,4,64,128]{4,3,2,1,0:T(8,128)S(1)} custom-call(f32[64,320,128]{2,1,0:T(8,128)} %all-gather.2.cloned.1.call-done.index_ref, f32[2,2,192,128]{3,2,1,0:T(8,128)S(1)} %pad_maximum_fusion.1.start_ref, f32[64,2,64,128]{3,2,1,0:T(8,128)S(1)} %forward.1.field_ref), custom_call_target="tpu_custom_call" | custom-call | tf_op jit(solution)/shard_map/backward/pallas_call | solution.py:402
  162.9 0.0 copy-start
  162.9 8.2 %all_to_all.15 = f32[2,8,4,64,128]{4,3,2,1,0:T(8,128)S(1)} all-to-all(f32[2,8,4,64,128]{4,3,2,1,0:T(8,128)S(1)} %backward.1), channel_id=1, replica_groups={{0,32},{64,96},{128,160},{192,224},{256,288},{320,352},{384,416},{448,4..., dimensions={0} | all-to-all | bytes 4194304 | tf_op jit(solution)/shard_map/all_to_all | solution.py:417
  171.1 0.1 fusion
  171.3 31.5 %all_to_all.16.parts_ref = f32[8,4,64,128]{3,2,1,0:T(8,128)S(1)} all-to-all(f32[8,4,64,128]{3,2,1,0:T(8,128)S(1)} %fusion), channel_id=1, replica_groups={{0,64,128,192,256,320,384,448},{32,96,160,224,288,352,416,480},{1,65,12..., dimensions={0} | all-to-all | bytes 2097152 | tf_op jit(solution)/shard_map/all_to_all | solution.py:419
  202.8 0.0 copy-done
  202.8 0.7 share.1
  203.5 16.6 %all_to_all.17.strips_ref = f32[32,16,128]{2,1,0:T(8,128)S(1)} all-to-all(f32[32,16,128]{2,1,0:T(8,128)S(1)} %get-tuple-element.10), channel_id=1, replica_groups=mesh['angle'=16,'tx'=4,'ty'=8] {'tx','ty'}, dimensions={0} | all-to-all | bytes 524288 | tf_op jit(solution)/shard_map/all_to_all | solution.py:332
  220.2 3.6 %collective-permute-start.8 = (f32[288,128]{1,0:T(8,128)S(1)}, f32[288,128]{1,0:T(8,128)S(1)}, u32[]{:S(2)}, u32[]{:S(2)}) collective-permute-start(f32[288,128]{1,0:T(8,128)S(1)} %get-tuple-element.12), channel_id=1, source_target_pairs={{0,32},{32,64},{64,96},{96,128},{128,160},{160,192},{192,224},{224... | collective-permute-start | bytes 442376 | tf_op jit(solution)/shard_map/ppermute | solution.py:341
  223.8 0.2 collective-permute-start.9
  224.0 1.9 collective-permute-done.8.low_ref
  225.9 2.8 %collective-permute-done.9.high_ref = f32[288,128]{1,0:T(8,128)S(1)} collective-permute-done((f32[288,128]{1,0:T(8,128)S(1)}, f32[288,128]{1,0:T(8,128)S(1)}, u32[]{:S(2)}, u32[]{:S(2)}) %collective-permute-start.9) | collective-permute-done | bytes 147488 | tf_op jit(solution)/shard_map/ppermute | solution.py:342
  228.7 4.8 %smooth.1 = f32[4,64,128]{2,1,0:T(8,128)} custom-call(f32[4,64,128]{2,1,0:T(8,128)S(1)} %get-tuple-element.9.vol_ref, f32[8,16,128]{2,1,0:T(8,128)S(1)} %get-tuple-element.11.near_ref, f32[288,128]{1,0:T(8,128)S(1)} %collective-permute-done.8.low_ref, f32[288,128]{1,0:T(8,128)S(1)} %collective-permute-done.9.high_ref), custom_call_target="tpu_custom_call" | custom-call | tf_op jit(solution)/shard_map/smooth/pallas_call | solution.py:344
  (15 shorter events, 0.2 us)
Async XLA Ops:
  7.2 31.0 %copy-start.3 = (s32[1,2]{1,0:T(1,128)S(1)}, s32[1,2]{1,0:T(1,128)}, u32[]{:S(2)}) copy-start(s32[1,2]{1,0:T(1,128)} %param.5) | copy-start | bytes 28
  7.2 33.8 %copy-start.2 = (f32[2,1,64,128]{3,2,1,0:T(8,128)S(1)}, f32[2,1,64,128]{3,2,1,0:T(8,128)}, u32[]{:S(2)}) copy-start(f32[2,1,64,128]{3,2,1,0:T(8,128)} %param.4) | copy-start | bytes 196612
  7.2 104.7 %all-gather.2.cloned.1.call-start = ((), (), s32[]{:S(2)}) async-start(), calls=%async_computation.3 | async-start | bytes 11141120 | tf_op jit(solution)/shard_map/all_gather | solution.py:374
  8.4 8.8 %collective-permute-start.1 = (f32[2,64,128]{2,1,0:T(8,128)S(1)}, f32[2,64,128]{2,1,0:T(8,128)S(1)}, u32[]{:S(2)}, u32[]{:S(2)}) collective-permute-start(f32[2,64,128]{2,1,0:T(8,128)S(1)} %pad_maximum_fusion.5), channel_id=1, source_target_pairs={{0,8},{8,16},{16,24},{24,0},{1,9},{9,17},{17,25},{25,1},{2,10},{10... | collective-permute-start | bytes 196616 | tf_op jit(solution)/shard_map/ppermute | solution.py:188
  13.5 8.5 %collective-permute-start = (f32[2,64,128]{2,1,0:T(8,128)S(1)}, f32[2,64,128]{2,1,0:T(8,128)S(1)}, u32[]{:S(2)}, u32[]{:S(2)}) collective-permute-start(f32[2,64,128]{2,1,0:T(8,128)S(1)} %pad_maximum_fusion.4), channel_id=1, source_target_pairs={{0,24},{8,0},{16,8},{24,16},{1,25},{9,1},{17,9},{25,17},{2,26},{10... | collective-permute-start | bytes 196616 | tf_op jit(solution)/shard_map/ppermute | solution.py:189
  23.1 7.4 %collective-permute-start.3 = (f32[4,2,64,128]{3,2,0,1:T(8,128)S(1)}, f32[4,2,64,128]{3,2,0,1:T(8,128)S(1)}, u32[]{:S(2)}, u32[]{:S(2)}) collective-permute-start(f32[4,2,64,128]{3,2,0,1:T(8,128)S(1)} %pad_maximum_fusion.2), channel_id=1, source_target_pairs={{0,7},{1,0},{2,1},{3,2},{4,3},{5,4},{6,5},{7,6},{8,15},{9,8},{10,9... | collective-permute-start | bytes 786440 | tf_op jit(solution)/shard_map/ppermute | solution.py:192
  26.3 9.8 %collective-permute-start.2 = (f32[4,2,64,128]{3,2,0,1:T(8,128)S(1)}, f32[4,2,64,128]{3,2,0,1:T(8,128)S(1)}, u32[]{:S(2)}, u32[]{:S(2)}) collective-permute-start(f32[4,2,64,128]{3,2,0,1:T(8,128)S(1)} %pad_maximum_fusion.2), channel_id=1, source_target_pairs={{0,1},{1,2},{2,3},{3,4},{4,5},{5,6},{6,7},{7,0},{8,9},{9,10},{10,1... | collective-permute-start | bytes 786440 | tf_op jit(solution)/shard_map/ppermute | solution.py:191
  37.3 0.9 copy-start.1
  125.9 7.5 %collective-permute-start.5 = (f32[1,64,128]{2,1,0:T(8,128)S(1)}, f32[1,64,128]{2,1,0:T(8,128)S(1)}, u32[]{:S(2)}, u32[]{:S(2)}) collective-permute-start(f32[1,64,128]{2,1,0:T(8,128)S(1)} %pad_maximum_fusion.7), channel_id=1, source_target_pairs={{0,8},{8,16},{16,24},{24,0},{1,9},{9,17},{17,25},{25,1},{2,10},{10... | collective-permute-start | bytes 98312 | tf_op jit(solution)/shard_map/ppermute | solution.py:188
  130.0 7.0 %collective-permute-start.4 = (f32[1,64,128]{2,1,0:T(8,128)S(1)}, f32[1,64,128]{2,1,0:T(8,128)S(1)}, u32[]{:S(2)}, u32[]{:S(2)}) collective-permute-start(f32[1,64,128]{2,1,0:T(8,128)S(1)} %pad_maximum_fusion.6), channel_id=1, source_target_pairs={{0,24},{8,0},{16,8},{24,16},{1,25},{9,1},{17,9},{25,17},{2,26},{10... | collective-permute-start | bytes 98312 | tf_op jit(solution)/shard_map/ppermute | solution.py:189
  137.2 5.9 %collective-permute-start.7 = (f32[2,2,64,128]{3,2,1,0:T(8,128)S(1)}, f32[2,2,64,128]{3,2,1,0:T(8,128)S(1)}, u32[]{:S(2)}, u32[]{:S(2)}) collective-permute-start(f32[2,2,64,128]{3,2,1,0:T(8,128)S(1)} %pad_maximum_fusion.3), channel_id=1, source_target_pairs={{0,7},{1,0},{2,1},{3,2},{4,3},{5,4},{6,5},{7,6},{8,15},{9,8},{10,9... | collective-permute-start | bytes 393224 | tf_op jit(solution)/shard_map/ppermute | solution.py:192
  141.2 7.8 %collective-permute-start.6 = (f32[2,2,64,128]{3,2,1,0:T(8,128)S(1)}, f32[2,2,64,128]{3,2,1,0:T(8,128)S(1)}, u32[]{:S(2)}, u32[]{:S(2)}) collective-permute-start(f32[2,2,64,128]{3,2,1,0:T(8,128)S(1)} %pad_maximum_fusion.3), channel_id=1, source_target_pairs={{0,1},{1,2},{2,3},{3,4},{4,5},{5,6},{6,7},{7,0},{8,9},{9,10},{10,1... | collective-permute-start | bytes 393224 | tf_op jit(solution)/shard_map/ppermute | solution.py:191
  162.9 39.9 %copy-start = (f32[4,64,128]{2,1,0:T(8,128)S(1)}, f32[4,64,128]{2,1,0:T(8,128)}, u32[]{:S(2)}) copy-start(f32[4,64,128]{2,1,0:T(8,128)} %index_ref.1) | copy-start | bytes 393220
  220.2 5.7 %collective-permute-start.8 = (f32[288,128]{1,0:T(8,128)S(1)}, f32[288,128]{1,0:T(8,128)S(1)}, u32[]{:S(2)}, u32[]{:S(2)}) collective-permute-start(f32[288,128]{1,0:T(8,128)S(1)} %get-tuple-element.12), channel_id=1, source_target_pairs={{0,32},{32,64},{64,96},{96,128},{128,160},{160,192},{192,224},{224... | collective-permute-start | bytes 442376 | tf_op jit(solution)/shard_map/ppermute | solution.py:341
  223.8 4.9 %collective-permute-start.9 = (f32[288,128]{1,0:T(8,128)S(1)}, f32[288,128]{1,0:T(8,128)S(1)}, u32[]{:S(2)}, u32[]{:S(2)}) collective-permute-start(f32[288,128]{1,0:T(8,128)S(1)} %get-tuple-element.13), channel_id=1, source_target_pairs={{0,480},{32,0},{64,32},{96,64},{128,96},{160,128},{192,160},{224,1... | collective-permute-start | bytes 442376 | tf_op jit(solution)/shard_map/ppermute | solution.py:342
Sparse Core Ops, SparseCore 0:
  38.3 73.5 all-gather.1

commit v4 on v3

--- a/solution.py
+++ b/solution.py
@@ -10,7 +10,6 @@
 from jax.sharding import PartitionSpec as P
 
 TV_STEPS = 3
-HALO = 64
 GROUP = 8
 
 damping = 0.2
@@ -64,24 +63,53 @@
     return mid, out
 
 
-def index_rows(index_ref, j, half, c, chunks):
-    third = chunks // 3
-    if half == 0:
-        return index_ref[j, pl.ds(8 * c, 8), :]
-    if c < third:
-        return index_ref[j, pl.ds(8 * (4 * third + c), 8), :]
-    if c < 2 * third:
-        return index_ref[j, pl.ds(8 * (2 * third + c), 8), :]
-    return pltpu.roll(index_ref[j, pl.ds(8 * (2 * third + c), 8), :], 64, 1)
-
-
 def lane_masks():
     lane = lax.broadcasted_iota(jnp.int32, (8, 128), 1)
     return lane == 0, lane == 127
 
 
-def forward_kernel(rows, index_ref, start_ref, field_ref, buf):
-    chunks = rows // 8
+def near_lanes():
+    lane = lax.broadcasted_iota(jnp.int32, (8, 128), 1)
+    return (lane < 32) | (lane >= 96)
+
+
+def near_index(near_ref, pair, odd, half, c):
+    tall = near_ref.shape[1] // 3
+    if half == 0:
+        return near_ref[pair, pl.ds(tall * odd + 8 * c, 8), :]
+    rows = near_ref[pair, pl.ds(2 * tall + 8 * c, 8), :]
+    return pltpu.roll(rows, 64, 1) if odd else rows
+
+
+def full_index(near_ref, far_ref, pair, odd, half, c, is_near):
+    tall = near_ref.shape[1] // 3
+    edge = tall // 4
+    rim = edge // 8
+    cn = c - rim
+    corner = 4 * edge + tall + edge * odd
+    if 0 <= cn < tall // 8:
+        if half == 0:
+            return near_index(near_ref, pair, odd, half, cn)
+        inner = near_ref[pair, pl.ds(2 * tall + 8 * cn, 8), :]
+        outer = far_ref[pair, pl.ds(4 * edge + 8 * cn, 8), :]
+        if odd:
+            return pltpu.roll(jnp.where(is_near, outer, inner), 64, 1)
+        return jnp.where(is_near, inner, outer)
+    if cn < 0:
+        if half == 0:
+            return far_ref[pair, pl.ds(2 * edge * odd + 8 * c, 8), :]
+        return far_ref[pair, pl.ds(corner + 8 * c, 8), :]
+    c = cn - tall // 8
+    if half == 0:
+        return far_ref[pair, pl.ds(2 * edge * odd + edge + 8 * c, 8), :]
+    return pltpu.roll(far_ref[pair, pl.ds(corner + 8 * c, 8), :], 64, 1)
+
+
+def forward_kernel(near_ref, start_ref, field_ref, buf):
+    tall = start_ref.shape[2]
+    chunks = tall // 8
+    own_first = (tall - field_ref.shape[2]) // 16
+    own_last = chunks - own_first
     pid = pl.program_id(0)
     first, last = lane_masks()
 
@@ -89,117 +117,149 @@
     def _():
         buf[...] = jnp.zeros_like(buf)
         for q in range(4):
-            buf[0, q, 8 : 8 + rows, :] = start_ref[q // 2, q % 2]
-
-    def step(j, parity, lo, hi):
+            buf[0, q, 8 : 8 + tall, :] = start_ref[q // 2, q % 2]
+
+    def step(pair, odd, lo, hi):
         for c in range(lo, hi):
             row = 8 + 8 * c
-            re, sum_re = neighbours(buf, parity, 0, row, first, last)
-            im, sum_im = neighbours(buf, parity, 1, row, first, last)
+            re, sum_re = neighbours(buf, odd, 0, row, first, last)
+            im, sum_im = neighbours(buf, odd, 1, row, first, last)
             for half in range(2):
-                cosine, sine = phase_factor(index_rows(index_ref, j, half, c, chunks))
+                cosine, sine = phase_factor(near_index(near_ref, pair, odd, half, c))
                 wre = sum_re[half] + (im[half] + im[half])
                 wim = sum_im[half] - (re[half] + re[half])
                 nre = cosine * wre - sine * wim
                 nim = cosine * wim + sine * wre
-                buf[1 - parity, half, pl.ds(row, 8), :] = nre
-                buf[1 - parity, 2 + half, pl.ds(row, 8), :] = nim
-                if half == 0 and chunks // 3 <= c < 2 * chunks // 3:
-                    own = 8 * (c - chunks // 3)
-                    field_ref[j, 0, pl.ds(own, 8), :] = nre
-                    field_ref[j, 1, pl.ds(own, 8), :] = nim
-
-    for k in range(8):
+                buf[1 - odd, half, pl.ds(row, 8), :] = nre
+                buf[1 - odd, 2 + half, pl.ds(row, 8), :] = nim
+                if half == 0 and own_first <= c < own_last:
+                    own = pl.ds(8 * (c - own_first), 8)
+                    field_ref[2 * pair + odd, 0, own, :] = nre
+                    field_ref[2 * pair + odd, 1, own, :] = nim
+
+    for k in range(own_first):
 
         @pl.when(pid == k)
         def _(k=k):
             @pl.loop(0, GROUP // 2)
             def _(pair):
-                step(2 * pair, 0, k, chunks - k)
-                step(2 * pair + 1, 1, k, chunks - k)
-
-
-def backward_kernel(rows, index_ref, start_ref, field_ref, grad_ref, buf):
-    chunks = rows // 8
+                step(pair, 0, k, chunks - k)
+                step(pair, 1, k, chunks - k)
+
+
+def backward_kernel(near_ref, far_ref, start_ref, early_ref, late_ref, grad_ref, buf):
+    tall = start_ref.shape[2]
+    chunks = tall // 8
+    own_first = (tall - early_ref.shape[2]) // 16
+    own_last = chunks - own_first
+    rim = own_first // 2
     pid = pl.program_id(0)
     first, last = lane_masks()
+    is_near = near_lanes()
+    slab = GROUP // 2
 
     @pl.when(pid == 0)
     def _():
         buf[...] = jnp.zeros_like(buf)
 
-    def finish(j, parity, c, half, are, aim):
-        if half == 0 and chunks // 3 <= c < 2 * chunks // 3:
-            own = 8 * (c - chunks // 3)
-            fre = field_ref[j, 0, pl.ds(own, 8), :]
-            fim = field_ref[j, 1, pl.ds(own, 8), :]
-            slab = GROUP // 2
-            grad_ref[j // slab, 0, j % slab, pl.ds(own, 8), :] = phase_scale * (aim * fre - are * fim)
-        cosine, sine = phase_factor(index_rows(index_ref, j, half, c, chunks))
-        row = 8 + 8 * c
-        buf[parity, half, pl.ds(row, 8), :] = cosine * are + sine * aim
-        buf[parity, 2 + half, pl.ds(row, 8), :] = cosine * aim - sine * are
-
-    def step(j, parity, lo, hi):
+    def finish(wide, pair, odd, c, half, are, aim):
+        j = 2 * pair + odd
+        if half == 0 and own_first <= c < own_last:
+            own = pl.ds(8 * (c - own_first), 8)
+            field_ref = late_ref if wide else early_ref
+            fre = field_ref[j, 0, own, :]
+            fim = field_ref[j, 1, own, :]
+            grad_ref[j // slab, 0, j % slab, own, :] = phase_scale * (aim * fre - are * fim)
+        if wide:
+            index = full_index(near_ref, far_ref, pair, odd, half, c, is_near)
+        else:
+            index = near_index(near_ref, pair, odd, half, c - rim)
+        cosine, sine = phase_factor(index)
+        row = pl.ds(8 + 8 * c, 8)
+        buf[odd, half, row, :] = cosine * are + sine * aim
+        buf[odd, 2 + half, row, :] = cosine * aim - sine * are
+
+    def step(wide, pair, odd, lo, hi):
         for c in range(lo, hi):
             row = 8 + 8 * c
-            re, sum_re = neighbours(buf, 1 - parity, 0, row, first, last)
-            im, sum_im = neighbours(buf, 1 - parity, 1, row, first, last)
+            re, sum_re = neighbours(buf, 1 - odd, 0, row, first, last)
+            im, sum_im = neighbours(buf, 1 - odd, 1, row, first, last)
             for half in range(2):
                 are = sum_re[half] - (im[half] + im[half])
                 aim = sum_im[half] + (re[half] + re[half])
-                finish(j, parity, c, half, are, aim)
-
-    for k in range(8):
+                finish(wide, pair, odd, c, half, are, aim)
+
+    for k in range(own_first):
 
         @pl.when(pid == k)
         def _(k=k):
-            skip = 0
+            wide = k < rim
+            top = GROUP // 2 - 1
             if k == 0:
-                skip = 1
                 for c in range(chunks):
                     for half in range(2):
-                        finish(
-                            GROUP - 1,
-                            1,
-                            c,
-                            half,
-                            start_ref[0, half, pl.ds(8 * c, 8), :],
-                            start_ref[1, half, pl.ds(8 * c, 8), :],
-                        )
-                step(GROUP - 2, 0, k, chunks - k)
-
-            @pl.loop(skip, GROUP // 2)
-            def _(pair):
-                step(GROUP - 1 - 2 * pair, 1, k, chunks - k)
-                step(GROUP - 2 - 2 * pair, 0, k, chunks - k)
+                        rows = pl.ds(8 * c, 8)
+                        finish(wide, top, 1, c, half, start_ref[0, half, rows, :], start_ref[1, half, rows, :])
+                step(wide, top, 0, k, chunks - k)
+
+            @pl.loop(1 if k == 0 else 0, GROUP // 2)
+            def _(back):
+                step(wide, top - back, 1, k, chunks - k)
+                step(wide, top - back, 0, k, chunks - k)
 
 
 def ring(count, by):
     return [(i, (i + by) % count) for i in range(count)]
 
 
-def widen(block, axis_x, axis_y):
+def widen_x(block):
     n, rows, cols = block.shape
     half = cols // 2
-    nx, ny = lax.axis_size(axis_x), lax.axis_size(axis_y)
+    nx = lax.axis_size("tx")
     pack = lambda v: jnp.concatenate([v[: n // 2], v[n // 2 :]], axis=2)
     unpack = lambda v: jnp.concatenate([v[:, :, :half], v[:, :, half:]], axis=0)
-    left = unpack(lax.ppermute(pack(block[:, :, half:]), axis_x, ring(nx, 1)))
-    right = unpack(lax.ppermute(pack(block[:, :, :half]), axis_x, ring(nx, -1)))
-    wide = jnp.stack([block, jnp.concatenate([right, left], axis=2)], axis=1)
-    above = lax.ppermute(wide, axis_y, ring(ny, 1))
-    below = lax.ppermute(wide, axis_y, ring(ny, -1))
-    return above, wide, below
-
-
-def pack_corners(above, wide, below):
-    _, _, rows, cols = wide.shape
-    lane = lax.broadcasted_iota(jnp.int32, (rows, cols), 1)
-    away = jnp.where(lane < cols // 2, lane + 1, cols - lane)
-    from_above = away <= lax.broadcasted_iota(jnp.int32, (rows, cols), 0)
-    corners = jnp.where(from_above, above[:, 1], jnp.roll(below[:, 1], cols // 2, axis=2))
-    return jnp.concatenate([above[:, 0], wide[:, 0], below[:, 0], wide[:, 1], corners], axis=1)
+    left = unpack(lax.ppermute(pack(block[:, :, half:]), "tx", ring(nx, 1)))
+    right = unpack(lax.ppermute(pack(block[:, :, :half]), "tx", ring(nx, -1)))
+    return jnp.stack([block, jnp.concatenate([right, left], axis=2)], axis=1)
+
+
+def rows_around(wide, start, stop):
+    rows = wide.shape[2]
+    ny = lax.axis_size("ty")
+    above = lax.ppermute(wide[:, :, rows - stop : rows - start], "ty", ring(ny, 1))
+    below = lax.ppermute(wide[:, :, start:stop], "ty", ring(ny, -1))
+    return above, below
+
+
+def widen(block, reach):
+    wide = widen_x(block)
+    above, below = rows_around(wide, 0, reach)
+    return jnp.concatenate([above, wide, below], axis=2)
+
+
+def turned(block):
+    return jnp.roll(block, block.shape[-1] // 2, axis=-1)
+
+
+def gather_index(index):
+    slab, rows, cols = index.shape
+    reach = rows // 2
+    lane = lax.broadcasted_iota(jnp.int32, (1, cols), 1)
+    inner = (lane < cols // 4) | (lane >= cols - cols // 4)
+    wide = widen_x(index)
+    above, below = rows_around(wide, 0, reach)
+    tall = rows + 2 * reach
+    sides = jnp.concatenate([above[:, 1], wide[:, 1], below[:, 1]], axis=1).reshape(slab // 2, 2, tall, cols)
+    even, odd = sides[:, 0], turned(sides[:, 1])
+    middle = jnp.concatenate([above[:, 0], wide[:, 0], below[:, 0]], axis=1).reshape(slab // 2, 2 * tall, cols)
+    near = jnp.concatenate([middle, jnp.where(inner, even, odd)], axis=1)
+    near = lax.all_gather(near, "angle", axis=0, tiled=True)
+    above, below = rows_around(wide, reach, 2 * reach)
+    middle = jnp.concatenate([above[:, 0], below[:, 0]], axis=1).reshape(slab // 2, 4 * reach, cols)
+    corners = jnp.where(inner, above[:, 1], turned(below[:, 1])).reshape(slab // 2, 2 * reach, cols)
+    far = jnp.concatenate([middle, jnp.where(inner, odd, even), corners], axis=1)
+    far = lax.all_gather(far, "angle", axis=0, tiled=True)
+    return near, far
 
 
 AROUND = [(0, -1), (0, 1), (1, -1), (1, 0), (1, 1), (-1, -1), (-1, 0), (-1, 1)]
@@ -351,68 +411,78 @@
     return gradient, smoothed
 
 
+def incident(illum, shape, reach):
+    rows, cols = shape
+    nx = cols * lax.axis_size("tx")
+    ny = rows * lax.axis_size("ty")
+    block = (2, rows + 2 * reach, cols)
+    half = lax.broadcasted_iota(jnp.int32, block, 0)
+    lane = lax.broadcasted_iota(jnp.int32, block, 2)
+    beside = jnp.where(lane < cols // 2, lane + cols, lane - cols)
+    gx = lax.axis_index("tx") * cols + jnp.where(half == 0, lane, beside)
+    gy = lax.axis_index("ty") * rows - reach + lax.broadcasted_iota(jnp.int32, block, 1)
+    whole = math.lcm(nx, ny)
+    parts = illum[0, 0] * gx * (whole // nx) + illum[0, 1] * gy * (whole // ny)
+    parts = lax.rem(lax.rem(parts, whole) + whole, whole)
+    q = (2.0 * math.pi / whole) * parts.astype(jnp.float32)
+    return jnp.stack([jnp.cos(q), jnp.sin(q)])
+
+
 def body(index, measured, illum):
     slab, rows, cols = index.shape
     depth = lax.axis_size("angle")
     nz = slab * depth
-    nx = cols * lax.axis_size("tx")
-    ny = rows * lax.axis_size("ty")
-    tall = 3 * rows
+    reach = rows // 2
     core_groups = [[2 * i, 2 * i + 1] for i in range(depth // 2)]
     chip_groups = [list(range(c, depth, 2)) for c in range(2)]
 
-    half = lax.broadcasted_iota(jnp.int32, (2, tall, cols), 0)
-    lane = lax.broadcasted_iota(jnp.int32, (2, tall, cols), 2)
-    gx = lax.axis_index("tx") * cols + jnp.where(half == 0, lane, jnp.where(lane < cols // 2, lane + cols, lane - cols))
-    gy = lax.axis_index("ty") * rows - rows + lax.broadcasted_iota(jnp.int32, (2, tall, cols), 1)
-    turns = (illum[0, 0] * gx * (ny // math.gcd(nx, ny)) + illum[0, 1] * gy * (nx // math.gcd(nx, ny)))
-    whole = math.lcm(nx, ny)
-    turns = lax.rem(lax.rem(turns, whole) + whole, whole)
-    q = (2.0 * math.pi / whole) * turns.astype(jnp.float32)
-    start = jnp.stack([jnp.cos(q), jnp.sin(q)])
-
-    column = lax.all_gather(pack_corners(*widen(index, "tx", "ty")), "angle", axis=0, tiled=True)
-
-    index_block = (GROUP, 5 * rows, cols)
+    near, far = gather_index(index)
+
+    steps = nz // GROUP
+    near_block = (GROUP // 2,) + near.shape[1:]
+    far_block = (GROUP // 2,) + far.shape[1:]
     field_block = (GROUP, 2, rows, cols)
-    steps = nz // GROUP
-    scratch = [pltpu.VMEM((2, 4, tall + 16, cols), jnp.float32)]
     params = pltpu.CompilerParams(dimension_semantics=("arbitrary",), vmem_limit_bytes=40 * 2**20)
-    fields = pl.pallas_call(
-        functools.partial(forward_kernel, tall),
-        grid=(steps,),
-        in_specs=[
-            pl.BlockSpec(index_block, lambda i: (i, 0, 0)),
-            pl.BlockSpec((2, 2, tall, cols), lambda i: (0, 0, 0, 0)),
-        ],
-        out_specs=pl.BlockSpec(field_block, lambda i: (i, 0, 0, 0)),
-        out_shape=jax.ShapeDtypeStruct((nz, 2, rows, cols), jnp.float32),
-        scratch_shapes=scratch,
-        compiler_params=params,
-        name="forward",
-    )(column, start)
-
-    back = (TURN.conjugate() ** nz)
+
+    def forward(start, first_step):
+        whole = pl.BlockSpec(start.shape, lambda i: (0, 0, 0, 0))
+        return pl.pallas_call(
+            forward_kernel,
+            grid=(steps // 2,),
+            in_specs=[pl.BlockSpec(near_block, lambda i: (i + first_step, 0, 0)), whole],
+            out_specs=pl.BlockSpec(field_block, lambda i: (i, 0, 0, 0)),
+            out_shape=jax.ShapeDtypeStruct((nz // 2, 2, rows, cols), jnp.float32),
+            scratch_shapes=[pltpu.VMEM((2, 4, rows + 2 * reach + 16, cols), jnp.float32)],
+            compiler_params=params,
+            name="forward",
+        )(near, start)
+
+    early = forward(incident(illum, (rows, cols), reach), 0)
+    late = forward(widen(early[nz // 2 - 1], reach), steps // 2)
+
+    back = TURN.conjugate() ** nz
     back = back / abs(back)
     target_re = back.real * measured[0] - back.imag * measured[1]
     target_im = back.real * measured[1] + back.imag * measured[0]
-    residual = fields[nz - 1] - jnp.concatenate([target_re, target_im], axis=0)
-    adjoint = jnp.concatenate(widen(residual, "tx", "ty"), axis=2)
+    residual = late[nz // 2 - 1] - jnp.concatenate([target_re, target_im], axis=0)
+    adjoint = widen(residual, rows)
 
     grads = pl.pallas_call(
-        functools.partial(backward_kernel, tall),
+        backward_kernel,
         grid=(steps,),
         in_specs=[
-            pl.BlockSpec(index_block, lambda i: (steps - 1 - i, 0, 0)),
-            pl.BlockSpec((2, 2, tall, cols), lambda i: (0, 0, 0, 0)),
-            pl.BlockSpec(field_block, lambda i: (steps - 1 - i, 0, 0, 0)),
+            pl.BlockSpec(near_block, lambda i: (steps - 1 - i, 0, 0)),
+            pl.BlockSpec(far_block, lambda i: (jnp.maximum(steps - 1 - i, steps // 2), 0, 0)),
+            pl.BlockSpec(adjoint.shape, lambda i: (0, 0, 0, 0)),
+            pl.BlockSpec(field_block, lambda i: (jnp.minimum(steps - 1 - i, steps // 2 - 1), 0, 0, 0)),
+            pl.BlockSpec(field_block, lambda i: (jnp.maximum(steps // 2 - 1 - i, 0), 0, 0, 0)),
         ],
         out_specs=pl.BlockSpec((2, 1, slab, rows, cols), lambda i: (0, steps - 1 - i, 0, 0, 0)),
         out_shape=jax.ShapeDtypeStruct((2, depth // 2, slab, rows, cols), jnp.float32),
-        scratch_shapes=scratch,
+        scratch_shapes=[pltpu.VMEM((2, 4, 3 * rows + 16, cols), jnp.float32)],
         compiler_params=params,
         name="backward",
-    )(column, adjoint, fields)
+    )(near, far, adjoint, early, late)
 
     pair = lax.all_to_all(grads, "angle", 0, 0, tiled=True, axis_index_groups=core_groups)
     both = pair[0] + pair[1]

time: 241 us -> 243 us (level)
  waiting for transfers between devices: 97 us -> 70.5 us
  starting transfers between devices: 31.4 us -> 57.3 us
  local copies, waits for them, and re-layouts: 3.9 us -> 9.33 us
  Pallas kernels: 33.2 us -> 29.6 us
    all_gather x1 -> x2, waiting for transfers between devices: 70.8 us -> 42.8 us  [the longest x1 42.8 us: gather_index(): near = lax.all_gather(near, 'angle', axis=0, tiled=True)]
    ppermute x8 -> x14, starting transfers between devices: 27.5 us -> 53.6 us  [the longest x4 18.4 us: rows_around(): below = lax.ppermute(wide[:, :, start:stop], 'ty', ring(ny, -1))]
    unnamed x11 -> x14, local copies, waits for them, and re-layouts: 1.8 us -> 6.87 us
    pallas_call x2 -> x3, Pallas kernels: 27.7 us -> 24 us  [the longest x1 13.9 us: body(): pl.pallas_call(backward_kernel, grid=(steps,), in_specs=[pl.BlockSpec(nea...]
    all_to_all x1, blocking collectives: 16.6 us -> 13.5 us  [step_and_smooth(): strips = lax.all_to_all(strips, ('tx', 'ty'), 0, 0, tiled=True)]
    ppermute x8 -> x14, waiting for transfers between devices: 21.5 us -> 23.4 us  [the longest x3 12.4 us: widen_x(): right = unpack(lax.ppermute(pack(block[:, :, :half]), 'tx', ring(nx, -1)))]
  transfers between devices with their start and end apart: 11 -> 18, of which waited for: 8 -> 12; matrix products, arithmetic and copies ran while one was open for 1% -> 2% of each run, Pallas kernels for 0% -> 4%
where the time goes in v4:
time: 243 us
  waiting for transfers between devices  70.5 us (29%)
  starting transfers between devices  57.3 us (24%)
  blocking collectives  55.5 us (23%)
  Pallas kernels  29.6 us (12%)
  between operations  14.5 us (6%)
  local copies, waits for them, and re-layouts  9.33 us (4%)
  other arithmetic  5.73 us (2%)
    all_gather x1, waiting for transfers between devices, gather_index(): near = lax.all_gather(near, 'angle', axis=0, tiled=True)  42.8 us
    all_to_all x1, blocking collectives, body(): lax.all_to_all(both, 'angle', 0, 0, tiled=True, axis_index_groups=chip_gr...  31.6 us
    ppermute x4, starting transfers between devices, rows_around(): below = lax.ppermute(wide[:, :, start:stop], 'ty', ring(ny, -1))  18.4 us
    ppermute x3, starting transfers between devices, widen_x(): left = unpack(lax.ppermute(pack(block[:, :, half:]), 'tx', ring(nx, 1)))  14.2 us
    pallas_call x1, Pallas kernels, body(): pl.pallas_call(backward_kernel, grid=(steps,), in_specs=[pl.BlockSpec(nea...  13.9 us
    all_to_all x1, blocking collectives, step_and_smooth(): strips = lax.all_to_all(strips, ('tx', 'ty'), 0, 0, tiled=True)  13.5 us
    ppermute x3, waiting for transfers between devices, widen_x(): right = unpack(lax.ppermute(pack(block[:, :, :half]), 'tx', ring(nx, -1)))  12.4 us
    ppermute x4, starting transfers between devices, rows_around(): lax.ppermute(wide[:, :, rows - stop:rows - start], 'ty', ring(ny, 1))  11.8 us
  transfers between devices with their start and end apart: 18, of which 12 were waited for; matrix products, arithmetic and copies ran while one was open for 2% of the time, Pallas kernels for 4%

profile of v4, /device:TPU:1, one launch (start us, length us, event | category | flops | bytes accessed | tf_op | source)
XLA Modules:
  0.0 242.5 jit_solution(13418467878854512050)
XLA Ops:
  7.2 1.0 fusion.13
  8.3 0.1 pad_maximum_fusion.13
  8.3 5.0 %collective-permute-start.1 = (f32[2,64,128]{2,1,0:T(8,128)S(1)}, f32[2,64,128]{2,1,0:T(8,128)S(1)}, u32[]{:S(2)}, u32[]{:S(2)}) collective-permute-start(f32[2,64,128]{2,1,0:T(8,128)S(1)} %pad_maximum_fusion.13), channel_id=1, source_target_pairs={{0,8},{8,16},{16,24},{24,0},{1,9},{9,17},{17,25},{25,1},{2,10},{10... | collective-permute-start | bytes 196616 | tf_op jit(solution)/shard_map/ppermute | solution.py:221
  13.4 0.1 pad_maximum_fusion.12
  13.5 3.6 %collective-permute-start = (f32[2,64,128]{2,1,0:T(8,128)S(1)}, f32[2,64,128]{2,1,0:T(8,128)S(1)}, u32[]{:S(2)}, u32[]{:S(2)}) collective-permute-start(f32[2,64,128]{2,1,0:T(8,128)S(1)} %pad_maximum_fusion.12), channel_id=1, source_target_pairs={{0,24},{8,0},{16,8},{24,16},{1,25},{9,1},{17,9},{25,17},{2,26},{10... | collective-permute-start | bytes 196616 | tf_op jit(solution)/shard_map/ppermute | solution.py:222
  17.1 0.1 fusion.18
  17.2 4.8 %collective-permute-done = f32[2,64,128]{2,1,0:T(8,128)S(1)} collective-permute-done((f32[2,64,128]{2,1,0:T(8,128)S(1)}, f32[2,64,128]{2,1,0:T(8,128)S(1)}, u32[]{:S(2)}, u32[]{:S(2)}) %collective-permute-start) | collective-permute-done | bytes 65568 | tf_op jit(solution)/shard_map/ppermute | solution.py:222
  22.0 0.1 fusion.17
  22.1 0.1 fusion.24
  22.2 0.9 fusion.6
  23.1 3.7 %collective-permute-start.2 = (f32[4,2,32,128]{3,2,0,1:T(8,128)S(1)}, f32[4,2,32,128]{3,2,0,1:T(8,128)S(1)}, u32[]{:S(2)}, u32[]{:S(2)}) collective-permute-start(f32[4,2,32,128]{3,2,0,1:T(8,128)S(1)} %get-tuple-element.18), channel_id=1, source_target_pairs={{0,1},{1,2},{2,3},{3,4},{4,5},{5,6},{6,7},{7,0},{8,9},{9,10},{10,1... | collective-permute-start | bytes 393224 | tf_op jit(solution)/shard_map/ppermute | solution.py:229
  26.8 3.7 %collective-permute-start.3 = (f32[4,2,32,128]{3,2,0,1:T(8,128)S(1)}, f32[4,2,32,128]{3,2,0,1:T(8,128)S(1)}, u32[]{:S(2)}, u32[]{:S(2)}) collective-permute-start(f32[4,2,32,128]{3,2,0,1:T(8,128)S(1)} %get-tuple-element.19), channel_id=1, source_target_pairs={{0,7},{1,0},{2,1},{3,2},{4,3},{5,4},{6,5},{7,6},{8,15},{9,8},{10,9... | collective-permute-start | bytes 393224 | tf_op jit(solution)/shard_map/ppermute | solution.py:230
  30.5 0.1 maximum_maximum_fusion
  30.6 0.3 collective-permute-done.2
  30.9 1.6 collective-permute-done.3
  32.5 0.1 fusion.12
  32.7 0.1 fusion.7
  32.8 0.8 pad_maximum_fusion
  33.6 3.1 %collective-permute-start.4 = (f32[4,2,32,128]{3,2,0,1:T(8,128)S(1)}, f32[4,2,32,128]{3,2,0,1:T(8,128)S(1)}, u32[]{:S(2)}, u32[]{:S(2)}) collective-permute-start(f32[4,2,32,128]{3,2,0,1:T(8,128)S(1)} %get-tuple-element.19), channel_id=1, source_target_pairs={{0,1},{1,2},{2,3},{3,4},{4,5},{5,6},{6,7},{7,0},{8,9},{9,10},{10,1... | collective-permute-start | bytes 393224 | tf_op jit(solution)/shard_map/ppermute | solution.py:229
  36.8 4.6 %collective-permute-start.5 = (f32[4,2,32,128]{3,2,0,1:T(8,128)S(1)}, f32[4,2,32,128]{3,2,0,1:T(8,128)S(1)}, u32[]{:S(2)}, u32[]{:S(2)}) collective-permute-start(f32[4,2,32,128]{3,2,0,1:T(8,128)S(1)} %get-tuple-element.18), channel_id=1, source_target_pairs={{0,7},{1,0},{2,1},{3,2},{4,3},{5,4},{6,5},{7,6},{8,15},{9,8},{10,9... | collective-permute-start | bytes 393224 | tf_op jit(solution)/shard_map/ppermute | solution.py:230
  41.4 0.4 collective-permute-done.4
  41.8 1.5 collective-permute-done.5
  43.4 0.1 fusion.16
  43.5 0.1 maximum_select_fusion
  43.5 0.7 pad_maximum_fusion.2
  44.3 0.6 fusion.23
  44.9 0.6 add_multiply_fusion
  45.6 1.2 fusion.11
  46.9 42.8 %all-gather.3.cloned.1.call-done.near_ref = f32[32,384,128]{2,1,0:T(8,128)} async-done(((f32[2,384,128]{2,1,0:T(8,128)}), f32[32,384,128]{2,1,0:T(8,128)}) %all-gather.3.cloned.1.call-update) | async-done | bytes 6291472 | tf_op jit(solution)/shard_map/all_gather | solution.py:256
  89.7 2.8 %copy-done = f32[32,384,128]{2,1,0:T(8,128)S(1)} copy-done((f32[32,384,128]{2,1,0:T(8,128)S(1)}, f32[32,384,128]{2,1,0:T(8,128)}, u32[]{:S(2)}) %copy-start) | copy-done | bytes 6291480
  92.4 5.0 %forward.2.early_ref = f32[32,2,64,128]{3,2,1,0:T(8,128)S(1)} custom-call(f32[32,384,128]{2,1,0:T(8,128)S(1)} %copy-done, f32[2,2,128,128]{3,2,1,0:T(8,128)S(1)} %pad_maximum_fusion.5.start_ref), custom_call_target="tpu_custom_call" | custom-call | tf_op jit(solution)/shard_map/forward/pallas_call | solution.py:449
  97.5 0.1 fusion.15
  97.6 0.1 pad_maximum_fusion.15
  97.7 4.0 %collective-permute-start.7 = (f32[1,64,128]{2,1,0:T(8,128)S(1)}, f32[1,64,128]{2,1,0:T(8,128)S(1)}, u32[]{:S(2)}, u32[]{:S(2)}) collective-permute-start(f32[1,64,128]{2,1,0:T(8,128)S(1)} %pad_maximum_fusion.15), channel_id=1, source_target_pairs={{0,8},{8,16},{16,24},{24,0},{1,9},{9,17},{17,25},{25,1},{2,10},{10... | collective-permute-start | bytes 98312 | tf_op jit(solution)/shard_map/ppermute | solution.py:221
  101.7 0.1 pad_maximum_fusion.14
  101.8 3.3 %collective-permute-start.6 = (f32[1,64,128]{2,1,0:T(8,128)S(1)}, f32[1,64,128]{2,1,0:T(8,128)S(1)}, u32[]{:S(2)}, u32[]{:S(2)}) collective-permute-start(f32[1,64,128]{2,1,0:T(8,128)S(1)} %pad_maximum_fusion.14), channel_id=1, source_target_pairs={{0,24},{8,0},{16,8},{24,16},{1,25},{9,1},{17,9},{25,17},{2,26},{10... | collective-permute-start | bytes 98312 | tf_op jit(solution)/shard_map/ppermute | solution.py:222
  105.2 3.8 %collective-permute-done.6 = f32[1,64,128]{2,1,0:T(8,128)S(1)} collective-permute-done((f32[1,64,128]{2,1,0:T(8,128)S(1)}, f32[1,64,128]{2,1,0:T(8,128)S(1)}, u32[]{:S(2)}, u32[]{:S(2)}) %collective-permute-start.6) | collective-permute-done | bytes 32800 | tf_op jit(solution)/shard_map/ppermute | solution.py:222
  109.2 0.1 maximum_bitcast_fusion
  109.3 3.1 %collective-permute-start.8 = (f32[2,2,32,128]{3,2,1,0:T(8,128)S(1)}, f32[2,2,32,128]{3,2,1,0:T(8,128)S(1)}, u32[]{:S(2)}, u32[]{:S(2)}) collective-permute-start(f32[2,2,32,128]{3,2,1,0:T(8,128)S(1)} %get-tuple-element.20), channel_id=1, source_target_pairs={{0,1},{1,2},{2,3},{3,4},{4,5},{5,6},{6,7},{7,0},{8,9},{9,10},{10,1... | collective-permute-start | bytes 196616 | tf_op jit(solution)/shard_map/ppermute | solution.py:229
  112.4 4.3 %collective-permute-start.9 = (f32[2,2,32,128]{3,2,1,0:T(8,128)S(1)}, f32[2,2,32,128]{3,2,1,0:T(8,128)S(1)}, u32[]{:S(2)}, u32[]{:S(2)}) collective-permute-start(f32[2,2,32,128]{3,2,1,0:T(8,128)S(1)} %get-tuple-element.21), channel_id=1, source_target_pairs={{0,7},{1,0},{2,1},{3,2},{4,3},{5,4},{6,5},{7,6},{8,15},{9,8},{10,9... | collective-permute-start | bytes 196616 | tf_op jit(solution)/shard_map/ppermute | solution.py:230
  116.7 1.3 collective-permute-done.9
  118.0 5.1 %forward.3.late_ref = f32[32,2,64,128]{3,2,1,0:T(8,128)S(1)} custom-call(f32[32,384,128]{2,1,0:T(8,128)S(1)} %copy-done, f32[2,2,128,128]{3,2,1,0:T(8,128)S(1)} %pad_maximum_fusion.6.start_ref), custom_call_target="tpu_custom_call" | custom-call | tf_op jit(solution)/shard_map/forward/pallas_call | solution.py:449
  123.1 0.1 fusion.14
  123.2 0.1 pad_maximum_fusion.17
  123.3 5.1 %collective-permute-start.11 = (f32[1,64,128]{2,1,0:T(8,128)S(1)}, f32[1,64,128]{2,1,0:T(8,128)S(1)}, u32[]{:S(2)}, u32[]{:S(2)}) collective-permute-start(f32[1,64,128]{2,1,0:T(8,128)S(1)} %pad_maximum_fusion.17), channel_id=1, source_target_pairs={{0,8},{8,16},{16,24},{24,0},{1,9},{9,17},{17,25},{25,1},{2,10},{10... | collective-permute-start | bytes 98312 | tf_op jit(solution)/shard_map/ppermute | solution.py:221
  128.5 2.3 collective-permute-start.10
  130.8 3.8 %collective-permute-done.10 = f32[1,64,128]{2,1,0:T(8,128)S(1)} collective-permute-done((f32[1,64,128]{2,1,0:T(8,128)S(1)}, f32[1,64,128]{2,1,0:T(8,128)S(1)}, u32[]{:S(2)}, u32[]{:S(2)}) %collective-permute-start.10) | collective-permute-done | bytes 32800 | tf_op jit(solution)/shard_map/ppermute | solution.py:222
  134.7 0.1 maximum_bitcast_fusion.1
  134.8 5.7 %collective-permute-start.13 = (f32[2,2,64,128]{3,2,1,0:T(8,128)S(1)}, f32[2,2,64,128]{3,2,1,0:T(8,128)S(1)}, u32[]{:S(2)}, u32[]{:S(2)}) collective-permute-start(f32[2,2,64,128]{3,2,1,0:T(8,128)S(1)} %pad_maximum_fusion.10), channel_id=1, source_target_pairs={{0,7},{1,0},{2,1},{3,2},{4,3},{5,4},{6,5},{7,6},{8,15},{9,8},{10,9... | collective-permute-start | bytes 393224 | tf_op jit(solution)/shard_map/ppermute | solution.py:230
  140.6 1.9 collective-permute-start.12
  142.5 5.9 %collective-permute-done.12 = f32[2,2,64,128]{3,2,1,0:T(8,128)S(1)} collective-permute-done((f32[2,2,64,128]{3,2,1,0:T(8,128)S(1)}, f32[2,2,64,128]{3,2,1,0:T(8,128)S(1)}, u32[]{:S(2)}, u32[]{:S(2)}) %collective-permute-start.12) | collective-permute-done | bytes 131104 | tf_op jit(solution)/shard_map/ppermute | solution.py:229
  148.5 1.6 copy-done.2
  150.0 2.5 %copy-done.3 = f32[32,320,128]{2,1,0:T(8,128)S(1)} copy-done((f32[32,320,128]{2,1,0:T(8,128)S(1)}, f32[32,320,128]{2,1,0:T(8,128)}, u32[]{:S(2)}) %copy-start.3) | copy-done | bytes 5242904
  152.5 13.9 %backward.1 = f32[2,8,4,64,128]{4,3,2,1,0:T(8,128)S(1)} custom-call(f32[32,384,128]{2,1,0:T(8,128)} %all-gather.3.cloned.1.call-done.near_ref, f32[32,320,128]{2,1,0:T(8,128)S(1)} %copy-done.3, f32[2,2,192,128]{3,2,1,0:T(8,128)S(1)} %pad_maximum_fusion.1.start_ref, f32[32,2,64,128]{3,2,1,0:T(8,128)S(1)} %copy-done.2, f32[32,2,64,128]{3,2,1,0:T(8,128)S(1)} %forward.3.late_ref), custom_call_target="tpu_custom_call" | custom-call | tf_op jit(solution)/shard_map/backward/pallas_call | solution.py:470
  166.5 10.4 %all_to_all.15 = f32[2,8,4,64,128]{4,3,2,1,0:T(8,128)S(1)} all-to-all(f32[2,8,4,64,128]{4,3,2,1,0:T(8,128)S(1)} %backward.1), channel_id=1, replica_groups={{0,32},{64,96},{128,160},{192,224},{256,288},{320,352},{384,416},{448,4..., dimensions={0} | all-to-all | bytes 4194304 | tf_op jit(solution)/shard_map/all_to_all | solution.py:487
  176.9 0.2 fusion
  177.1 31.6 %all_to_all.16.parts_ref = f32[8,4,64,128]{3,2,1,0:T(8,128)S(1)} all-to-all(f32[8,4,64,128]{3,2,1,0:T(8,128)S(1)} %fusion), channel_id=1, replica_groups={{0,64,128,192,256,320,384,448},{32,96,160,224,288,352,416,480},{1,65,12..., dimensions={0} | all-to-all | bytes 2097152 | tf_op jit(solution)/shard_map/all_to_all | solution.py:489
  208.7 0.7 share.1
  209.4 13.5 %all_to_all.17.strips_ref = f32[32,16,128]{2,1,0:T(8,128)S(1)} all-to-all(f32[32,16,128]{2,1,0:T(8,128)S(1)} %get-tuple-element.10), channel_id=1, replica_groups=mesh['angle'=16,'tx'=4,'ty'=8] {'tx','ty'}, dimensions={0} | all-to-all | bytes 524288 | tf_op jit(solution)/shard_map/all_to_all | solution.py:392
  222.9 3.1 %collective-permute-start.14 = (f32[288,128]{1,0:T(8,128)S(1)}, f32[288,128]{1,0:T(8,128)S(1)}, u32[]{:S(2)}, u32[]{:S(2)}) collective-permute-start(f32[288,128]{1,0:T(8,128)S(1)} %get-tuple-element.12), channel_id=1, source_target_pairs={{0,32},{32,64},{64,96},{96,128},{128,160},{160,192},{192,224},{224... | collective-permute-start | bytes 442376 | tf_op jit(solution)/shard_map/ppermute | solution.py:401
  226.0 0.5 collective-permute-start.15
  226.5 1.6 collective-permute-done.14.low_ref
  228.1 2.8 %collective-permute-done.15.high_ref = f32[288,128]{1,0:T(8,128)S(1)} collective-permute-done((f32[288,128]{1,0:T(8,128)S(1)}, f32[288,128]{1,0:T(8,128)S(1)}, u32[]{:S(2)}, u32[]{:S(2)}) %collective-permute-start.15) | collective-permute-done | bytes 147488 | tf_op jit(solution)/shard_map/ppermute | solution.py:402
  230.9 4.8 %smooth.1 = f32[4,64,128]{2,1,0:T(8,128)} custom-call(f32[4,64,128]{2,1,0:T(8,128)S(1)} %get-tuple-element.9.vol_ref, f32[8,16,128]{2,1,0:T(8,128)S(1)} %get-tuple-element.11.near_ref, f32[288,128]{1,0:T(8,128)S(1)} %collective-permute-done.14.low_ref, f32[288,128]{1,0:T(8,128)S(1)} %collective-permute-done.15.high_ref), custom_call_target="tpu_custom_call" | custom-call | tf_op jit(solution)/shard_map/smooth/pallas_call | solution.py:404
  (48 shorter events, 0.8 us)
Async XLA Ops:
  7.2 82.5 %all-gather.3.cloned.1.call-start = ((), (), s32[]{:S(2)}) async-start(), calls=%async_computation.3 | async-start | bytes 6684672 | tf_op jit(solution)/shard_map/all_gather | solution.py:256
  8.2 24.4 %copy-start.4 = (f32[4,64,128]{2,1,0:T(8,128)S(1)}, f32[4,64,128]{2,1,0:T(8,128)}, u32[]{:S(2)}) copy-start(f32[4,64,128]{2,1,0:T(8,128)} %index_ref.1) | copy-start | bytes 393220
  8.3 8.7 %collective-permute-start.1 = (f32[2,64,128]{2,1,0:T(8,128)S(1)}, f32[2,64,128]{2,1,0:T(8,128)S(1)}, u32[]{:S(2)}, u32[]{:S(2)}) collective-permute-start(f32[2,64,128]{2,1,0:T(8,128)S(1)} %pad_maximum_fusion.13), channel_id=1, source_target_pairs={{0,8},{8,16},{16,24},{24,0},{1,9},{9,17},{17,25},{25,1},{2,10},{10... | collective-permute-start | bytes 196616 | tf_op jit(solution)/shard_map/ppermute | solution.py:221
  13.5 8.5 %collective-permute-start = (f32[2,64,128]{2,1,0:T(8,128)S(1)}, f32[2,64,128]{2,1,0:T(8,128)S(1)}, u32[]{:S(2)}, u32[]{:S(2)}) collective-permute-start(f32[2,64,128]{2,1,0:T(8,128)S(1)} %pad_maximum_fusion.12), channel_id=1, source_target_pairs={{0,24},{8,0},{16,8},{24,16},{1,25},{9,1},{17,9},{25,17},{2,26},{10... | collective-permute-start | bytes 196616 | tf_op jit(solution)/shard_map/ppermute | solution.py:222
  23.1 7.8 %collective-permute-start.2 = (f32[4,2,32,128]{3,2,0,1:T(8,128)S(1)}, f32[4,2,32,128]{3,2,0,1:T(8,128)S(1)}, u32[]{:S(2)}, u32[]{:S(2)}) collective-permute-start(f32[4,2,32,128]{3,2,0,1:T(8,128)S(1)} %get-tuple-element.18), channel_id=1, source_target_pairs={{0,1},{1,2},{2,3},{3,4},{4,5},{5,6},{6,7},{7,0},{8,9},{9,10},{10,1... | collective-permute-start | bytes 393224 | tf_op jit(solution)/shard_map/ppermute | solution.py:229
  26.8 5.7 %collective-permute-start.3 = (f32[4,2,32,128]{3,2,0,1:T(8,128)S(1)}, f32[4,2,32,128]{3,2,0,1:T(8,128)S(1)}, u32[]{:S(2)}, u32[]{:S(2)}) collective-permute-start(f32[4,2,32,128]{3,2,0,1:T(8,128)S(1)} %get-tuple-element.19), channel_id=1, source_target_pairs={{0,7},{1,0},{2,1},{3,2},{4,3},{5,4},{6,5},{7,6},{8,15},{9,8},{10,9... | collective-permute-start | bytes 393224 | tf_op jit(solution)/shard_map/ppermute | solution.py:230
  32.7 11.7 %copy-start.6 = (s32[1,2]{1,0:T(1,128)S(1)}, s32[1,2]{1,0:T(1,128)}, u32[]{:S(2)}) copy-start(s32[1,2]{1,0:T(1,128)} %param.5) | copy-start | bytes 28
  33.6 114.8 %all-gather.5.cloned.1.call-start = ((), (), s32[]{:S(2)}) async-start(), calls=%async_computation.4 | async-start | bytes 5570560 | tf_op jit(solution)/shard_map/all_gather | solution.py:261
  33.6 8.2 %collective-permute-start.4 = (f32[4,2,32,128]{3,2,0,1:T(8,128)S(1)}, f32[4,2,32,128]{3,2,0,1:T(8,128)S(1)}, u32[]{:S(2)}, u32[]{:S(2)}) collective-permute-start(f32[4,2,32,128]{3,2,0,1:T(8,128)S(1)} %get-tuple-element.19), channel_id=1, source_target_pairs={{0,1},{1,2},{2,3},{3,4},{4,5},{5,6},{6,7},{7,0},{8,9},{9,10},{10,1... | collective-permute-start | bytes 393224 | tf_op jit(solution)/shard_map/ppermute | solution.py:229
  36.8 6.6 %collective-permute-start.5 = (f32[4,2,32,128]{3,2,0,1:T(8,128)S(1)}, f32[4,2,32,128]{3,2,0,1:T(8,128)S(1)}, u32[]{:S(2)}, u32[]{:S(2)}) collective-permute-start(f32[4,2,32,128]{3,2,0,1:T(8,128)S(1)} %get-tuple-element.18), channel_id=1, source_target_pairs={{0,7},{1,0},{2,1},{3,2},{4,3},{5,4},{6,5},{7,6},{8,15},{9,8},{10,9... | collective-permute-start | bytes 393224 | tf_op jit(solution)/shard_map/ppermute | solution.py:230
  89.7 2.8 %copy-start = (f32[32,384,128]{2,1,0:T(8,128)S(1)}, f32[32,384,128]{2,1,0:T(8,128)}, u32[]{:S(2)}) copy-start(f32[32,384,128]{2,1,0:T(8,128)} %all-gather.3.cloned.1.call-done.near_ref) | copy-start | bytes 18874372
  92.4 24.2 %copy-start.5 = (f32[2,1,64,128]{3,2,1,0:T(8,128)S(1)}, f32[2,1,64,128]{3,2,1,0:T(8,128)}, u32[]{:S(2)}) copy-start(f32[2,1,64,128]{3,2,1,0:T(8,128)} %param.4) | copy-start | bytes 196612
  97.5 25.6 %copy-start.1 = (f32[32,2,64,128]{3,2,1,0:T(8,128)}, f32[32,2,64,128]{3,2,1,0:T(8,128)S(1)}, u32[]{:S(2)}) copy-start(f32[32,2,64,128]{3,2,1,0:T(8,128)S(1)} %forward.2.early_ref) | copy-start | bytes 6291460
  97.7 7.5 %collective-permute-start.7 = (f32[1,64,128]{2,1,0:T(8,128)S(1)}, f32[1,64,128]{2,1,0:T(8,128)S(1)}, u32[]{:S(2)}, u32[]{:S(2)}) collective-permute-start(f32[1,64,128]{2,1,0:T(8,128)S(1)} %pad_maximum_fusion.15), channel_id=1, source_target_pairs={{0,8},{8,16},{16,24},{24,0},{1,9},{9,17},{17,25},{25,1},{2,10},{10... | collective-permute-start | bytes 98312 | tf_op jit(solution)/shard_map/ppermute | solution.py:221
  101.8 7.3 %collective-permute-start.6 = (f32[1,64,128]{2,1,0:T(8,128)S(1)}, f32[1,64,128]{2,1,0:T(8,128)S(1)}, u32[]{:S(2)}, u32[]{:S(2)}) collective-permute-start(f32[1,64,128]{2,1,0:T(8,128)S(1)} %pad_maximum_fusion.14), channel_id=1, source_target_pairs={{0,24},{8,0},{16,8},{24,16},{1,25},{9,1},{17,9},{25,17},{2,26},{10... | collective-permute-start | bytes 98312 | tf_op jit(solution)/shard_map/ppermute | solution.py:222
  109.3 7.4 %collective-permute-start.8 = (f32[2,2,32,128]{3,2,1,0:T(8,128)S(1)}, f32[2,2,32,128]{3,2,1,0:T(8,128)S(1)}, u32[]{:S(2)}, u32[]{:S(2)}) collective-permute-start(f32[2,2,32,128]{3,2,1,0:T(8,128)S(1)} %get-tuple-element.20), channel_id=1, source_target_pairs={{0,1},{1,2},{2,3},{3,4},{4,5},{5,6},{6,7},{7,0},{8,9},{9,10},{10,1... | collective-permute-start | bytes 196616 | tf_op jit(solution)/shard_map/ppermute | solution.py:229
  112.4 5.6 %collective-permute-start.9 = (f32[2,2,32,128]{3,2,1,0:T(8,128)S(1)}, f32[2,2,32,128]{3,2,1,0:T(8,128)S(1)}, u32[]{:S(2)}, u32[]{:S(2)}) collective-permute-start(f32[2,2,32,128]{3,2,1,0:T(8,128)S(1)} %get-tuple-element.21), channel_id=1, source_target_pairs={{0,7},{1,0},{2,1},{3,2},{4,3},{5,4},{6,5},{7,6},{8,15},{9,8},{10,9... | collective-permute-start | bytes 196616 | tf_op jit(solution)/shard_map/ppermute | solution.py:230
  123.3 7.5 %collective-permute-start.11 = (f32[1,64,128]{2,1,0:T(8,128)S(1)}, f32[1,64,128]{2,1,0:T(8,128)S(1)}, u32[]{:S(2)}, u32[]{:S(2)}) collective-permute-start(f32[1,64,128]{2,1,0:T(8,128)S(1)} %pad_maximum_fusion.17), channel_id=1, source_target_pairs={{0,8},{8,16},{16,24},{24,0},{1,9},{9,17},{17,25},{25,1},{2,10},{10... | collective-permute-start | bytes 98312 | tf_op jit(solution)/shard_map/ppermute | solution.py:221
  128.5 6.2 %collective-permute-start.10 = (f32[1,64,128]{2,1,0:T(8,128)S(1)}, f32[1,64,128]{2,1,0:T(8,128)S(1)}, u32[]{:S(2)}, u32[]{:S(2)}) collective-permute-start(f32[1,64,128]{2,1,0:T(8,128)S(1)} %pad_maximum_fusion.16), channel_id=1, source_target_pairs={{0,24},{8,0},{16,8},{24,16},{1,25},{9,1},{17,9},{25,17},{2,26},{10... | collective-permute-start | bytes 98312 | tf_op jit(solution)/shard_map/ppermute | solution.py:222
  134.8 7.7 %collective-permute-start.13 = (f32[2,2,64,128]{3,2,1,0:T(8,128)S(1)}, f32[2,2,64,128]{3,2,1,0:T(8,128)S(1)}, u32[]{:S(2)}, u32[]{:S(2)}) collective-permute-start(f32[2,2,64,128]{3,2,1,0:T(8,128)S(1)} %pad_maximum_fusion.10), channel_id=1, source_target_pairs={{0,7},{1,0},{2,1},{3,2},{4,3},{5,4},{6,5},{7,6},{8,15},{9,8},{10,9... | collective-permute-start | bytes 393224 | tf_op jit(solution)/shard_map/ppermute | solution.py:230
  140.6 7.8 %collective-permute-start.12 = (f32[2,2,64,128]{3,2,1,0:T(8,128)S(1)}, f32[2,2,64,128]{3,2,1,0:T(8,128)S(1)}, u32[]{:S(2)}, u32[]{:S(2)}) collective-permute-start(f32[2,2,64,128]{3,2,1,0:T(8,128)S(1)} %pad_maximum_fusion.10), channel_id=1, source_target_pairs={{0,1},{1,2},{2,3},{3,4},{4,5},{5,6},{6,7},{7,0},{8,9},{9,10},{10,1... | collective-permute-start | bytes 393224 | tf_op jit(solution)/shard_map/ppermute | solution.py:229
  148.4 1.6 copy-start.2
  150.0 2.5 %copy-start.3 = (f32[32,320,128]{2,1,0:T(8,128)S(1)}, f32[32,320,128]{2,1,0:T(8,128)}, u32[]{:S(2)}) copy-start(f32[32,320,128]{2,1,0:T(8,128)} %all-gather.5.cloned.1.call-done.far_ref) | copy-start | bytes 15728644
  222.9 5.2 %collective-permute-start.14 = (f32[288,128]{1,0:T(8,128)S(1)}, f32[288,128]{1,0:T(8,128)S(1)}, u32[]{:S(2)}, u32[]{:S(2)}) collective-permute-start(f32[288,128]{1,0:T(8,128)S(1)} %get-tuple-element.12), channel_id=1, source_target_pairs={{0,32},{32,64},{64,96},{96,128},{128,160},{160,192},{192,224},{224... | collective-permute-start | bytes 442376 | tf_op jit(solution)/shard_map/ppermute | solution.py:401
  226.0 4.9 %collective-permute-start.15 = (f32[288,128]{1,0:T(8,128)S(1)}, f32[288,128]{1,0:T(8,128)S(1)}, u32[]{:S(2)}, u32[]{:S(2)}) collective-permute-start(f32[288,128]{1,0:T(8,128)S(1)} %get-tuple-element.13), channel_id=1, source_target_pairs={{0,480},{32,0},{64,32},{96,64},{128,96},{160,128},{192,160},{224,1... | collective-permute-start | bytes 442376 | tf_op jit(solution)/shard_map/ppermute | solution.py:402
Sparse Core Ops, SparseCore 0:
  33.7 55.8 all-gather.2
  91.8 44.8 all-gather.4

commit v5 on v3

--- a/solution.py
+++ b/solution.py
@@ -50,29 +50,30 @@
     return cosine, sine * t
 
 
-def neighbours(buf, slot, part, row, first, last):
-    mid = [buf[slot, 2 * part + half, pl.ds(row, 8), :] for half in range(2)]
-    low = [pltpu.roll(m, 1, 1) for m in mid]
-    high = [pltpu.roll(m, 127, 1) for m in mid]
+def neighbours(buf, slot, part, row):
+    even, odd = [buf[slot, 2 * part + parity, pl.ds(row, 8), :] for parity in range(2)]
+    sides = (odd + pltpu.roll(odd, 1, 1), even + pltpu.roll(even, 127, 1))
     out = []
-    for half in range(2):
-        left = jnp.where(first, low[1 - half], low[half])
-        right = jnp.where(last, high[1 - half], high[half])
-        up = buf[slot, 2 * part + half, pl.ds(row - 1, 8), :]
-        down = buf[slot, 2 * part + half, pl.ds(row + 1, 8), :]
-        out.append((left + right) + (up + down))
-    return mid, out
-
-
-def index_rows(index_ref, j, half, c, chunks):
+    for parity in range(2):
+        up = buf[slot, 2 * part + parity, pl.ds(row - 1, 8), :]
+        down = buf[slot, 2 * part + parity, pl.ds(row + 1, 8), :]
+        out.append(sides[parity] + (up + down))
+    return (even, odd), out
+
+
+def index_rows(index_ref, j, parity, c, chunks):
     third = chunks // 3
-    if half == 0:
-        return index_ref[j, pl.ds(8 * c, 8), :]
-    if c < third:
-        return index_ref[j, pl.ds(8 * (4 * third + c), 8), :]
+    rows = index_ref.shape[1] // 5
     if c < 2 * third:
-        return index_ref[j, pl.ds(8 * (2 * third + c), 8), :]
-    return pltpu.roll(index_ref[j, pl.ds(8 * (2 * third + c), 8), :], 64, 1)
+        return index_ref[j, pl.ds(2 * rows * parity + 8 * c, 8), :]
+    c = c - 2 * third
+    corner = index_ref[j, pl.ds(2 * rows * parity + 8 * c, 8), :]
+    own = index_ref[j, pl.ds(4 * rows + 8 * c, 8), :]
+    if parity:
+        own = pltpu.roll(own, 64, 1)
+    lane = lax.broadcasted_iota(jnp.int32, (8, 128), 1)
+    corner = jnp.where(lane < 96, pltpu.roll(corner, 96, 1), pltpu.roll(corner, 32, 1))
+    return jnp.where(lane < 64, own, corner)
 
 
 def lane_masks():
@@ -83,7 +84,6 @@
 def forward_kernel(rows, index_ref, start_ref, field_ref, buf):
     chunks = rows // 8
     pid = pl.program_id(0)
-    first, last = lane_masks()
 
     @pl.when(pid == 0)
     def _():
@@ -94,8 +94,8 @@
     def step(j, parity, lo, hi):
         for c in range(lo, hi):
             row = 8 + 8 * c
-            re, sum_re = neighbours(buf, parity, 0, row, first, last)
-            im, sum_im = neighbours(buf, parity, 1, row, first, last)
+            re, sum_re = neighbours(buf, parity, 0, row)
+            im, sum_im = neighbours(buf, parity, 1, row)
             for half in range(2):
                 cosine, sine = phase_factor(index_rows(index_ref, j, half, c, chunks))
                 wre = sum_re[half] + (im[half] + im[half])
@@ -104,10 +104,10 @@
                 nim = cosine * wim + sine * wre
                 buf[1 - parity, half, pl.ds(row, 8), :] = nre
                 buf[1 - parity, 2 + half, pl.ds(row, 8), :] = nim
-                if half == 0 and chunks // 3 <= c < 2 * chunks // 3:
+                if chunks // 3 <= c < 2 * chunks // 3:
                     own = 8 * (c - chunks // 3)
-                    field_ref[j, 0, pl.ds(own, 8), :] = nre
-                    field_ref[j, 1, pl.ds(own, 8), :] = nim
+                    field_ref[j, 0, half, pl.ds(own, 8), :] = nre
+                    field_ref[j, 1, half, pl.ds(own, 8), :] = nim
 
     for k in range(8):
 
@@ -122,33 +122,37 @@
 def backward_kernel(rows, index_ref, start_ref, field_ref, grad_ref, buf):
     chunks = rows // 8
     pid = pl.program_id(0)
-    first, last = lane_masks()
 
     @pl.when(pid == 0)
     def _():
         buf[...] = jnp.zeros_like(buf)
 
-    def finish(j, parity, c, half, are, aim):
-        if half == 0 and chunks // 3 <= c < 2 * chunks // 3:
-            own = 8 * (c - chunks // 3)
-            fre = field_ref[j, 0, pl.ds(own, 8), :]
-            fim = field_ref[j, 1, pl.ds(own, 8), :]
+    def finish(j, slot, c, are, aim):
+        if chunks // 3 <= c < 2 * chunks // 3:
+            own = pl.ds(8 * (c - chunks // 3), 8)
+            parts = []
+            for half in range(2):
+                fre = field_ref[j, 0, half, own, :]
+                fim = field_ref[j, 1, half, own, :]
+                parts.append(phase_scale * (aim[half] * fre - are[half] * fim))
             slab = GROUP // 2
-            grad_ref[j // slab, 0, j % slab, pl.ds(own, 8), :] = phase_scale * (aim * fre - are * fim)
-        cosine, sine = phase_factor(index_rows(index_ref, j, half, c, chunks))
+            lane = lax.broadcasted_iota(jnp.int32, (8, 128), 1)
+            both = jnp.where(lane < 64, parts[0], pltpu.roll(parts[1], 64, 1))
+            grad_ref[j // slab, 0, j % slab, own, :] = both
         row = 8 + 8 * c
-        buf[parity, half, pl.ds(row, 8), :] = cosine * are + sine * aim
-        buf[parity, 2 + half, pl.ds(row, 8), :] = cosine * aim - sine * are
+        for half in range(2):
+            cosine, sine = phase_factor(index_rows(index_ref, j, half, c, chunks))
+            buf[slot, half, pl.ds(row, 8), :] = cosine * are[half] + sine * aim[half]
+            buf[slot, 2 + half, pl.ds(row, 8), :] = cosine * aim[half] - sine * are[half]
 
     def step(j, parity, lo, hi):
         for c in range(lo, hi):
             row = 8 + 8 * c
-            re, sum_re = neighbours(buf, 1 - parity, 0, row, first, last)
-            im, sum_im = neighbours(buf, 1 - parity, 1, row, first, last)
-            for half in range(2):
-                are = sum_re[half] - (im[half] + im[half])
-                aim = sum_im[half] + (re[half] + re[half])
-                finish(j, parity, c, half, are, aim)
+            re, sum_re = neighbours(buf, 1 - parity, 0, row)
+            im, sum_im = neighbours(buf, 1 - parity, 1, row)
+            are = [sum_re[half] - (im[half] + im[half]) for half in range(2)]
+            aim = [sum_im[half] + (re[half] + re[half]) for half in range(2)]
+            finish(j, parity, c, are, aim)
 
     for k in range(8):
 
@@ -158,15 +162,14 @@
             if k == 0:
                 skip = 1
                 for c in range(chunks):
-                    for half in range(2):
-                        finish(
-                            GROUP - 1,
-                            1,
-                            c,
-                            half,
-                            start_ref[0, half, pl.ds(8 * c, 8), :],
-                            start_ref[1, half, pl.ds(8 * c, 8), :],
-                        )
+                    here = pl.ds(8 * c, 8)
+                    finish(
+                        GROUP - 1,
+                        1,
+                        c,
+                        [start_ref[0, half, here, :] for half in range(2)],
+                        [start_ref[1, half, here, :] for half in range(2)],
+                    )
                 step(GROUP - 2, 0, k, chunks - k)
 
             @pl.loop(skip, GROUP // 2)
@@ -179,27 +182,46 @@
     return [(i, (i + by) % count) for i in range(count)]
 
 
+def parity_order(cols):
+    order = np.concatenate([np.arange(0, cols, 2), np.arange(1, cols, 2)])
+    return jnp.asarray(np.eye(cols, dtype=np.float32)[:, order])
+
+
+def reorder(block, matrix):
+    return lax.dot_general(block, matrix, (((block.ndim - 1,), (0,)), ((), ())), precision=lax.Precision.HIGHEST)
+
+
 def widen(block, axis_x, axis_y):
     n, rows, cols = block.shape
-    half = cols // 2
+    half, quarter = cols // 2, cols // 4
     nx, ny = lax.axis_size(axis_x), lax.axis_size(axis_y)
+    side = lambda start: jnp.concatenate(
+        [block[..., start : start + quarter], block[..., start + half : start + half + quarter]], axis=2
+    )
     pack = lambda v: jnp.concatenate([v[: n // 2], v[n // 2 :]], axis=2)
     unpack = lambda v: jnp.concatenate([v[:, :, :half], v[:, :, half:]], axis=0)
-    left = unpack(lax.ppermute(pack(block[:, :, half:]), axis_x, ring(nx, 1)))
-    right = unpack(lax.ppermute(pack(block[:, :, :half]), axis_x, ring(nx, -1)))
-    wide = jnp.stack([block, jnp.concatenate([right, left], axis=2)], axis=1)
+    left = unpack(lax.ppermute(pack(side(quarter)), axis_x, ring(nx, 1)))
+    right = unpack(lax.ppermute(pack(side(0)), axis_x, ring(nx, -1)))
+    even = jnp.concatenate([block[..., :half], right[..., :quarter], left[..., :quarter]], axis=2)
+    odd = jnp.concatenate([block[..., half:], right[..., quarter:], left[..., quarter:]], axis=2)
+    wide = jnp.stack([even, odd], axis=1)
     above = lax.ppermute(wide, axis_y, ring(ny, 1))
     below = lax.ppermute(wide, axis_y, ring(ny, -1))
     return above, wide, below
 
 
 def pack_corners(above, wide, below):
-    _, _, rows, cols = wide.shape
-    lane = lax.broadcasted_iota(jnp.int32, (rows, cols), 1)
-    away = jnp.where(lane < cols // 2, lane + 1, cols - lane)
-    from_above = away <= lax.broadcasted_iota(jnp.int32, (rows, cols), 0)
-    corners = jnp.where(from_above, above[:, 1], jnp.roll(below[:, 1], cols // 2, axis=2))
-    return jnp.concatenate([above[:, 0], wide[:, 0], below[:, 0], wide[:, 1], corners], axis=1)
+    n, _, rows, cols = wide.shape
+    half, quarter = cols // 2, cols // 4
+    lane = lax.broadcasted_iota(jnp.int32, (2, rows, cols), 2)
+    parity = lax.broadcasted_iota(jnp.int32, (2, rows, cols), 0)
+    away = jnp.where(lane < cols - quarter, 2 * (lane - half) + 1 + parity, 2 * (cols - lane) - parity)
+    own = lane < half
+    from_above = own | (away <= lax.broadcasted_iota(jnp.int32, (2, rows, cols), 1))
+    swapped = jnp.concatenate([below[..., :half], below[..., cols - quarter :], below[..., half : cols - quarter]], axis=3)
+    upper = jnp.concatenate([jnp.where(from_above, above, swapped), wide], axis=2).reshape(n, 4 * rows, cols)
+    lower = jnp.concatenate([below[:, 0, :, :half], below[:, 1, :, :half]], axis=2)
+    return jnp.concatenate([upper, lower], axis=1)
 
 
 AROUND = [(0, -1), (0, 1), (1, -1), (1, 0), (1, 1), (-1, -1), (-1, 0), (-1, 1)]
@@ -211,13 +233,14 @@
     return lax.rem(tx + dx + nx, nx) * ny + lax.rem(ty + dy + ny, ny)
 
 
-def share_kernel(nx, ny, parts_ref, index_ref, grad_ref, vol_ref, out_ref):
+def share_kernel(nx, ny, parts_ref, index_ref, order_ref, grad_ref, vol_ref, out_ref):
     slab, rows, cols = index_ref.shape
     out_ref[...] = jnp.zeros_like(out_ref)
     for s in range(slab):
         grad = parts_ref[0, s]
         for p in range(1, parts_ref.shape[0]):
             grad = grad + parts_ref[p, s]
+        grad = jnp.dot(grad, order_ref[...], precision=lax.Precision.HIGHEST, preferred_element_type=jnp.float32)
         vol = index_ref[s] - step_size * grad
         grad_ref[s] = grad
         vol_ref[s] = vol
@@ -317,7 +340,7 @@
                         v[z, half, here, :] = new
 
 
-def step_and_smooth(parts, index, nz):
+def step_and_smooth(parts, index, order, nz):
     slab, rows, cols = index.shape
     nx, ny = lax.axis_size("tx"), lax.axis_size("ty")
     block = jax.ShapeDtypeStruct(index.shape, jnp.float32)
@@ -328,7 +351,7 @@
         out_shape=(block, block, jax.ShapeDtypeStruct((nx * ny, strip_rows, cols), jnp.float32)),
         compiler_params=params,
         name="share",
-    )(parts, index)
+    )(parts, index, order)
     strips = lax.all_to_all(strips, ("tx", "ty"), 0, 0, tiled=True)
     outward = jax.ShapeDtypeStruct((TV_STEPS * (rows + 8 * STRIDE), cols), jnp.float32)
     near, up, down = pl.pallas_call(
@@ -361,23 +384,25 @@
     core_groups = [[2 * i, 2 * i + 1] for i in range(depth // 2)]
     chip_groups = [list(range(c, depth, 2)) for c in range(2)]
 
-    half = lax.broadcasted_iota(jnp.int32, (2, tall, cols), 0)
-    lane = lax.broadcasted_iota(jnp.int32, (2, tall, cols), 2)
-    gx = lax.axis_index("tx") * cols + jnp.where(half == 0, lane, jnp.where(lane < cols // 2, lane + cols, lane - cols))
-    gy = lax.axis_index("ty") * rows - rows + lax.broadcasted_iota(jnp.int32, (2, tall, cols), 1)
+    block = (2, tall, cols)
+    lane = lax.broadcasted_iota(jnp.int32, block, 2)
+    column = 2 * lane + lax.broadcasted_iota(jnp.int32, block, 0)
+    gx = lax.axis_index("tx") * cols + jnp.where(lane < cols - cols // 4, column, column - 2 * cols)
+    gy = lax.axis_index("ty") * rows - rows + lax.broadcasted_iota(jnp.int32, block, 1)
     turns = (illum[0, 0] * gx * (ny // math.gcd(nx, ny)) + illum[0, 1] * gy * (nx // math.gcd(nx, ny)))
     whole = math.lcm(nx, ny)
     turns = lax.rem(lax.rem(turns, whole) + whole, whole)
     q = (2.0 * math.pi / whole) * turns.astype(jnp.float32)
     start = jnp.stack([jnp.cos(q), jnp.sin(q)])
 
-    column = lax.all_gather(pack_corners(*widen(index, "tx", "ty")), "angle", axis=0, tiled=True)
+    order = parity_order(cols)
+    column = lax.all_gather(pack_corners(*widen(reorder(index, order), "tx", "ty")), "angle", axis=0, tiled=True)
 
     index_block = (GROUP, 5 * rows, cols)
-    field_block = (GROUP, 2, rows, cols)
+    field_block = (GROUP, 2, 2, rows, cols)
     steps = nz // GROUP
     scratch = [pltpu.VMEM((2, 4, tall + 16, cols), jnp.float32)]
-    params = pltpu.CompilerParams(dimension_semantics=("arbitrary",), vmem_limit_bytes=40 * 2**20)
+    params = pltpu.CompilerParams(dimension_semantics=("arbitrary",), vmem_limit_bytes=50 * 2**20)
     fields = pl.pallas_call(
         functools.partial(forward_kernel, tall),
         grid=(steps,),
@@ -385,8 +410,8 @@
             pl.BlockSpec(index_block, lambda i: (i, 0, 0)),
             pl.BlockSpec((2, 2, tall, cols), lambda i: (0, 0, 0, 0)),
         ],
-        out_specs=pl.BlockSpec(field_block, lambda i: (i, 0, 0, 0)),
-        out_shape=jax.ShapeDtypeStruct((nz, 2, rows, cols), jnp.float32),
+        out_specs=pl.BlockSpec(field_block, lambda i: (i, 0, 0, 0, 0)),
+        out_shape=jax.ShapeDtypeStruct((nz, 2, 2, rows, cols), jnp.float32),
         scratch_shapes=scratch,
         compiler_params=params,
         name="forward",
@@ -394,9 +419,12 @@
 
     back = (TURN.conjugate() ** nz)
     back = back / abs(back)
-    target_re = back.real * measured[0] - back.imag * measured[1]
-    target_im = back.real * measured[1] + back.imag * measured[0]
-    residual = fields[nz - 1] - jnp.concatenate([target_re, target_im], axis=0)
+    target = reorder(measured[:, 0], order)
+    target_re = back.real * target[0] - back.imag * target[1]
+    target_im = back.real * target[1] + back.imag * target[0]
+    reached = fields[nz - 1]
+    reached = jnp.concatenate([reached[:, 0, :, : cols // 2], reached[:, 1, :, : cols // 2]], axis=2)
+    residual = reached - jnp.stack([target_re, target_im])
     adjoint = jnp.concatenate(widen(residual, "tx", "ty"), axis=2)
 
     grads = pl.pallas_call(
@@ -405,7 +433,7 @@
         in_specs=[
             pl.BlockSpec(index_block, lambda i: (steps - 1 - i, 0, 0)),
             pl.BlockSpec((2, 2, tall, cols), lambda i: (0, 0, 0, 0)),
-            pl.BlockSpec(field_block, lambda i: (steps - 1 - i, 0, 0, 0)),
+            pl.BlockSpec(field_block, lambda i: (steps - 1 - i, 0, 0, 0, 0)),
         ],
         out_specs=pl.BlockSpec((2, 1, slab, rows, cols), lambda i: (0, steps - 1 - i, 0, 0, 0)),
         out_shape=jax.ShapeDtypeStruct((2, depth // 2, slab, rows, cols), jnp.float32),
@@ -417,7 +445,7 @@
     pair = lax.all_to_all(grads, "angle", 0, 0, tiled=True, axis_index_groups=core_groups)
     both = pair[0] + pair[1]
     parts = lax.all_to_all(both, "angle", 0, 0, tiled=True, axis_index_groups=chip_groups)
-    return step_and_smooth(parts, index, nz)
+    return step_and_smooth(parts, index, order.T, nz)
 
 
 def solution(mesh):

time: 241 us -> 249 us (1.033)
  Pallas kernels: 33.2 us -> 40.5 us
    pallas_call x1, Pallas kernels: 13.9 us -> 20.5 us  [body(): pl.pallas_call(functools.partial(backward_kernel, tall), grid=(steps,), i...]
  transfers between devices with their start and end apart: 11 -> 11, of which waited for: 8 -> 8; matrix products, arithmetic and copies ran while one was open for 1% -> 2% of each run, Pallas kernels for 0% -> 0%
where the time goes in v5:
time: 249 us; the launch traced here: 248 us
  waiting for transfers between devices  98 us (39%)
  blocking collectives  54.9 us (22%)
  Pallas kernels  40.5 us (16%)
  starting transfers between devices  31.5 us (13%)
  between operations  14.5 us (6%)
  other arithmetic  4.85 us (2%)
  local copies, waits for them, and re-layouts  2.55 us (1%)
    all_gather x1, waiting for transfers between devices, body(): lax.all_gather(pack_corners(*widen(reorder(index, order), 'tx', 'ty')), '...  70.6 us
    all_to_all x1, blocking collectives, body(): lax.all_to_all(both, 'angle', 0, 0, tiled=True, axis_index_groups=chip_gr...  31.5 us
    pallas_call x1, Pallas kernels, body(): pl.pallas_call(functools.partial(backward_kernel, tall), grid=(steps,), i...  20.5 us
    all_to_all x1, blocking collectives, step_and_smooth(): strips = lax.all_to_all(strips, ('tx', 'ty'), 0, 0, tiled=True)  14.8 us
    pallas_call x1, Pallas kernels, body(): pl.pallas_call(functools.partial(forward_kernel, tall), grid=(steps,), in...  14.2 us
    ppermute x2, waiting for transfers between devices, widen(): above = lax.ppermute(wide, axis_y, ring(ny, 1))  11.3 us
    ppermute x2, starting transfers between devices, widen(): right = unpack(lax.ppermute(pack(side(0)), axis_x, ring(nx, -1)))  8.92 us
    all_to_all x1, blocking collectives, body(): lax.all_to_all(grads, 'angle', 0, 0, tiled=True, axis_index_groups=core_g...  8.54 us
  transfers between devices with their start and end apart: 11, of which 8 were waited for; matrix products, arithmetic and copies ran while one was open for 2% of the time, Pallas kernels for 0%

profile of v5, /device:TPU:1, one launch (start us, length us, event | category | flops | bytes accessed | tf_op | source)
XLA Modules:
  0.0 248.2 jit_solution(9653183635514819612)
XLA Ops:
  7.2 0.0 copy-start
  7.2 0.0 copy-start.3
  7.2 0.0 all-gather.2.cloned.1.call-start
  7.2 1.2 convolution_bitcast_fusion
  8.5 0.2 fusion.36
  8.6 0.1 fusion.17
  8.7 0.1 fusion.22
  8.8 5.0 %collective-permute-start.1 = (f32[2,64,128]{2,1,0:T(8,128)S(1)}, f32[2,64,128]{2,1,0:T(8,128)S(1)}, u32[]{:S(2)}, u32[]{:S(2)}) collective-permute-start(f32[2,64,128]{2,1,0:T(8,128)S(1)} %fusion.22), channel_id=1, source_target_pairs={{0,8},{8,16},{16,24},{24,0},{1,9},{9,17},{17,25},{25,1},{2,10},{10... | collective-permute-start | bytes 196616 | tf_op jit(solution)/shard_map/ppermute | solution.py:203
  13.9 0.1 fusion.18
  14.0 0.1 fusion.23
  14.1 3.6 %collective-permute-start = (f32[2,64,128]{2,1,0:T(8,128)S(1)}, f32[2,64,128]{2,1,0:T(8,128)S(1)}, u32[]{:S(2)}, u32[]{:S(2)}) collective-permute-start(f32[2,64,128]{2,1,0:T(8,128)S(1)} %fusion.23), channel_id=1, source_target_pairs={{0,24},{8,0},{16,8},{24,16},{1,25},{9,1},{17,9},{25,17},{2,26},{10... | collective-permute-start | bytes 196616 | tf_op jit(solution)/shard_map/ppermute | solution.py:204
  17.7 0.1 fusion.35
  17.8 4.8 %collective-permute-done = f32[2,64,128]{2,1,0:T(8,128)S(1)} collective-permute-done((f32[2,64,128]{2,1,0:T(8,128)S(1)}, f32[2,64,128]{2,1,0:T(8,128)S(1)}, u32[]{:S(2)}, u32[]{:S(2)}) %collective-permute-start) | collective-permute-done | bytes 65568 | tf_op jit(solution)/shard_map/ppermute | solution.py:204
  22.6 0.1 fusion.39
  22.7 0.0 collective-permute-done.1
  22.7 0.1 fusion.40
  22.8 0.2 fusion.10
  23.0 3.2 %collective-permute-start.3 = (f32[4,2,64,128]{3,2,0,1:T(8,128)S(1)}, f32[4,2,64,128]{3,2,0,1:T(8,128)S(1)}, u32[]{:S(2)}, u32[]{:S(2)}) collective-permute-start(f32[4,2,64,128]{3,2,0,1:T(8,128)S(1)} %pad_maximum_fusion.2), channel_id=1, source_target_pairs={{0,7},{1,0},{2,1},{3,2},{4,3},{5,4},{6,5},{7,6},{8,15},{9,8},{10,9... | collective-permute-start | bytes 786440 | tf_op jit(solution)/shard_map/ppermute | solution.py:209
  26.2 2.4 collective-permute-start.2
  28.7 1.8 collective-permute-done.3
  30.4 0.2 fusion.34
  30.6 5.4 %collective-permute-done.2 = f32[4,2,64,128]{3,2,0,1:T(8,128)S(1)} collective-permute-done((f32[4,2,64,128]{3,2,0,1:T(8,128)S(1)}, f32[4,2,64,128]{3,2,0,1:T(8,128)S(1)}, u32[]{:S(2)}, u32[]{:S(2)}) %collective-permute-start.2) | collective-permute-done | bytes 262176 | tf_op jit(solution)/shard_map/ppermute | solution.py:208
  36.0 0.2 maximum_select_fusion
  36.3 1.0 maximum_maximum_fusion
  37.3 0.0 all-gather.2.cloned.1.call-update
  37.4 0.6 fusion.43
  37.9 0.6 add_multiply_fusion
  38.6 1.5 fusion.14
  40.2 0.2 convolution_bitcast_fusion.1
  40.4 70.6 %all-gather.2.cloned.1.call-done.index_ref = f32[64,320,128]{2,1,0:T(8,128)} async-done(((f32[4,320,128]{2,1,0:T(8,128)}), f32[64,320,128]{2,1,0:T(8,128)}) %all-gather.2.cloned.1.call-update) | async-done | bytes 10485776 | tf_op jit(solution)/shard_map/all_gather | solution.py:399
  111.0 14.2 %forward.1.field_ref = f32[64,2,2,64,128]{4,3,2,1,0:T(8,128)} custom-call(f32[64,320,128]{2,1,0:T(8,128)} %all-gather.2.cloned.1.call-done.index_ref, f32[2,2,192,128]{3,2,1,0:T(8,128)S(1)} %pad_maximum_fusion.start_ref), custom_call_target="tpu_custom_call" | custom-call | tf_op jit(solution)/shard_map/forward/pallas_call | solution.py:406
  125.2 0.9 copy_bitcast_fusion
  126.1 0.1 maximum_subtract_fusion
  126.2 0.1 fusion.37
  126.3 0.1 fusion.38
  126.4 0.1 fusion.28
  126.5 0.1 fusion.30
  126.6 5.3 %collective-permute-start.4 = (f32[1,64,128]{2,1,0:T(8,128)S(1)}, f32[1,64,128]{2,1,0:T(8,128)S(1)}, u32[]{:S(2)}, u32[]{:S(2)}) collective-permute-start(f32[1,64,128]{2,1,0:T(8,128)S(1)} %fusion.30), channel_id=1, source_target_pairs={{0,24},{8,0},{16,8},{24,16},{1,25},{9,1},{17,9},{25,17},{2,26},{10... | collective-permute-start | bytes 98312 | tf_op jit(solution)/shard_map/ppermute | solution.py:204
  131.9 0.1 fusion.27
  132.0 0.1 fusion.29
  132.1 1.9 collective-permute-start.5
  134.0 0.0 collective-permute-done.4
  134.1 0.1 fusion.41
  134.1 4.8 %collective-permute-done.5 = f32[1,64,128]{2,1,0:T(8,128)S(1)} collective-permute-done((f32[1,64,128]{2,1,0:T(8,128)S(1)}, f32[1,64,128]{2,1,0:T(8,128)S(1)}, u32[]{:S(2)}, u32[]{:S(2)}) %collective-permute-start.5) | collective-permute-done | bytes 32800 | tf_op jit(solution)/shard_map/ppermute | solution.py:203
  138.9 0.1 fusion.42
  139.0 0.1 fusion.20
  139.1 0.1 maximum_bitcast_fusion.1
  139.2 4.3 %collective-permute-start.7 = (f32[2,2,64,128]{3,2,1,0:T(8,128)S(1)}, f32[2,2,64,128]{3,2,1,0:T(8,128)S(1)}, u32[]{:S(2)}, u32[]{:S(2)}) collective-permute-start(f32[2,2,64,128]{3,2,1,0:T(8,128)S(1)} %pad_maximum_fusion.3), channel_id=1, source_target_pairs={{0,7},{1,0},{2,1},{3,2},{4,3},{5,4},{6,5},{7,6},{8,15},{9,8},{10,9... | collective-permute-start | bytes 393224 | tf_op jit(solution)/shard_map/ppermute | solution.py:209
  143.6 1.9 collective-permute-start.6
  145.5 0.0 collective-permute-done.7
  145.5 5.9 %collective-permute-done.6 = f32[2,2,64,128]{3,2,1,0:T(8,128)S(1)} collective-permute-done((f32[2,2,64,128]{3,2,1,0:T(8,128)S(1)}, f32[2,2,64,128]{3,2,1,0:T(8,128)S(1)}, u32[]{:S(2)}, u32[]{:S(2)}) %collective-permute-start.6) | collective-permute-done | bytes 131104 | tf_op jit(solution)/shard_map/ppermute | solution.py:208
  151.4 20.5 %backward.1 = f32[2,8,4,64,128]{4,3,2,1,0:T(8,128)S(1)} custom-call(f32[64,320,128]{2,1,0:T(8,128)} %all-gather.2.cloned.1.call-done.index_ref, f32[2,2,192,128]{3,2,1,0:T(8,128)S(1)} %pad_maximum_fusion.1.start_ref, f32[64,2,2,64,128]{4,3,2,1,0:T(8,128)} %forward.1.field_ref), custom_call_target="tpu_custom_call" | custom-call | tf_op jit(solution)/shard_map/backward/pallas_call | solution.py:430
  171.9 0.0 copy-start.1
  171.9 0.0 copy-start.2
  171.9 8.5 %all_to_all.15 = f32[2,8,4,64,128]{4,3,2,1,0:T(8,128)S(1)} all-to-all(f32[2,8,4,64,128]{4,3,2,1,0:T(8,128)S(1)} %backward.1), channel_id=1, replica_groups={{0,32},{64,96},{128,160},{192,224},{256,288},{320,352},{384,416},{448,4..., dimensions={0} | all-to-all | bytes 4194304 | tf_op jit(solution)/shard_map/all_to_all | solution.py:445
  180.5 0.1 fusion
  180.6 31.5 %all_to_all.16.parts_ref = f32[8,4,64,128]{3,2,1,0:T(8,128)S(1)} all-to-all(f32[8,4,64,128]{3,2,1,0:T(8,128)S(1)} %fusion), channel_id=1, replica_groups={{0,64,128,192,256,320,384,448},{32,96,160,224,288,352,416,480},{1,65,12..., dimensions={0} | all-to-all | bytes 2097152 | tf_op jit(solution)/shard_map/all_to_all | solution.py:447
  212.1 1.0 share.1
  213.1 14.8 %all_to_all.17.strips_ref = f32[32,16,128]{2,1,0:T(8,128)S(1)} all-to-all(f32[32,16,128]{2,1,0:T(8,128)S(1)} %get-tuple-element.10), channel_id=1, replica_groups=mesh['angle'=16,'tx'=4,'ty'=8] {'tx','ty'}, dimensions={0} | all-to-all | bytes 524288 | tf_op jit(solution)/shard_map/all_to_all | solution.py:355
  228.0 3.6 %collective-permute-start.8 = (f32[288,128]{1,0:T(8,128)S(1)}, f32[288,128]{1,0:T(8,128)S(1)}, u32[]{:S(2)}, u32[]{:S(2)}) collective-permute-start(f32[288,128]{1,0:T(8,128)S(1)} %get-tuple-element.12), channel_id=1, source_target_pairs={{0,32},{32,64},{64,96},{96,128},{128,160},{160,192},{192,224},{224... | collective-permute-start | bytes 442376 | tf_op jit(solution)/shard_map/ppermute | solution.py:364
  231.6 0.2 collective-permute-start.9
  231.8 1.9 collective-permute-done.8.low_ref
  233.7 2.8 %collective-permute-done.9.high_ref = f32[288,128]{1,0:T(8,128)S(1)} collective-permute-done((f32[288,128]{1,0:T(8,128)S(1)}, f32[288,128]{1,0:T(8,128)S(1)}, u32[]{:S(2)}, u32[]{:S(2)}) %collective-permute-start.9) | collective-permute-done | bytes 147488 | tf_op jit(solution)/shard_map/ppermute | solution.py:365
  236.5 4.8 %smooth.1 = f32[4,64,128]{2,1,0:T(8,128)} custom-call(f32[4,64,128]{2,1,0:T(8,128)S(1)} %get-tuple-element.9.vol_ref, f32[8,16,128]{2,1,0:T(8,128)S(1)} %get-tuple-element.11.near_ref, f32[288,128]{1,0:T(8,128)S(1)} %collective-permute-done.8.low_ref, f32[288,128]{1,0:T(8,128)S(1)} %collective-permute-done.9.high_ref), custom_call_target="tpu_custom_call" | custom-call | tf_op jit(solution)/shard_map/smooth/pallas_call | solution.py:367
  (24 shorter events, 0.3 us)
Async XLA Ops:
  7.2 33.0 %copy-start = (f32[2,1,64,128]{3,2,1,0:T(8,128)S(1)}, f32[2,1,64,128]{3,2,1,0:T(8,128)}, u32[]{:S(2)}) copy-start(f32[2,1,64,128]{3,2,1,0:T(8,128)} %param.5) | copy-start | bytes 196612
  7.2 33.0 %copy-start.3 = (f32[128,128,1]{1,0,2:T(8,128)S(1)}, f32[128,128,1]{1,0,2:T(8,128)}, u32[]{:S(2)}) copy-start(f32[128,128,1]{1,0,2:T(8,128)} %constant.49) | copy-start | bytes 196612
  7.2 30.2 %copy-start.4 = (s32[1,2]{1,0:T(1,128)S(1)}, s32[1,2]{1,0:T(1,128)}, u32[]{:S(2)}) copy-start(s32[1,2]{1,0:T(1,128)} %param.6) | copy-start | bytes 28
  7.2 103.8 %all-gather.2.cloned.1.call-start = ((), (), s32[]{:S(2)}) async-start(), calls=%async_computation.3 | async-start | bytes 11141120 | tf_op jit(solution)/shard_map/all_gather | solution.py:399
  8.8 13.8 %collective-permute-start.1 = (f32[2,64,128]{2,1,0:T(8,128)S(1)}, f32[2,64,128]{2,1,0:T(8,128)S(1)}, u32[]{:S(2)}, u32[]{:S(2)}) collective-permute-start(f32[2,64,128]{2,1,0:T(8,128)S(1)} %fusion.22), channel_id=1, source_target_pairs={{0,8},{8,16},{16,24},{24,0},{1,9},{9,17},{17,25},{25,1},{2,10},{10... | collective-permute-start | bytes 196616 | tf_op jit(solution)/shard_map/ppermute | solution.py:203
  14.1 8.5 %collective-permute-start = (f32[2,64,128]{2,1,0:T(8,128)S(1)}, f32[2,64,128]{2,1,0:T(8,128)S(1)}, u32[]{:S(2)}, u32[]{:S(2)}) collective-permute-start(f32[2,64,128]{2,1,0:T(8,128)S(1)} %fusion.23), channel_id=1, source_target_pairs={{0,24},{8,0},{16,8},{24,16},{1,25},{9,1},{17,9},{25,17},{2,26},{10... | collective-permute-start | bytes 196616 | tf_op jit(solution)/shard_map/ppermute | solution.py:204
  23.0 7.4 %collective-permute-start.3 = (f32[4,2,64,128]{3,2,0,1:T(8,128)S(1)}, f32[4,2,64,128]{3,2,0,1:T(8,128)S(1)}, u32[]{:S(2)}, u32[]{:S(2)}) collective-permute-start(f32[4,2,64,128]{3,2,0,1:T(8,128)S(1)} %pad_maximum_fusion.2), channel_id=1, source_target_pairs={{0,7},{1,0},{2,1},{3,2},{4,3},{5,4},{6,5},{7,6},{8,15},{9,8},{10,9... | collective-permute-start | bytes 786440 | tf_op jit(solution)/shard_map/ppermute | solution.py:209
  26.2 9.8 %collective-permute-start.2 = (f32[4,2,64,128]{3,2,0,1:T(8,128)S(1)}, f32[4,2,64,128]{3,2,0,1:T(8,128)S(1)}, u32[]{:S(2)}, u32[]{:S(2)}) collective-permute-start(f32[4,2,64,128]{3,2,0,1:T(8,128)S(1)} %pad_maximum_fusion.2), channel_id=1, source_target_pairs={{0,1},{1,2},{2,3},{3,4},{4,5},{5,6},{6,7},{7,0},{8,9},{9,10},{10,1... | collective-permute-start | bytes 786440 | tf_op jit(solution)/shard_map/ppermute | solution.py:208
  126.6 7.4 %collective-permute-start.4 = (f32[1,64,128]{2,1,0:T(8,128)S(1)}, f32[1,64,128]{2,1,0:T(8,128)S(1)}, u32[]{:S(2)}, u32[]{:S(2)}) collective-permute-start(f32[1,64,128]{2,1,0:T(8,128)S(1)} %fusion.30), channel_id=1, source_target_pairs={{0,24},{8,0},{16,8},{24,16},{1,25},{9,1},{17,9},{25,17},{2,26},{10... | collective-permute-start | bytes 98312 | tf_op jit(solution)/shard_map/ppermute | solution.py:204
  132.1 6.8 %collective-permute-start.5 = (f32[1,64,128]{2,1,0:T(8,128)S(1)}, f32[1,64,128]{2,1,0:T(8,128)S(1)}, u32[]{:S(2)}, u32[]{:S(2)}) collective-permute-start(f32[1,64,128]{2,1,0:T(8,128)S(1)} %fusion.29), channel_id=1, source_target_pairs={{0,8},{8,16},{16,24},{24,0},{1,9},{9,17},{17,25},{25,1},{2,10},{10... | collective-permute-start | bytes 98312 | tf_op jit(solution)/shard_map/ppermute | solution.py:203
  139.2 6.2 %collective-permute-start.7 = (f32[2,2,64,128]{3,2,1,0:T(8,128)S(1)}, f32[2,2,64,128]{3,2,1,0:T(8,128)S(1)}, u32[]{:S(2)}, u32[]{:S(2)}) collective-permute-start(f32[2,2,64,128]{3,2,1,0:T(8,128)S(1)} %pad_maximum_fusion.3), channel_id=1, source_target_pairs={{0,7},{1,0},{2,1},{3,2},{4,3},{5,4},{6,5},{7,6},{8,15},{9,8},{10,9... | collective-permute-start | bytes 393224 | tf_op jit(solution)/shard_map/ppermute | solution.py:209
  143.6 7.8 %collective-permute-start.6 = (f32[2,2,64,128]{3,2,1,0:T(8,128)S(1)}, f32[2,2,64,128]{3,2,1,0:T(8,128)S(1)}, u32[]{:S(2)}, u32[]{:S(2)}) collective-permute-start(f32[2,2,64,128]{3,2,1,0:T(8,128)S(1)} %pad_maximum_fusion.3), channel_id=1, source_target_pairs={{0,1},{1,2},{2,3},{3,4},{4,5},{5,6},{6,7},{7,0},{8,9},{9,10},{10,1... | collective-permute-start | bytes 393224 | tf_op jit(solution)/shard_map/ppermute | solution.py:208
  171.9 40.2 %copy-start.1 = (f32[4,64,128]{2,1,0:T(8,128)S(1)}, f32[4,64,128]{2,1,0:T(8,128)}, u32[]{:S(2)}) copy-start(f32[4,64,128]{2,1,0:T(8,128)} %index_ref.1) | copy-start | bytes 393220
  171.9 40.2 %copy-start.2 = (f32[128,128]{1,0:T(8,128)S(1)}, f32[128,128]{1,0:T(8,128)}, u32[]{:S(2)}) copy-start(f32[128,128]{1,0:T(8,128)} %constant.48.order_ref) | copy-start | bytes 196612
  228.0 5.7 %collective-permute-start.8 = (f32[288,128]{1,0:T(8,128)S(1)}, f32[288,128]{1,0:T(8,128)S(1)}, u32[]{:S(2)}, u32[]{:S(2)}) collective-permute-start(f32[288,128]{1,0:T(8,128)S(1)} %get-tuple-element.12), channel_id=1, source_target_pairs={{0,32},{32,64},{64,96},{96,128},{128,160},{160,192},{192,224},{224... | collective-permute-start | bytes 442376 | tf_op jit(solution)/shard_map/ppermute | solution.py:364
  231.6 4.9 %collective-permute-start.9 = (f32[288,128]{1,0:T(8,128)S(1)}, f32[288,128]{1,0:T(8,128)S(1)}, u32[]{:S(2)}, u32[]{:S(2)}) collective-permute-start(f32[288,128]{1,0:T(8,128)S(1)} %get-tuple-element.13), channel_id=1, source_target_pairs={{0,480},{32,0},{64,32},{96,64},{128,96},{160,128},{192,160},{224,1... | collective-permute-start | bytes 442376 | tf_op jit(solution)/shard_map/ppermute | solution.py:365
Sparse Core Ops, SparseCore 0:
  37.4 73.5 all-gather.1

commit v6 on v4

--- a/solution.py
+++ b/solution.py
@@ -68,44 +68,26 @@
     return lane == 0, lane == 127
 
 
-def near_lanes():
-    lane = lax.broadcasted_iota(jnp.int32, (8, 128), 1)
-    return (lane < 32) | (lane >= 96)
-
-
-def near_index(near_ref, pair, odd, half, c):
-    tall = near_ref.shape[1] // 3
-    if half == 0:
-        return near_ref[pair, pl.ds(tall * odd + 8 * c, 8), :]
-    rows = near_ref[pair, pl.ds(2 * tall + 8 * c, 8), :]
-    return pltpu.roll(rows, 64, 1) if odd else rows
-
-
-def full_index(near_ref, far_ref, pair, odd, half, c, is_near):
-    tall = near_ref.shape[1] // 3
-    edge = tall // 4
-    rim = edge // 8
-    cn = c - rim
-    corner = 4 * edge + tall + edge * odd
+def near_index(near_ref, j, half, c):
+    tall = near_ref.shape[1] // 2
+    return near_ref[j, pl.ds(tall * half + 8 * c, 8), :]
+
+
+def full_index(near_ref, far_ref, j, half, c):
+    edge = far_ref.shape[1] // 3
+    cn = c - edge // 8
+    tall = near_ref.shape[1] // 2
     if 0 <= cn < tall // 8:
-        if half == 0:
-            return near_index(near_ref, pair, odd, half, cn)
-        inner = near_ref[pair, pl.ds(2 * tall + 8 * cn, 8), :]
-        outer = far_ref[pair, pl.ds(4 * edge + 8 * cn, 8), :]
-        if odd:
-            return pltpu.roll(jnp.where(is_near, outer, inner), 64, 1)
-        return jnp.where(is_near, inner, outer)
+        return near_index(near_ref, j, half, cn)
     if cn < 0:
-        if half == 0:
-            return far_ref[pair, pl.ds(2 * edge * odd + 8 * c, 8), :]
-        return far_ref[pair, pl.ds(corner + 8 * c, 8), :]
+        return far_ref[j, pl.ds(2 * edge * half + 8 * c, 8), :]
     c = cn - tall // 8
     if half == 0:
-        return far_ref[pair, pl.ds(2 * edge * odd + edge + 8 * c, 8), :]
-    return pltpu.roll(far_ref[pair, pl.ds(corner + 8 * c, 8), :], 64, 1)
-
-
-def forward_kernel(near_ref, start_ref, field_ref, buf):
+        return far_ref[j, pl.ds(edge + 8 * c, 8), :]
+    return pltpu.roll(far_ref[j, pl.ds(2 * edge + 8 * c, 8), :], 64, 1)
+
+
+def forward_kernel(near_ref, start_ref, field_ref, last_ref, buf):
     tall = start_ref.shape[2]
     chunks = tall // 8
     own_first = (tall - field_ref.shape[2]) // 16
@@ -125,7 +107,7 @@
             re, sum_re = neighbours(buf, odd, 0, row, first, last)
             im, sum_im = neighbours(buf, odd, 1, row, first, last)
             for half in range(2):
-                cosine, sine = phase_factor(near_index(near_ref, pair, odd, half, c))
+                cosine, sine = phase_factor(near_index(near_ref, 2 * pair + odd, half, c))
                 wre = sum_re[half] + (im[half] + im[half])
                 wim = sum_im[half] - (re[half] + re[half])
                 nre = cosine * wre - sine * wim
@@ -146,6 +128,10 @@
                 step(pair, 0, k, chunks - k)
                 step(pair, 1, k, chunks - k)
 
+            if k == own_first - 1:
+                for q in range(4):
+                    last_ref[q // 2, q % 2] = buf[0, q, 8 + 8 * own_first : 8 + 8 * own_last, :]
+
 
 def backward_kernel(near_ref, far_ref, start_ref, early_ref, late_ref, grad_ref, buf):
     tall = start_ref.shape[2]
@@ -155,7 +141,6 @@
     rim = own_first // 2
     pid = pl.program_id(0)
     first, last = lane_masks()
-    is_near = near_lanes()
     slab = GROUP // 2
 
     @pl.when(pid == 0)
@@ -171,9 +156,9 @@
             fim = field_ref[j, 1, own, :]
             grad_ref[j // slab, 0, j % slab, own, :] = phase_scale * (aim * fre - are * fim)
         if wide:
-            index = full_index(near_ref, far_ref, pair, odd, half, c, is_near)
+            index = full_index(near_ref, far_ref, j, half, c)
         else:
-            index = near_index(near_ref, pair, odd, half, c - rim)
+            index = near_index(near_ref, j, half, c - rim)
         cosine, sine = phase_factor(index)
         row = pl.ds(8 + 8 * c, 8)
         buf[odd, half, row, :] = cosine * are + sine * aim
@@ -231,9 +216,9 @@
     return above, below
 
 
-def widen(block, reach):
+def widen(block):
     wide = widen_x(block)
-    above, below = rows_around(wide, 0, reach)
+    above, below = rows_around(wide, 0, wide.shape[2])
     return jnp.concatenate([above, wide, below], axis=2)
 
 
@@ -248,16 +233,11 @@
     inner = (lane < cols // 4) | (lane >= cols - cols // 4)
     wide = widen_x(index)
     above, below = rows_around(wide, 0, reach)
-    tall = rows + 2 * reach
-    sides = jnp.concatenate([above[:, 1], wide[:, 1], below[:, 1]], axis=1).reshape(slab // 2, 2, tall, cols)
-    even, odd = sides[:, 0], turned(sides[:, 1])
-    middle = jnp.concatenate([above[:, 0], wide[:, 0], below[:, 0]], axis=1).reshape(slab // 2, 2 * tall, cols)
-    near = jnp.concatenate([middle, jnp.where(inner, even, odd)], axis=1)
+    near = jnp.concatenate([above, wide, below], axis=2).reshape(slab, 2 * (rows + 2 * reach), cols)
     near = lax.all_gather(near, "angle", axis=0, tiled=True)
     above, below = rows_around(wide, reach, 2 * reach)
-    middle = jnp.concatenate([above[:, 0], below[:, 0]], axis=1).reshape(slab // 2, 4 * reach, cols)
-    corners = jnp.where(inner, above[:, 1], turned(below[:, 1])).reshape(slab // 2, 2 * reach, cols)
-    far = jnp.concatenate([middle, jnp.where(inner, odd, even), corners], axis=1)
+    corners = jnp.where(inner, above[:, 1], turned(below[:, 1]))
+    far = jnp.concatenate([above[:, 0], below[:, 0], corners], axis=1)
     far = lax.all_gather(far, "angle", axis=0, tiled=True)
     return near, far
 
@@ -439,10 +419,10 @@
     near, far = gather_index(index)
 
     steps = nz // GROUP
-    near_block = (GROUP // 2,) + near.shape[1:]
-    far_block = (GROUP // 2,) + far.shape[1:]
+    near_block = (GROUP,) + near.shape[1:]
+    far_block = (GROUP,) + far.shape[1:]
     field_block = (GROUP, 2, rows, cols)
-    params = pltpu.CompilerParams(dimension_semantics=("arbitrary",), vmem_limit_bytes=40 * 2**20)
+    params = pltpu.CompilerParams(dimension_semantics=("arbitrary",), vmem_limit_bytes=61 * 2**20)
 
     def forward(start, first_step):
         whole = pl.BlockSpec(start.shape, lambda i: (0, 0, 0, 0))
@@ -450,22 +430,29 @@
             forward_kernel,
             grid=(steps // 2,),
             in_specs=[pl.BlockSpec(near_block, lambda i: (i + first_step, 0, 0)), whole],
-            out_specs=pl.BlockSpec(field_block, lambda i: (i, 0, 0, 0)),
-            out_shape=jax.ShapeDtypeStruct((nz // 2, 2, rows, cols), jnp.float32),
+            out_specs=(
+                pl.BlockSpec(field_block, lambda i: (i, 0, 0, 0)),
+                pl.BlockSpec((2, 2, rows, cols), lambda i: (0, 0, 0, 0)),
+            ),
+            out_shape=(
+                jax.ShapeDtypeStruct((nz // 2, 2, rows, cols), jnp.float32),
+                jax.ShapeDtypeStruct((2, 2, rows, cols), jnp.float32),
+            ),
             scratch_shapes=[pltpu.VMEM((2, 4, rows + 2 * reach + 16, cols), jnp.float32)],
             compiler_params=params,
             name="forward",
         )(near, start)
 
-    early = forward(incident(illum, (rows, cols), reach), 0)
-    late = forward(widen(early[nz // 2 - 1], reach), steps // 2)
+    early, reached = forward(incident(illum, (rows, cols), reach), 0)
+    above, below = rows_around(reached, 0, reach)
+    late, reached = forward(jnp.concatenate([above, reached, below], axis=2), steps // 2)
 
     back = TURN.conjugate() ** nz
     back = back / abs(back)
     target_re = back.real * measured[0] - back.imag * measured[1]
     target_im = back.real * measured[1] + back.imag * measured[0]
-    residual = late[nz // 2 - 1] - jnp.concatenate([target_re, target_im], axis=0)
-    adjoint = widen(residual, rows)
+    residual = reached[:, 0] - jnp.concatenate([target_re, target_im], axis=0)
+    adjoint = widen(residual)
 
     grads = pl.pallas_call(
         backward_kernel,

time: 243 us -> 247 us (1.016)
  starting transfers between devices: 57.3 us -> 49.8 us
  local copies, waits for them, and re-layouts: 9.33 us -> 3.04 us
  waiting for transfers between devices: 70.5 us -> 76.4 us
  Pallas kernels: 29.6 us -> 35.4 us
  other arithmetic: 5.73 us -> 9.97 us
    all_gather x1, waiting for transfers between devices: 42.8 us -> 52 us  [gather_index(): near = lax.all_gather(near, 'angle', axis=0, tiled=True)]
    unnamed x14 -> x7, local copies, waits for them, and re-layouts: 6.87 us -> 0.03 us
    ppermute x3 -> x2, starting transfers between devices: 14.2 us -> 9.08 us  [widen_x(): left = unpack(lax.ppermute(pack(block[:, :, half:]), 'tx', ring(nx, 1)))]
    pallas_call x2, Pallas kernels: 10.1 us -> 14.6 us  [forward(): pl.pallas_call(forward_kernel, grid=(steps // 2,), in_specs=[pl.BlockSpec...]
    ppermute x3 -> x2, waiting for transfers between devices: 12.4 us -> 8.65 us  [widen_x(): right = unpack(lax.ppermute(pack(block[:, :, :half]), 'tx', ring(nx, -1)))]
    ppermute x3 -> x2, starting transfers between devices: 9.2 us -> 6.94 us  [widen_x(): right = unpack(lax.ppermute(pack(block[:, :, :half]), 'tx', ring(nx, -1)))]
  transfers between devices with their start and end apart: 18 -> 16, of which waited for: 12 -> 11; matrix products, arithmetic and copies ran while one was open for 2% -> 4% of each run, Pallas kernels for 4% -> 6%
where the time goes in v6:
time: 247 us; the launch traced here: 246 us
  waiting for transfers between devices  76.4 us (31%)
  blocking collectives  57.4 us (23%)
  starting transfers between devices  49.8 us (20%)
  Pallas kernels  35.4 us (14%)
  between operations  14.4 us (6%)
  other arithmetic  9.97 us (4%)
  local copies, waits for them, and re-layouts  3.04 us (1%)
    all_gather x1, waiting for transfers between devices, gather_index(): near = lax.all_gather(near, 'angle', axis=0, tiled=True)  52 us
    all_to_all x1, blocking collectives, body(): lax.all_to_all(both, 'angle', 0, 0, tiled=True, axis_index_groups=chip_gr...  31.7 us
    ppermute x4, starting transfers between devices, rows_around(): below = lax.ppermute(wide[:, :, start:stop], 'ty', ring(ny, -1))  18.1 us
    all_to_all x1, blocking collectives, step_and_smooth(): strips = lax.all_to_all(strips, ('tx', 'ty'), 0, 0, tiled=True)  15.6 us
    pallas_call x1, Pallas kernels, body(): pl.pallas_call(backward_kernel, grid=(steps,), in_specs=[pl.BlockSpec(nea...  15.2 us
    pallas_call x2, Pallas kernels, forward(): pl.pallas_call(forward_kernel, grid=(steps // 2,), in_specs=[pl.BlockSpec...  14.6 us
    ppermute x4, starting transfers between devices, rows_around(): lax.ppermute(wide[:, :, rows - stop:rows - start], 'ty', ring(ny, 1))  11.8 us
    all_to_all x1, blocking collectives, body(): lax.all_to_all(grads, 'angle', 0, 0, tiled=True, axis_index_groups=core_g...  10.1 us
  transfers between devices with their start and end apart: 16, of which 11 were waited for; matrix products, arithmetic and copies ran while one was open for 4% of the time, Pallas kernels for 6%

profile of v6, /device:TPU:1, one launch (start us, length us, event | category | flops | bytes accessed | tf_op | source)
XLA Modules:
  0.0 246.3 jit_solution(8751370449637351354)
XLA Ops:
  7.2 0.0 all-gather.3.cloned.1.call-start
  7.2 1.1 fusion.11
  8.3 0.1 pad_maximum_fusion.8
  8.4 5.0 %collective-permute-start.1 = (f32[2,64,128]{2,1,0:T(8,128)S(1)}, f32[2,64,128]{2,1,0:T(8,128)S(1)}, u32[]{:S(2)}, u32[]{:S(2)}) collective-permute-start(f32[2,64,128]{2,1,0:T(8,128)S(1)} %pad_maximum_fusion.8), channel_id=1, source_target_pairs={{0,8},{8,16},{16,24},{24,0},{1,9},{9,17},{17,25},{25,1},{2,10},{10... | collective-permute-start | bytes 196616 | tf_op jit(solution)/shard_map/ppermute | solution.py:206
  13.4 0.1 pad_maximum_fusion.7
  13.5 3.6 %collective-permute-start = (f32[2,64,128]{2,1,0:T(8,128)S(1)}, f32[2,64,128]{2,1,0:T(8,128)S(1)}, u32[]{:S(2)}, u32[]{:S(2)}) collective-permute-start(f32[2,64,128]{2,1,0:T(8,128)S(1)} %pad_maximum_fusion.7), channel_id=1, source_target_pairs={{0,24},{8,0},{16,8},{24,16},{1,25},{9,1},{17,9},{25,17},{2,26},{10... | collective-permute-start | bytes 196616 | tf_op jit(solution)/shard_map/ppermute | solution.py:207
  17.1 0.1 fusion.15
  17.2 4.8 %collective-permute-done = f32[2,64,128]{2,1,0:T(8,128)S(1)} collective-permute-done((f32[2,64,128]{2,1,0:T(8,128)S(1)}, f32[2,64,128]{2,1,0:T(8,128)S(1)}, u32[]{:S(2)}, u32[]{:S(2)}) %collective-permute-start) | collective-permute-done | bytes 65568 | tf_op jit(solution)/shard_map/ppermute | solution.py:207
  22.0 0.1 fusion.14
  22.1 0.1 maximum_bitcast_fusion
  22.2 0.9 fusion.6
  23.1 3.7 %collective-permute-start.2 = (f32[4,2,32,128]{3,2,0,1:T(8,128)S(1)}, f32[4,2,32,128]{3,2,0,1:T(8,128)S(1)}, u32[]{:S(2)}, u32[]{:S(2)}) collective-permute-start(f32[4,2,32,128]{3,2,0,1:T(8,128)S(1)} %fusion.6), channel_id=1, source_target_pairs={{0,1},{1,2},{2,3},{3,4},{4,5},{5,6},{6,7},{7,0},{8,9},{9,10},{10,1... | collective-permute-start | bytes 393224 | tf_op jit(solution)/shard_map/ppermute | solution.py:214
  26.8 3.7 %collective-permute-start.3 = (f32[4,2,32,128]{3,2,1,0:T(8,128)S(1)}, f32[4,2,32,128]{3,2,1,0:T(8,128)S(1)}, u32[]{:S(2)}, u32[]{:S(2)}) collective-permute-start(f32[4,2,32,128]{3,2,1,0:T(8,128)S(1)} %copy.15), channel_id=1, source_target_pairs={{0,7},{1,0},{2,1},{3,2},{4,3},{5,4},{6,5},{7,6},{8,15},{9,8},{10,9... | collective-permute-start | bytes 393224 | tf_op jit(solution)/shard_map/ppermute | solution.py:215
  30.6 0.4 collective-permute-done.2
  30.9 1.6 collective-permute-done.3
  32.5 0.9 pad_maximum_fusion
  33.4 0.0 all-gather.3.cloned.1.call-update
  33.4 0.0 all-gather.5.cloned.1.call-start
  33.5 3.1 %collective-permute-start.4 = (f32[4,2,32,128]{3,2,1,0:T(8,128)S(1)}, f32[4,2,32,128]{3,2,1,0:T(8,128)S(1)}, u32[]{:S(2)}, u32[]{:S(2)}) collective-permute-start(f32[4,2,32,128]{3,2,1,0:T(8,128)S(1)} %copy.15), channel_id=1, source_target_pairs={{0,1},{1,2},{2,3},{3,4},{4,5},{5,6},{6,7},{7,0},{8,9},{9,10},{10,1... | collective-permute-start | bytes 393224 | tf_op jit(solution)/shard_map/ppermute | solution.py:214
  36.6 4.6 %collective-permute-start.5 = (f32[4,2,32,128]{3,2,0,1:T(8,128)S(1)}, f32[4,2,32,128]{3,2,0,1:T(8,128)S(1)}, u32[]{:S(2)}, u32[]{:S(2)}) collective-permute-start(f32[4,2,32,128]{3,2,0,1:T(8,128)S(1)} %fusion.6), channel_id=1, source_target_pairs={{0,7},{1,0},{2,1},{3,2},{4,3},{5,4},{6,5},{7,6},{8,15},{9,8},{10,9... | collective-permute-start | bytes 393224 | tf_op jit(solution)/shard_map/ppermute | solution.py:215
  41.2 0.4 collective-permute-done.4
  41.6 1.5 collective-permute-done.5
  43.2 0.1 fusion.13
  43.3 0.1 fusion.7
  43.4 0.7 pad_maximum_fusion.5
  44.1 0.0 all-gather.5.cloned.1.call-update
  44.1 0.6 fusion.18
  44.7 0.6 add_multiply_fusion
  45.4 1.2 fusion.9
  46.6 0.7 pad_maximum_fusion.3.start_ref
  47.3 52.0 %all-gather.3.cloned.1.call-done.near_ref = f32[64,256,128]{2,1,0:T(8,128)} async-done(((f32[4,256,128]{2,1,0:T(8,128)}), f32[64,256,128]{2,1,0:T(8,128)}) %all-gather.3.cloned.1.call-update) | async-done | bytes 8388624 | tf_op jit(solution)/shard_map/all_gather | solution.py:237
  99.3 7.3 %forward.2 = (f32[32,2,64,128]{3,2,1,0:T(8,128)}, f32[2,2,64,128]{3,2,1,0:T(8,128)}) custom-call(f32[64,256,128]{2,1,0:T(8,128)} %all-gather.3.cloned.1.call-done.near_ref, f32[2,2,128,128]{3,2,1,0:T(8,128)} %pad_maximum_fusion.3.start_ref), custom_call_target="tpu_custom_call" | custom-call | tf_op jit(solution)/shard_map/forward/pallas_call | solution.py:429
  106.6 0.9 fusion.10
  107.5 3.1 %collective-permute-start.6 = (f32[2,2,32,128]{3,2,1,0:T(8,128)S(1)}, f32[2,2,32,128]{3,2,1,0:T(8,128)S(1)}, u32[]{:S(2)}, u32[]{:S(2)}) collective-permute-start(f32[2,2,32,128]{3,2,1,0:T(8,128)S(1)} %get-tuple-element.22), channel_id=1, source_target_pairs={{0,1},{1,2},{2,3},{3,4},{4,5},{5,6},{6,7},{7,0},{8,9},{9,10},{10,1... | collective-permute-start | bytes 196616 | tf_op jit(solution)/shard_map/ppermute | solution.py:214
  110.6 4.3 %collective-permute-start.7 = (f32[2,2,32,128]{3,2,1,0:T(8,128)S(1)}, f32[2,2,32,128]{3,2,1,0:T(8,128)S(1)}, u32[]{:S(2)}, u32[]{:S(2)}) collective-permute-start(f32[2,2,32,128]{3,2,1,0:T(8,128)S(1)} %get-tuple-element.23), channel_id=1, source_target_pairs={{0,7},{1,0},{2,1},{3,2},{4,3},{5,4},{6,5},{7,6},{8,15},{9,8},{10,9... | collective-permute-start | bytes 196616 | tf_op jit(solution)/shard_map/ppermute | solution.py:215
  114.9 1.3 collective-permute-done.7
  116.2 1.6 pad_maximum_fusion.4.start_ref
  117.8 7.3 %forward.3 = (f32[32,2,64,128]{3,2,1,0:T(8,128)}, f32[2,2,64,128]{3,2,1,0:T(8,128)}) custom-call(f32[64,256,128]{2,1,0:T(8,128)} %all-gather.3.cloned.1.call-done.near_ref, f32[2,2,128,128]{3,2,1,0:T(8,128)} %pad_maximum_fusion.4.start_ref), custom_call_target="tpu_custom_call" | custom-call | tf_op jit(solution)/shard_map/forward/pallas_call | solution.py:429
  125.1 0.9 maximum_subtract_fusion.1
  126.0 0.1 fusion.12
  126.1 0.1 pad_maximum_fusion.10
  126.2 4.0 %collective-permute-start.9 = (f32[1,64,128]{2,1,0:T(8,128)S(1)}, f32[1,64,128]{2,1,0:T(8,128)S(1)}, u32[]{:S(2)}, u32[]{:S(2)}) collective-permute-start(f32[1,64,128]{2,1,0:T(8,128)S(1)} %pad_maximum_fusion.10), channel_id=1, source_target_pairs={{0,8},{8,16},{16,24},{24,0},{1,9},{9,17},{17,25},{25,1},{2,10},{10... | collective-permute-start | bytes 98312 | tf_op jit(solution)/shard_map/ppermute | solution.py:206
  130.2 0.9 maximum_subtract_fusion
  131.1 0.1 pad_maximum_fusion.9
  131.1 3.4 %collective-permute-start.8 = (f32[1,64,128]{2,1,0:T(8,128)S(1)}, f32[1,64,128]{2,1,0:T(8,128)S(1)}, u32[]{:S(2)}, u32[]{:S(2)}) collective-permute-start(f32[1,64,128]{2,1,0:T(8,128)S(1)} %pad_maximum_fusion.9), channel_id=1, source_target_pairs={{0,24},{8,0},{16,8},{24,16},{1,25},{9,1},{17,9},{25,17},{2,26},{10... | collective-permute-start | bytes 98312 | tf_op jit(solution)/shard_map/ppermute | solution.py:207
  134.5 0.1 fusion.17
  134.6 3.9 %collective-permute-done.8 = f32[1,64,128]{2,1,0:T(8,128)S(1)} collective-permute-done((f32[1,64,128]{2,1,0:T(8,128)S(1)}, f32[1,64,128]{2,1,0:T(8,128)S(1)}, u32[]{:S(2)}, u32[]{:S(2)}) %collective-permute-start.8) | collective-permute-done | bytes 32800 | tf_op jit(solution)/shard_map/ppermute | solution.py:207
  138.4 0.1 fusion.16
  138.5 0.1 maximum_bitcast_fusion.1
  138.6 5.4 %collective-permute-start.11 = (f32[2,2,64,128]{3,2,1,0:T(8,128)S(1)}, f32[2,2,64,128]{3,2,1,0:T(8,128)S(1)}, u32[]{:S(2)}, u32[]{:S(2)}) collective-permute-start(f32[2,2,64,128]{3,2,1,0:T(8,128)S(1)} %pad_maximum_fusion.6), channel_id=1, source_target_pairs={{0,7},{1,0},{2,1},{3,2},{4,3},{5,4},{6,5},{7,6},{8,15},{9,8},{10,9... | collective-permute-start | bytes 393224 | tf_op jit(solution)/shard_map/ppermute | solution.py:215
  144.0 1.9 collective-permute-start.10
  146.0 5.9 %collective-permute-done.10 = f32[2,2,64,128]{3,2,1,0:T(8,128)S(1)} collective-permute-done((f32[2,2,64,128]{3,2,1,0:T(8,128)S(1)}, f32[2,2,64,128]{3,2,1,0:T(8,128)S(1)}, u32[]{:S(2)}, u32[]{:S(2)}) %collective-permute-start.10) | collective-permute-done | bytes 131104 | tf_op jit(solution)/shard_map/ppermute | solution.py:214
  151.9 0.8 pad_maximum_fusion.1.start_ref
  152.6 15.2 %backward.1 = f32[2,8,4,64,128]{4,3,2,1,0:T(8,128)} custom-call(f32[64,256,128]{2,1,0:T(8,128)} %all-gather.3.cloned.1.call-done.near_ref, f32[64,96,128]{2,1,0:T(8,128)} %all-gather.5.cloned.1.call-done.far_ref, f32[2,2,192,128]{3,2,1,0:T(8,128)} %pad_maximum_fusion.1.start_ref, f32[32,2,64,128]{3,2,1,0:T(8,128)} %get-tuple-element.14.early_ref, ...), custom_call_target="tpu_custom_call" | custom-call | tf_op jit(solution)/shard_map/backward/pallas_call | solution.py:457
  167.9 10.1 %all_to_all.15 = f32[2,8,4,64,128]{4,3,2,1,0:T(8,128)S(1)} all-to-all(f32[2,8,4,64,128]{4,3,2,1,0:T(8,128)} %backward.1), channel_id=1, replica_groups={{0,32},{64,96},{128,160},{192,224},{256,288},{320,352},{384,416},{448,4..., dimensions={0} | all-to-all | bytes 4194304 | tf_op jit(solution)/shard_map/all_to_all | solution.py:474
  178.0 0.2 fusion
  178.1 31.7 %all_to_all.16.parts_ref = f32[8,4,64,128]{3,2,1,0:T(8,128)S(1)} all-to-all(f32[8,4,64,128]{3,2,1,0:T(8,128)S(1)} %fusion), channel_id=1, replica_groups={{0,64,128,192,256,320,384,448},{32,96,160,224,288,352,416,480},{1,65,12..., dimensions={0} | all-to-all | bytes 2097152 | tf_op jit(solution)/shard_map/all_to_all | solution.py:476
  209.9 0.7 share.1
  210.6 15.6 %all_to_all.17.strips_ref = f32[32,16,128]{2,1,0:T(8,128)S(1)} all-to-all(f32[32,16,128]{2,1,0:T(8,128)S(1)} %get-tuple-element.18), channel_id=1, replica_groups=mesh['angle'=16,'tx'=4,'ty'=8] {'tx','ty'}, dimensions={0} | all-to-all | bytes 524288 | tf_op jit(solution)/shard_map/all_to_all | solution.py:372
  226.2 3.6 %collective-permute-start.12 = (f32[288,128]{1,0:T(8,128)S(1)}, f32[288,128]{1,0:T(8,128)S(1)}, u32[]{:S(2)}, u32[]{:S(2)}) collective-permute-start(f32[288,128]{1,0:T(8,128)S(1)} %get-tuple-element.20), channel_id=1, source_target_pairs={{0,32},{32,64},{64,96},{96,128},{128,160},{160,192},{192,224},{224... | collective-permute-start | bytes 442376 | tf_op jit(solution)/shard_map/ppermute | solution.py:381
  229.8 0.2 collective-permute-start.13
  230.0 1.9 collective-permute-done.12.low_ref
  231.9 2.8 %collective-permute-done.13.high_ref = f32[288,128]{1,0:T(8,128)S(1)} collective-permute-done((f32[288,128]{1,0:T(8,128)S(1)}, f32[288,128]{1,0:T(8,128)S(1)}, u32[]{:S(2)}, u32[]{:S(2)}) %collective-permute-start.13) | collective-permute-done | bytes 147488 | tf_op jit(solution)/shard_map/ppermute | solution.py:382
  234.7 4.8 %smooth.1 = f32[4,64,128]{2,1,0:T(8,128)} custom-call(f32[4,64,128]{2,1,0:T(8,128)S(1)} %get-tuple-element.17.vol_ref, f32[8,16,128]{2,1,0:T(8,128)S(1)} %get-tuple-element.19.near_ref, f32[288,128]{1,0:T(8,128)S(1)} %collective-permute-done.12.low_ref, f32[288,128]{1,0:T(8,128)S(1)} %collective-permute-done.13.high_ref), custom_call_target="tpu_custom_call" | custom-call | tf_op jit(solution)/shard_map/smooth/pallas_call | solution.py:384
  (23 shorter events, 0.2 us)
Async XLA Ops:
  7.2 15.9 %copy-start = (f32[4,64,128]{2,1,0:T(8,128)S(1)}, f32[4,64,128]{2,1,0:T(8,128)}, u32[]{:S(2)}) copy-start(f32[4,64,128]{2,1,0:T(8,128)} %index_ref.1) | copy-start | bytes 393220
  7.2 92.2 %all-gather.3.cloned.1.call-start = ((), (), s32[]{:S(2)}) async-start(), calls=%async_computation.3 | async-start | bytes 8912896 | tf_op jit(solution)/shard_map/all_gather | solution.py:237
  8.4 8.7 %collective-permute-start.1 = (f32[2,64,128]{2,1,0:T(8,128)S(1)}, f32[2,64,128]{2,1,0:T(8,128)S(1)}, u32[]{:S(2)}, u32[]{:S(2)}) collective-permute-start(f32[2,64,128]{2,1,0:T(8,128)S(1)} %pad_maximum_fusion.8), channel_id=1, source_target_pairs={{0,8},{8,16},{16,24},{24,0},{1,9},{9,17},{17,25},{25,1},{2,10},{10... | collective-permute-start | bytes 196616 | tf_op jit(solution)/shard_map/ppermute | solution.py:206
  13.5 8.5 %collective-permute-start = (f32[2,64,128]{2,1,0:T(8,128)S(1)}, f32[2,64,128]{2,1,0:T(8,128)S(1)}, u32[]{:S(2)}, u32[]{:S(2)}) collective-permute-start(f32[2,64,128]{2,1,0:T(8,128)S(1)} %pad_maximum_fusion.7), channel_id=1, source_target_pairs={{0,24},{8,0},{16,8},{24,16},{1,25},{9,1},{17,9},{25,17},{2,26},{10... | collective-permute-start | bytes 196616 | tf_op jit(solution)/shard_map/ppermute | solution.py:207
  23.1 21.1 %copy-start.2 = (s32[1,2]{1,0:T(1,128)S(1)}, s32[1,2]{1,0:T(1,128)}, u32[]{:S(2)}) copy-start(s32[1,2]{1,0:T(1,128)} %param.5) | copy-start | bytes 28
  23.1 7.8 %collective-permute-start.2 = (f32[4,2,32,128]{3,2,0,1:T(8,128)S(1)}, f32[4,2,32,128]{3,2,0,1:T(8,128)S(1)}, u32[]{:S(2)}, u32[]{:S(2)}) collective-permute-start(f32[4,2,32,128]{3,2,0,1:T(8,128)S(1)} %fusion.6), channel_id=1, source_target_pairs={{0,1},{1,2},{2,3},{3,4},{4,5},{5,6},{6,7},{7,0},{8,9},{9,10},{10,1... | collective-permute-start | bytes 393224 | tf_op jit(solution)/shard_map/ppermute | solution.py:214
  26.8 5.7 %collective-permute-start.3 = (f32[4,2,32,128]{3,2,1,0:T(8,128)S(1)}, f32[4,2,32,128]{3,2,1,0:T(8,128)S(1)}, u32[]{:S(2)}, u32[]{:S(2)}) collective-permute-start(f32[4,2,32,128]{3,2,1,0:T(8,128)S(1)} %copy.15), channel_id=1, source_target_pairs={{0,7},{1,0},{2,1},{3,2},{4,3},{5,4},{6,5},{7,6},{8,15},{9,8},{10,9... | collective-permute-start | bytes 393224 | tf_op jit(solution)/shard_map/ppermute | solution.py:215
  33.4 119.2 %all-gather.5.cloned.1.call-start = ((), (), s32[]{:S(2)}) async-start(), calls=%async_computation.4 | async-start | bytes 3342336 | tf_op jit(solution)/shard_map/all_gather | solution.py:241
  33.5 8.2 %collective-permute-start.4 = (f32[4,2,32,128]{3,2,1,0:T(8,128)S(1)}, f32[4,2,32,128]{3,2,1,0:T(8,128)S(1)}, u32[]{:S(2)}, u32[]{:S(2)}) collective-permute-start(f32[4,2,32,128]{3,2,1,0:T(8,128)S(1)} %copy.15), channel_id=1, source_target_pairs={{0,1},{1,2},{2,3},{3,4},{4,5},{5,6},{6,7},{7,0},{8,9},{9,10},{10,1... | collective-permute-start | bytes 393224 | tf_op jit(solution)/shard_map/ppermute | solution.py:214
  36.6 6.6 %collective-permute-start.5 = (f32[4,2,32,128]{3,2,0,1:T(8,128)S(1)}, f32[4,2,32,128]{3,2,0,1:T(8,128)S(1)}, u32[]{:S(2)}, u32[]{:S(2)}) collective-permute-start(f32[4,2,32,128]{3,2,0,1:T(8,128)S(1)} %fusion.6), channel_id=1, source_target_pairs={{0,7},{1,0},{2,1},{3,2},{4,3},{5,4},{6,5},{7,6},{8,15},{9,8},{10,9... | collective-permute-start | bytes 393224 | tf_op jit(solution)/shard_map/ppermute | solution.py:215
  47.3 67.6 %copy-start.1 = (f32[2,1,64,128]{3,2,1,0:T(8,128)S(1)}, f32[2,1,64,128]{3,2,1,0:T(8,128)}, u32[]{:S(2)}) copy-start(f32[2,1,64,128]{3,2,1,0:T(8,128)} %param.4) | copy-start | bytes 196612
  107.5 7.4 %collective-permute-start.6 = (f32[2,2,32,128]{3,2,1,0:T(8,128)S(1)}, f32[2,2,32,128]{3,2,1,0:T(8,128)S(1)}, u32[]{:S(2)}, u32[]{:S(2)}) collective-permute-start(f32[2,2,32,128]{3,2,1,0:T(8,128)S(1)} %get-tuple-element.22), channel_id=1, source_target_pairs={{0,1},{1,2},{2,3},{3,4},{4,5},{5,6},{6,7},{7,0},{8,9},{9,10},{10,1... | collective-permute-start | bytes 196616 | tf_op jit(solution)/shard_map/ppermute | solution.py:214
  110.6 5.6 %collective-permute-start.7 = (f32[2,2,32,128]{3,2,1,0:T(8,128)S(1)}, f32[2,2,32,128]{3,2,1,0:T(8,128)S(1)}, u32[]{:S(2)}, u32[]{:S(2)}) collective-permute-start(f32[2,2,32,128]{3,2,1,0:T(8,128)S(1)} %get-tuple-element.23), channel_id=1, source_target_pairs={{0,7},{1,0},{2,1},{3,2},{4,3},{5,4},{6,5},{7,6},{8,15},{9,8},{10,9... | collective-permute-start | bytes 196616 | tf_op jit(solution)/shard_map/ppermute | solution.py:215
  126.2 8.3 %collective-permute-start.9 = (f32[1,64,128]{2,1,0:T(8,128)S(1)}, f32[1,64,128]{2,1,0:T(8,128)S(1)}, u32[]{:S(2)}, u32[]{:S(2)}) collective-permute-start(f32[1,64,128]{2,1,0:T(8,128)S(1)} %pad_maximum_fusion.10), channel_id=1, source_target_pairs={{0,8},{8,16},{16,24},{24,0},{1,9},{9,17},{17,25},{25,1},{2,10},{10... | collective-permute-start | bytes 98312 | tf_op jit(solution)/shard_map/ppermute | solution.py:206
  131.1 7.3 %collective-permute-start.8 = (f32[1,64,128]{2,1,0:T(8,128)S(1)}, f32[1,64,128]{2,1,0:T(8,128)S(1)}, u32[]{:S(2)}, u32[]{:S(2)}) collective-permute-start(f32[1,64,128]{2,1,0:T(8,128)S(1)} %pad_maximum_fusion.9), channel_id=1, source_target_pairs={{0,24},{8,0},{16,8},{24,16},{1,25},{9,1},{17,9},{25,17},{2,26},{10... | collective-permute-start | bytes 98312 | tf_op jit(solution)/shard_map/ppermute | solution.py:207
  138.6 7.4 %collective-permute-start.11 = (f32[2,2,64,128]{3,2,1,0:T(8,128)S(1)}, f32[2,2,64,128]{3,2,1,0:T(8,128)S(1)}, u32[]{:S(2)}, u32[]{:S(2)}) collective-permute-start(f32[2,2,64,128]{3,2,1,0:T(8,128)S(1)} %pad_maximum_fusion.6), channel_id=1, source_target_pairs={{0,7},{1,0},{2,1},{3,2},{4,3},{5,4},{6,5},{7,6},{8,15},{9,8},{10,9... | collective-permute-start | bytes 393224 | tf_op jit(solution)/shard_map/ppermute | solution.py:215
  144.0 7.8 %collective-permute-start.10 = (f32[2,2,64,128]{3,2,1,0:T(8,128)S(1)}, f32[2,2,64,128]{3,2,1,0:T(8,128)S(1)}, u32[]{:S(2)}, u32[]{:S(2)}) collective-permute-start(f32[2,2,64,128]{3,2,1,0:T(8,128)S(1)} %pad_maximum_fusion.6), channel_id=1, source_target_pairs={{0,1},{1,2},{2,3},{3,4},{4,5},{5,6},{6,7},{7,0},{8,9},{9,10},{10,1... | collective-permute-start | bytes 393224 | tf_op jit(solution)/shard_map/ppermute | solution.py:214
  226.2 5.7 %collective-permute-start.12 = (f32[288,128]{1,0:T(8,128)S(1)}, f32[288,128]{1,0:T(8,128)S(1)}, u32[]{:S(2)}, u32[]{:S(2)}) collective-permute-start(f32[288,128]{1,0:T(8,128)S(1)} %get-tuple-element.20), channel_id=1, source_target_pairs={{0,32},{32,64},{64,96},{96,128},{128,160},{160,192},{192,224},{224... | collective-permute-start | bytes 442376 | tf_op jit(solution)/shard_map/ppermute | solution.py:381
  229.8 4.9 %collective-permute-start.13 = (f32[288,128]{1,0:T(8,128)S(1)}, f32[288,128]{1,0:T(8,128)S(1)}, u32[]{:S(2)}, u32[]{:S(2)}) collective-permute-start(f32[288,128]{1,0:T(8,128)S(1)} %get-tuple-element.21), channel_id=1, source_target_pairs={{0,480},{32,0},{64,32},{96,64},{128,96},{160,128},{192,160},{224,1... | collective-permute-start | bytes 442376 | tf_op jit(solution)/shard_map/ppermute | solution.py:382
Sparse Core Ops, SparseCore 0:
  33.5 65.7 all-gather.2
  101.5 42.5 all-gather.4

commit v7 on v5

--- a/solution.py
+++ b/solution.py
@@ -76,6 +76,11 @@
     return jnp.where(lane < 64, own, corner)
 
 
+def both_parities(even, odd):
+    lane = lax.broadcasted_iota(jnp.int32, (8, 128), 1)
+    return jnp.where(lane < 64, even, pltpu.roll(odd, 64, 1))
+
+
 def lane_masks():
     lane = lax.broadcasted_iota(jnp.int32, (8, 128), 1)
     return lane == 0, lane == 127
@@ -104,10 +109,12 @@
                 nim = cosine * wim + sine * wre
                 buf[1 - parity, half, pl.ds(row, 8), :] = nre
                 buf[1 - parity, 2 + half, pl.ds(row, 8), :] = nim
-                if chunks // 3 <= c < 2 * chunks // 3:
-                    own = 8 * (c - chunks // 3)
-                    field_ref[j, 0, half, pl.ds(own, 8), :] = nre
-                    field_ref[j, 1, half, pl.ds(own, 8), :] = nim
+        for c in range(chunks // 3, 2 * chunks // 3):
+            row = pl.ds(8 + 8 * c, 8)
+            own = pl.ds(8 * (c - chunks // 3), 8)
+            for part in range(2):
+                even, odd = (buf[1 - parity, 2 * part + half, row, :] for half in range(2))
+                field_ref[j, part, own, :] = both_parities(even, odd)
 
     for k in range(8):
 
@@ -119,9 +126,10 @@
                 step(2 * pair + 1, 1, k, chunks - k)
 
 
-def backward_kernel(rows, index_ref, start_ref, field_ref, grad_ref, buf):
+def backward_kernel(rows, index_ref, start_ref, field_ref, grad_ref, buf, here):
     chunks = rows // 8
     pid = pl.program_id(0)
+    core = lax.rem(lax.axis_index("angle"), 2)
 
     @pl.when(pid == 0)
     def _():
@@ -130,20 +138,24 @@
     def finish(j, slot, c, are, aim):
         if chunks // 3 <= c < 2 * chunks // 3:
             own = pl.ds(8 * (c - chunks // 3), 8)
-            parts = []
             for half in range(2):
-                fre = field_ref[j, 0, half, own, :]
-                fim = field_ref[j, 1, half, own, :]
-                parts.append(phase_scale * (aim[half] * fre - are[half] * fim))
-            slab = GROUP // 2
-            lane = lax.broadcasted_iota(jnp.int32, (8, 128), 1)
-            both = jnp.where(lane < 64, parts[0], pltpu.roll(parts[1], 64, 1))
-            grad_ref[j // slab, 0, j % slab, own, :] = both
+                here[half, own, :] = are[half]
+                here[2 + half, own, :] = aim[half]
         row = 8 + 8 * c
         for half in range(2):
             cosine, sine = phase_factor(index_rows(index_ref, j, half, c, chunks))
             buf[slot, half, pl.ds(row, 8), :] = cosine * are[half] + sine * aim[half]
             buf[slot, 2 + half, pl.ds(row, 8), :] = cosine * aim[half] - sine * are[half]
+
+    def multiply(j):
+        slab = GROUP // 2
+        spot = lax.rem(j // slab + core, 2)
+        for c in range(chunks // 3):
+            own = pl.ds(8 * c, 8)
+            are = both_parities(here[0, own, :], here[1, own, :])
+            aim = both_parities(here[2, own, :], here[3, own, :])
+            grad = aim * field_ref[j, 0, own, :] - are * field_ref[j, 1, own, :]
+            grad_ref[spot, 0, j % slab, own, :] = phase_scale * grad
 
     def step(j, parity, lo, hi):
         for c in range(lo, hi):
@@ -153,6 +165,7 @@
             are = [sum_re[half] - (im[half] + im[half]) for half in range(2)]
             aim = [sum_im[half] + (re[half] + re[half]) for half in range(2)]
             finish(j, parity, c, are, aim)
+        multiply(j)
 
     for k in range(8):
 
@@ -162,14 +175,15 @@
             if k == 0:
                 skip = 1
                 for c in range(chunks):
-                    here = pl.ds(8 * c, 8)
+                    row = pl.ds(8 * c, 8)
                     finish(
                         GROUP - 1,
                         1,
                         c,
-                        [start_ref[0, half, here, :] for half in range(2)],
-                        [start_ref[1, half, here, :] for half in range(2)],
+                        [start_ref[0, half, row, :] for half in range(2)],
+                        [start_ref[1, half, row, :] for half in range(2)],
                     )
+                multiply(GROUP - 1)
                 step(GROUP - 2, 0, k, chunks - k)
 
             @pl.loop(skip, GROUP // 2)
@@ -308,7 +322,7 @@
         @pl.loop(t, depth - 1 - t)
         def _(z):
             inner = jnp.where(lax.rem(z_first + z, nz) == nz - 1, 0.0, 1.0)
-            for c in range(chunks):
+            for c in range(chunks - 1 if t == TV_STEPS - 1 else chunks):
                 row = base - 8 + 8 * c
                 mid = [v[z, half, pl.ds(row, 8), :] for half in range(2)]
                 ahead = [pltpu.roll(m, cols - 1, 1) for m in mid]
@@ -317,8 +331,9 @@
                     dy = v[z, half, pl.ds(row + 1, 8), :] - mid[half]
                     dx = jnp.where(last, ahead[1 - half], ahead[half]) - mid[half]
                     scale = lax.rsqrt(dz * dz + dy * dy + dx * dx + tv_smooth * tv_smooth)
-                    fz[z, half, pl.ds(row, 8), :] = dz * scale
-                    fy[z, half, pl.ds(row, 8), :] = dy * scale
+                    if half == 0 or t < TV_STEPS - 1:
+                        fz[z, half, pl.ds(row, 8), :] = dz * scale
+                        fy[z, half, pl.ds(row, 8), :] = dy * scale
                     fx[z, half, pl.ds(row, 8), :] = dx * scale
 
         @pl.loop(t + 1, depth - 1 - t)
@@ -381,7 +396,6 @@
     nx = cols * lax.axis_size("tx")
     ny = rows * lax.axis_size("ty")
     tall = 3 * rows
-    core_groups = [[2 * i, 2 * i + 1] for i in range(depth // 2)]
     chip_groups = [list(range(c, depth, 2)) for c in range(2)]
 
     block = (2, tall, cols)
@@ -399,10 +413,10 @@
     column = lax.all_gather(pack_corners(*widen(reorder(index, order), "tx", "ty")), "angle", axis=0, tiled=True)
 
     index_block = (GROUP, 5 * rows, cols)
-    field_block = (GROUP, 2, 2, rows, cols)
+    field_block = (GROUP, 2, rows, cols)
     steps = nz // GROUP
     scratch = [pltpu.VMEM((2, 4, tall + 16, cols), jnp.float32)]
-    params = pltpu.CompilerParams(dimension_semantics=("arbitrary",), vmem_limit_bytes=50 * 2**20)
+    params = pltpu.CompilerParams(dimension_semantics=("arbitrary",), vmem_limit_bytes=40 * 2**20)
     fields = pl.pallas_call(
         functools.partial(forward_kernel, tall),
         grid=(steps,),
@@ -410,8 +424,8 @@
             pl.BlockSpec(index_block, lambda i: (i, 0, 0)),
             pl.BlockSpec((2, 2, tall, cols), lambda i: (0, 0, 0, 0)),
         ],
-        out_specs=pl.BlockSpec(field_block, lambda i: (i, 0, 0, 0, 0)),
-        out_shape=jax.ShapeDtypeStruct((nz, 2, 2, rows, cols), jnp.float32),
+        out_specs=pl.BlockSpec(field_block, lambda i: (i, 0, 0, 0)),
+        out_shape=jax.ShapeDtypeStruct((nz, 2, rows, cols), jnp.float32),
         scratch_shapes=scratch,
         compiler_params=params,
         name="forward",
@@ -422,9 +436,7 @@
     target = reorder(measured[:, 0], order)
     target_re = back.real * target[0] - back.imag * target[1]
     target_im = back.real * target[1] + back.imag * target[0]
-    reached = fields[nz - 1]
-    reached = jnp.concatenate([reached[:, 0, :, : cols // 2], reached[:, 1, :, : cols // 2]], axis=2)
-    residual = reached - jnp.stack([target_re, target_im])
+    residual = fields[nz - 1] - jnp.stack([target_re, target_im])
     adjoint = jnp.concatenate(widen(residual, "tx", "ty"), axis=2)
 
     grads = pl.pallas_call(
@@ -433,17 +445,16 @@
         in_specs=[
             pl.BlockSpec(index_block, lambda i: (steps - 1 - i, 0, 0)),
             pl.BlockSpec((2, 2, tall, cols), lambda i: (0, 0, 0, 0)),
-            pl.BlockSpec(field_block, lambda i: (steps - 1 - i, 0, 0, 0, 0)),
+            pl.BlockSpec(field_block, lambda i: (steps - 1 - i, 0, 0, 0)),
         ],
         out_specs=pl.BlockSpec((2, 1, slab, rows, cols), lambda i: (0, steps - 1 - i, 0, 0, 0)),
         out_shape=jax.ShapeDtypeStruct((2, depth // 2, slab, rows, cols), jnp.float32),
-        scratch_shapes=scratch,
+        scratch_shapes=scratch + [pltpu.VMEM((4, rows, cols), jnp.float32)],
         compiler_params=params,
         name="backward",
     )(column, adjoint, fields)
 
-    pair = lax.all_to_all(grads, "angle", 0, 0, tiled=True, axis_index_groups=core_groups)
-    both = pair[0] + pair[1]
+    both = grads[0] + lax.ppermute(grads[1], "angle", [(i, i ^ 1) for i in range(depth)])
     parts = lax.all_to_all(both, "angle", 0, 0, tiled=True, axis_index_groups=chip_groups)
     return step_and_smooth(parts, index, order.T, nz)
 

time: 249 us -> 238 us (0.956)
  Pallas kernels: 40.5 us -> 31.9 us
  blocking collectives: 54.9 us -> 46.4 us
  starting transfers between devices: 31.5 us -> 36.9 us
    all_to_all x1 -> x0, blocking collectives: 8.54 us -> none  [body(): lax.all_to_all(grads, 'angle', 0, 0, tiled=True, axis_index_groups=core_g...]
    pallas_call x1, Pallas kernels: 20.5 us -> 13.2 us  [body(): pl.pallas_call(functools.partial(backward_kernel, tall), grid=(steps,), i...]
    ppermute x0 -> x1, starting transfers between devices: none -> 5.27 us  [body(): lax.ppermute(grads[1], 'angle', [(i, i ^ 1) for i in range(depth)])]
  transfers between devices with their start and end apart: 11 -> 12, of which waited for: 8 -> 9; matrix products, arithmetic and copies ran while one was open for 2% -> 2% of each run, Pallas kernels for 0% -> 0%
where the time goes in v7:
time: 238 us
  waiting for transfers between devices  100 us (42%)
  blocking collectives  46.4 us (19%)
  starting transfers between devices  36.9 us (16%)
  Pallas kernels  31.9 us (13%)
  between operations  14.5 us (6%)
  other arithmetic  4.82 us (2%)
    all_gather x1, waiting for transfers between devices, body(): lax.all_gather(pack_corners(*widen(reorder(index, order), 'tx', 'ty')), '...  70.6 us
    all_to_all x1, blocking collectives, body(): lax.all_to_all(both, 'angle', 0, 0, tiled=True, axis_index_groups=chip_gr...  31.5 us
    all_to_all x1, blocking collectives, step_and_smooth(): strips = lax.all_to_all(strips, ('tx', 'ty'), 0, 0, tiled=True)  14.8 us
    pallas_call x1, Pallas kernels, body(): pl.pallas_call(functools.partial(backward_kernel, tall), grid=(steps,), i...  13.2 us
    pallas_call x1, Pallas kernels, body(): pl.pallas_call(functools.partial(forward_kernel, tall), grid=(steps,), in...  12.9 us
    ppermute x2, waiting for transfers between devices, widen(): above = lax.ppermute(wide, axis_y, ring(ny, 1))  11.3 us
    ppermute x2, starting transfers between devices, widen(): right = unpack(lax.ppermute(pack(side(0)), axis_x, ring(nx, -1)))  8.92 us
    ppermute x2, starting transfers between devices, widen(): below = lax.ppermute(wide, axis_y, ring(ny, -1))  7.63 us
  transfers between devices with their start and end apart: 12, of which 9 were waited for; matrix products, arithmetic and copies ran while one was open for 2% of the time, Pallas kernels for 0%

profile of v7, /device:TPU:1, one launch (start us, length us, event | category | flops | bytes accessed | tf_op | source)
XLA Modules:
  0.0 237.8 jit_solution(7516329037249839615)
XLA Ops:
  7.2 0.0 copy-start
  7.2 0.0 all-gather.2.cloned.1.call-start
  7.2 1.2 convolution_bitcast_fusion
  8.4 0.2 fusion.37
  8.6 0.1 fusion.17
  8.7 0.1 fusion.23
  8.8 5.0 %collective-permute-start.1 = (f32[2,64,128]{2,1,0:T(8,128)S(1)}, f32[2,64,128]{2,1,0:T(8,128)S(1)}, u32[]{:S(2)}, u32[]{:S(2)}) collective-permute-start(f32[2,64,128]{2,1,0:T(8,128)S(1)} %fusion.23), channel_id=1, source_target_pairs={{0,8},{8,16},{16,24},{24,0},{1,9},{9,17},{17,25},{25,1},{2,10},{10... | collective-permute-start | bytes 196616 | tf_op jit(solution)/shard_map/ppermute | solution.py:217
  13.9 0.1 fusion.18
  14.0 0.1 fusion.24
  14.1 3.6 %collective-permute-start = (f32[2,64,128]{2,1,0:T(8,128)S(1)}, f32[2,64,128]{2,1,0:T(8,128)S(1)}, u32[]{:S(2)}, u32[]{:S(2)}) collective-permute-start(f32[2,64,128]{2,1,0:T(8,128)S(1)} %fusion.24), channel_id=1, source_target_pairs={{0,24},{8,0},{16,8},{24,16},{1,25},{9,1},{17,9},{25,17},{2,26},{10... | collective-permute-start | bytes 196616 | tf_op jit(solution)/shard_map/ppermute | solution.py:218
  17.7 0.1 fusion.36
  17.8 4.8 %collective-permute-done = f32[2,64,128]{2,1,0:T(8,128)S(1)} collective-permute-done((f32[2,64,128]{2,1,0:T(8,128)S(1)}, f32[2,64,128]{2,1,0:T(8,128)S(1)}, u32[]{:S(2)}, u32[]{:S(2)}) %collective-permute-start) | collective-permute-done | bytes 65568 | tf_op jit(solution)/shard_map/ppermute | solution.py:218
  22.5 0.1 fusion.40
  22.7 0.1 fusion.41
  22.8 0.0 copy-start.4
  22.8 0.2 fusion.10
  23.0 0.0 copy-start.3
  23.0 3.3 %collective-permute-start.3 = (f32[4,2,64,128]{3,2,0,1:T(8,128)S(1)}, f32[4,2,64,128]{3,2,0,1:T(8,128)S(1)}, u32[]{:S(2)}, u32[]{:S(2)}) collective-permute-start(f32[4,2,64,128]{3,2,0,1:T(8,128)S(1)} %pad_maximum_fusion.2), channel_id=1, source_target_pairs={{0,7},{1,0},{2,1},{3,2},{4,3},{5,4},{6,5},{7,6},{8,15},{9,8},{10,9... | collective-permute-start | bytes 786440 | tf_op jit(solution)/shard_map/ppermute | solution.py:223
  26.4 2.4 %collective-permute-start.2 = (f32[4,2,64,128]{3,2,0,1:T(8,128)S(1)}, f32[4,2,64,128]{3,2,0,1:T(8,128)S(1)}, u32[]{:S(2)}, u32[]{:S(2)}) collective-permute-start(f32[4,2,64,128]{3,2,0,1:T(8,128)S(1)} %pad_maximum_fusion.2), channel_id=1, source_target_pairs={{0,1},{1,2},{2,3},{3,4},{4,5},{5,6},{6,7},{7,0},{8,9},{9,10},{10,1... | collective-permute-start | bytes 786440 | tf_op jit(solution)/shard_map/ppermute | solution.py:222
  28.8 1.8 collective-permute-done.3
  30.6 0.2 fusion.35
  30.8 5.4 %collective-permute-done.2 = f32[4,2,64,128]{3,2,0,1:T(8,128)S(1)} collective-permute-done((f32[4,2,64,128]{3,2,0,1:T(8,128)S(1)}, f32[4,2,64,128]{3,2,0,1:T(8,128)S(1)}, u32[]{:S(2)}, u32[]{:S(2)}) %collective-permute-start.2) | collective-permute-done | bytes 262176 | tf_op jit(solution)/shard_map/ppermute | solution.py:222
  36.1 0.2 maximum_select_fusion
  36.5 1.0 maximum_maximum_fusion
  37.4 0.0 all-gather.2.cloned.1.call-update
  37.5 0.6 fusion.44
  38.1 0.6 add_multiply_fusion
  38.7 1.5 fusion.14
  40.3 0.2 convolution_bitcast_fusion.1
  40.5 70.6 %all-gather.2.cloned.1.call-done.index_ref = f32[64,320,128]{2,1,0:T(8,128)} async-done(((f32[4,320,128]{2,1,0:T(8,128)}), f32[64,320,128]{2,1,0:T(8,128)}) %all-gather.2.cloned.1.call-update) | async-done | bytes 10485776 | tf_op jit(solution)/shard_map/all_gather | solution.py:413
  111.2 12.9 %forward.1.field_ref = f32[64,2,64,128]{3,2,1,0:T(8,128)S(1)} custom-call(f32[64,320,128]{2,1,0:T(8,128)} %all-gather.2.cloned.1.call-done.index_ref, f32[2,2,192,128]{3,2,1,0:T(8,128)S(1)} %pad_maximum_fusion.start_ref), custom_call_target="tpu_custom_call" | custom-call | tf_op jit(solution)/shard_map/forward/pallas_call | solution.py:420
  124.0 0.1 fusion.38
  124.1 0.1 fusion.39
  124.3 0.1 fusion.29
  124.3 0.1 fusion.31
  124.4 5.3 %collective-permute-start.4 = (f32[1,64,128]{2,1,0:T(8,128)S(1)}, f32[1,64,128]{2,1,0:T(8,128)S(1)}, u32[]{:S(2)}, u32[]{:S(2)}) collective-permute-start(f32[1,64,128]{2,1,0:T(8,128)S(1)} %fusion.31), channel_id=1, source_target_pairs={{0,24},{8,0},{16,8},{24,16},{1,25},{9,1},{17,9},{25,17},{2,26},{10... | collective-permute-start | bytes 98312 | tf_op jit(solution)/shard_map/ppermute | solution.py:218
  129.8 0.1 fusion.28
  129.9 0.1 fusion.30
  129.9 1.9 collective-permute-start.5
  131.9 0.0 collective-permute-done.4
  131.9 0.1 fusion.42
  132.0 4.8 %collective-permute-done.5 = f32[1,64,128]{2,1,0:T(8,128)S(1)} collective-permute-done((f32[1,64,128]{2,1,0:T(8,128)S(1)}, f32[1,64,128]{2,1,0:T(8,128)S(1)}, u32[]{:S(2)}, u32[]{:S(2)}) %collective-permute-start.5) | collective-permute-done | bytes 32800 | tf_op jit(solution)/shard_map/ppermute | solution.py:217
  136.8 0.1 fusion.43
  136.8 0.1 fusion.20
  136.9 0.1 maximum_bitcast_fusion.1
  137.1 4.3 %collective-permute-start.7 = (f32[2,2,64,128]{3,2,1,0:T(8,128)S(1)}, f32[2,2,64,128]{3,2,1,0:T(8,128)S(1)}, u32[]{:S(2)}, u32[]{:S(2)}) collective-permute-start(f32[2,2,64,128]{3,2,1,0:T(8,128)S(1)} %pad_maximum_fusion.3), channel_id=1, source_target_pairs={{0,7},{1,0},{2,1},{3,2},{4,3},{5,4},{6,5},{7,6},{8,15},{9,8},{10,9... | collective-permute-start | bytes 393224 | tf_op jit(solution)/shard_map/ppermute | solution.py:223
  141.4 1.9 collective-permute-start.6
  143.3 0.0 collective-permute-done.7
  143.3 5.9 %collective-permute-done.6 = f32[2,2,64,128]{3,2,1,0:T(8,128)S(1)} collective-permute-done((f32[2,2,64,128]{3,2,1,0:T(8,128)S(1)}, f32[2,2,64,128]{3,2,1,0:T(8,128)S(1)}, u32[]{:S(2)}, u32[]{:S(2)}) %collective-permute-start.6) | collective-permute-done | bytes 131104 | tf_op jit(solution)/shard_map/ppermute | solution.py:222
  149.2 13.2 %backward.1 = f32[2,8,4,64,128]{4,3,2,1,0:T(8,128)S(1)} custom-call(f32[64,320,128]{2,1,0:T(8,128)} %all-gather.2.cloned.1.call-done.index_ref, f32[2,2,192,128]{3,2,1,0:T(8,128)S(1)} %pad_maximum_fusion.1.start_ref, f32[64,2,64,128]{3,2,1,0:T(8,128)S(1)} %forward.1.field_ref), custom_call_target="tpu_custom_call" | custom-call | tf_op jit(solution)/shard_map/backward/pallas_call | solution.py:442
  162.4 0.0 copy-start.1
  162.4 0.0 copy-start.2
  162.4 0.1 slice_bitcast_fusion
  162.6 5.3 %collective-permute-start.8 = (f32[8,4,64,128]{3,2,1,0:T(8,128)S(1)}, f32[8,4,64,128]{3,2,1,0:T(8,128)S(1)}, u32[]{:S(2)}, u32[]{:S(2)}) collective-permute-start(f32[8,4,64,128]{3,2,1,0:T(8,128)S(1)} %slice_bitcast_fusion), channel_id=1, source_target_pairs={{0,32},{32,0},{64,96},{96,64},{128,160},{160,128},{192,224},{224,1... | collective-permute-start | bytes 3145736 | tf_op jit(solution)/shard_map/ppermute | solution.py:457
  167.8 2.3 collective-permute-done.8
  170.1 0.2 fusion
  170.3 31.5 %all_to_all.10.parts_ref = f32[8,4,64,128]{3,2,1,0:T(8,128)S(1)} all-to-all(f32[8,4,64,128]{3,2,1,0:T(8,128)S(1)} %fusion), channel_id=1, replica_groups={{0,64,128,192,256,320,384,448},{32,96,160,224,288,352,416,480},{1,65,12..., dimensions={0} | all-to-all | bytes 2097152 | tf_op jit(solution)/shard_map/all_to_all | solution.py:458
  201.8 1.0 share.1
  202.8 14.8 %all_to_all.11.strips_ref = f32[32,16,128]{2,1,0:T(8,128)S(1)} all-to-all(f32[32,16,128]{2,1,0:T(8,128)S(1)} %get-tuple-element.10), channel_id=1, replica_groups=mesh['angle'=16,'tx'=4,'ty'=8] {'tx','ty'}, dimensions={0} | all-to-all | bytes 524288 | tf_op jit(solution)/shard_map/all_to_all | solution.py:370
  217.7 3.6 %collective-permute-start.9 = (f32[288,128]{1,0:T(8,128)S(1)}, f32[288,128]{1,0:T(8,128)S(1)}, u32[]{:S(2)}, u32[]{:S(2)}) collective-permute-start(f32[288,128]{1,0:T(8,128)S(1)} %get-tuple-element.12), channel_id=1, source_target_pairs={{0,32},{32,64},{64,96},{96,128},{128,160},{160,192},{192,224},{224... | collective-permute-start | bytes 442376 | tf_op jit(solution)/shard_map/ppermute | solution.py:379
  221.3 0.2 collective-permute-start.10
  221.5 1.9 collective-permute-done.9.low_ref
  223.4 2.8 %collective-permute-done.10.high_ref = f32[288,128]{1,0:T(8,128)S(1)} collective-permute-done((f32[288,128]{1,0:T(8,128)S(1)}, f32[288,128]{1,0:T(8,128)S(1)}, u32[]{:S(2)}, u32[]{:S(2)}) %collective-permute-start.10) | collective-permute-done | bytes 147488 | tf_op jit(solution)/shard_map/ppermute | solution.py:380
  226.2 4.8 %smooth.1 = f32[4,64,128]{2,1,0:T(8,128)} custom-call(f32[4,64,128]{2,1,0:T(8,128)S(1)} %get-tuple-element.9.vol_ref, f32[8,16,128]{2,1,0:T(8,128)S(1)} %get-tuple-element.11.near_ref, f32[288,128]{1,0:T(8,128)S(1)} %collective-permute-done.9.low_ref, f32[288,128]{1,0:T(8,128)S(1)} %collective-permute-done.10.high_ref), custom_call_target="tpu_custom_call" | custom-call | tf_op jit(solution)/shard_map/smooth/pallas_call | solution.py:382
  (24 shorter events, 0.3 us)
Async XLA Ops:
  7.2 33.1 %copy-start = (f32[2,1,64,128]{3,2,1,0:T(8,128)S(1)}, f32[2,1,64,128]{3,2,1,0:T(8,128)}, u32[]{:S(2)}) copy-start(f32[2,1,64,128]{3,2,1,0:T(8,128)} %param.5) | copy-start | bytes 196612
  7.2 104.0 %all-gather.2.cloned.1.call-start = ((), (), s32[]{:S(2)}) async-start(), calls=%async_computation.2 | async-start | bytes 11141120 | tf_op jit(solution)/shard_map/all_gather | solution.py:413
  8.8 13.8 %collective-permute-start.1 = (f32[2,64,128]{2,1,0:T(8,128)S(1)}, f32[2,64,128]{2,1,0:T(8,128)S(1)}, u32[]{:S(2)}, u32[]{:S(2)}) collective-permute-start(f32[2,64,128]{2,1,0:T(8,128)S(1)} %fusion.23), channel_id=1, source_target_pairs={{0,8},{8,16},{16,24},{24,0},{1,9},{9,17},{17,25},{25,1},{2,10},{10... | collective-permute-start | bytes 196616 | tf_op jit(solution)/shard_map/ppermute | solution.py:217
  14.1 8.5 %collective-permute-start = (f32[2,64,128]{2,1,0:T(8,128)S(1)}, f32[2,64,128]{2,1,0:T(8,128)S(1)}, u32[]{:S(2)}, u32[]{:S(2)}) collective-permute-start(f32[2,64,128]{2,1,0:T(8,128)S(1)} %fusion.24), channel_id=1, source_target_pairs={{0,24},{8,0},{16,8},{24,16},{1,25},{9,1},{17,9},{25,17},{2,26},{10... | collective-permute-start | bytes 196616 | tf_op jit(solution)/shard_map/ppermute | solution.py:218
  22.8 14.7 %copy-start.4 = (s32[1,2]{1,0:T(1,128)S(1)}, s32[1,2]{1,0:T(1,128)}, u32[]{:S(2)}) copy-start(s32[1,2]{1,0:T(1,128)} %param.6) | copy-start | bytes 28
  23.0 17.3 %copy-start.3 = (f32[128,128,1]{1,0,2:T(8,128)S(1)}, f32[128,128,1]{1,0,2:T(8,128)}, u32[]{:S(2)}) copy-start(f32[128,128,1]{1,0,2:T(8,128)} %constant.49) | copy-start | bytes 196612
  23.0 7.5 %collective-permute-start.3 = (f32[4,2,64,128]{3,2,0,1:T(8,128)S(1)}, f32[4,2,64,128]{3,2,0,1:T(8,128)S(1)}, u32[]{:S(2)}, u32[]{:S(2)}) collective-permute-start(f32[4,2,64,128]{3,2,0,1:T(8,128)S(1)} %pad_maximum_fusion.2), channel_id=1, source_target_pairs={{0,7},{1,0},{2,1},{3,2},{4,3},{5,4},{6,5},{7,6},{8,15},{9,8},{10,9... | collective-permute-start | bytes 786440 | tf_op jit(solution)/shard_map/ppermute | solution.py:223
  26.4 9.8 %collective-permute-start.2 = (f32[4,2,64,128]{3,2,0,1:T(8,128)S(1)}, f32[4,2,64,128]{3,2,0,1:T(8,128)S(1)}, u32[]{:S(2)}, u32[]{:S(2)}) collective-permute-start(f32[4,2,64,128]{3,2,0,1:T(8,128)S(1)} %pad_maximum_fusion.2), channel_id=1, source_target_pairs={{0,1},{1,2},{2,3},{3,4},{4,5},{5,6},{6,7},{7,0},{8,9},{9,10},{10,1... | collective-permute-start | bytes 786440 | tf_op jit(solution)/shard_map/ppermute | solution.py:222
  124.4 7.4 %collective-permute-start.4 = (f32[1,64,128]{2,1,0:T(8,128)S(1)}, f32[1,64,128]{2,1,0:T(8,128)S(1)}, u32[]{:S(2)}, u32[]{:S(2)}) collective-permute-start(f32[1,64,128]{2,1,0:T(8,128)S(1)} %fusion.31), channel_id=1, source_target_pairs={{0,24},{8,0},{16,8},{24,16},{1,25},{9,1},{17,9},{25,17},{2,26},{10... | collective-permute-start | bytes 98312 | tf_op jit(solution)/shard_map/ppermute | solution.py:218
  129.9 6.8 %collective-permute-start.5 = (f32[1,64,128]{2,1,0:T(8,128)S(1)}, f32[1,64,128]{2,1,0:T(8,128)S(1)}, u32[]{:S(2)}, u32[]{:S(2)}) collective-permute-start(f32[1,64,128]{2,1,0:T(8,128)S(1)} %fusion.30), channel_id=1, source_target_pairs={{0,8},{8,16},{16,24},{24,0},{1,9},{9,17},{17,25},{25,1},{2,10},{10... | collective-permute-start | bytes 98312 | tf_op jit(solution)/shard_map/ppermute | solution.py:217
  137.1 6.2 %collective-permute-start.7 = (f32[2,2,64,128]{3,2,1,0:T(8,128)S(1)}, f32[2,2,64,128]{3,2,1,0:T(8,128)S(1)}, u32[]{:S(2)}, u32[]{:S(2)}) collective-permute-start(f32[2,2,64,128]{3,2,1,0:T(8,128)S(1)} %pad_maximum_fusion.3), channel_id=1, source_target_pairs={{0,7},{1,0},{2,1},{3,2},{4,3},{5,4},{6,5},{7,6},{8,15},{9,8},{10,9... | collective-permute-start | bytes 393224 | tf_op jit(solution)/shard_map/ppermute | solution.py:223
  141.4 7.8 %collective-permute-start.6 = (f32[2,2,64,128]{3,2,1,0:T(8,128)S(1)}, f32[2,2,64,128]{3,2,1,0:T(8,128)S(1)}, u32[]{:S(2)}, u32[]{:S(2)}) collective-permute-start(f32[2,2,64,128]{3,2,1,0:T(8,128)S(1)} %pad_maximum_fusion.3), channel_id=1, source_target_pairs={{0,1},{1,2},{2,3},{3,4},{4,5},{5,6},{6,7},{7,0},{8,9},{9,10},{10,1... | collective-permute-start | bytes 393224 | tf_op jit(solution)/shard_map/ppermute | solution.py:222
  162.4 39.4 %copy-start.1 = (f32[4,64,128]{2,1,0:T(8,128)S(1)}, f32[4,64,128]{2,1,0:T(8,128)}, u32[]{:S(2)}) copy-start(f32[4,64,128]{2,1,0:T(8,128)} %index_ref.1) | copy-start | bytes 393220
  162.4 39.4 %copy-start.2 = (f32[128,128]{1,0:T(8,128)S(1)}, f32[128,128]{1,0:T(8,128)}, u32[]{:S(2)}) copy-start(f32[128,128]{1,0:T(8,128)} %constant.48.order_ref) | copy-start | bytes 196612
  162.6 7.5 %collective-permute-start.8 = (f32[8,4,64,128]{3,2,1,0:T(8,128)S(1)}, f32[8,4,64,128]{3,2,1,0:T(8,128)S(1)}, u32[]{:S(2)}, u32[]{:S(2)}) collective-permute-start(f32[8,4,64,128]{3,2,1,0:T(8,128)S(1)} %slice_bitcast_fusion), channel_id=1, source_target_pairs={{0,32},{32,0},{64,96},{96,64},{128,160},{160,128},{192,224},{224,1... | collective-permute-start | bytes 3145736 | tf_op jit(solution)/shard_map/ppermute | solution.py:457
  217.7 5.7 %collective-permute-start.9 = (f32[288,128]{1,0:T(8,128)S(1)}, f32[288,128]{1,0:T(8,128)S(1)}, u32[]{:S(2)}, u32[]{:S(2)}) collective-permute-start(f32[288,128]{1,0:T(8,128)S(1)} %get-tuple-element.12), channel_id=1, source_target_pairs={{0,32},{32,64},{64,96},{96,128},{128,160},{160,192},{192,224},{224... | collective-permute-start | bytes 442376 | tf_op jit(solution)/shard_map/ppermute | solution.py:379
  221.3 4.9 %collective-permute-start.10 = (f32[288,128]{1,0:T(8,128)S(1)}, f32[288,128]{1,0:T(8,128)S(1)}, u32[]{:S(2)}, u32[]{:S(2)}) collective-permute-start(f32[288,128]{1,0:T(8,128)S(1)} %get-tuple-element.13), channel_id=1, source_target_pairs={{0,480},{32,0},{64,32},{96,64},{128,96},{160,128},{192,160},{224,1... | collective-permute-start | bytes 442376 | tf_op jit(solution)/shard_map/ppermute | solution.py:380
Sparse Core Ops, SparseCore 0:
  37.6 73.5 all-gather.1

commit v8 on v7

--- a/solution.py
+++ b/solution.py
@@ -309,8 +309,8 @@
         for row, k in ((0, 2), (cols - TV_STEPS, 5)):
             above, beside, below = near[k : k + 3]
             ends = jnp.where(lane3 < 3 * cols // 4, pltpu.roll(below, rows, 1), pltpu.roll(above, rows, 1))
-            turn[pl.ds(row, TV_STEPS), :] = jnp.where(lane3 < rows, beside, ends)
-        sides = turn[...].T
+            turn[z, pl.ds(row, TV_STEPS), :] = jnp.where(lane3 < rows, beside, ends)
+        sides = turn[z].T
         v[z, 1, pl.ds(base, rows), :] = sides[:rows]
         v[z, 1, pl.ds(base + rows, TV_STEPS), :] = sides[rows : rows + TV_STEPS]
         v[z, 1, pl.ds(base - TV_STEPS, TV_STEPS), :] = sides[cols - TV_STEPS :]
@@ -318,9 +318,7 @@
     z_first = lax.axis_index("angle") * slab - TV_STEPS + nz
     chunks = rows // 8 + 2
     for t in range(TV_STEPS):
-
-        @pl.loop(t, depth - 1 - t)
-        def _(z):
+        for z in range(t, depth - 1 - t):
             inner = jnp.where(lax.rem(z_first + z, nz) == nz - 1, 0.0, 1.0)
             for c in range(chunks - 1 if t == TV_STEPS - 1 else chunks):
                 row = base - 8 + 8 * c
@@ -336,8 +334,7 @@
                         fy[z, half, pl.ds(row, 8), :] = dy * scale
                     fx[z, half, pl.ds(row, 8), :] = dx * scale
 
-        @pl.loop(t + 1, depth - 1 - t)
-        def _(z):
+        for z in range(t + 1, depth - 1 - t):
             final = t == TV_STEPS - 1
             for c in range(1, chunks - 1) if final else range(chunks):
                 row = base - 8 + 8 * c
@@ -382,7 +379,7 @@
     smoothed = pl.pallas_call(
         functools.partial(smooth_kernel, nz),
         out_shape=block,
-        scratch_shapes=[whole, whole, whole, whole, pltpu.VMEM((cols, cols), jnp.float32)],
+        scratch_shapes=[whole, whole, whole, whole, pltpu.VMEM((slab + 2 * TV_STEPS, cols, cols), jnp.float32)],
         compiler_params=params,
         name="smooth",
     )(volume, near, low, high)

time: 238 us -> 236 us (level)
  Pallas kernels: 31.9 us -> 29.3 us
    pallas_call x1, Pallas kernels: 4.8 us -> 2.24 us  [step_and_smooth(): pl.pallas_call(functools.partial(smooth_kernel, nz), out_shape=block, scr...]
where the time goes in v8:
time: 236 us; the launch traced here: 235 us
  waiting for transfers between devices  100 us (42%)
  blocking collectives  46.4 us (20%)
  starting transfers between devices  36.9 us (16%)
  Pallas kernels  29.3 us (12%)
  between operations  14.5 us (6%)
  other arithmetic  4.82 us (2%)
    all_gather x1, waiting for transfers between devices, body(): lax.all_gather(pack_corners(*widen(reorder(index, order), 'tx', 'ty')), '...  70.6 us
    all_to_all x1, blocking collectives, body(): lax.all_to_all(both, 'angle', 0, 0, tiled=True, axis_index_groups=chip_gr...  31.5 us
    all_to_all x1, blocking collectives, step_and_smooth(): strips = lax.all_to_all(strips, ('tx', 'ty'), 0, 0, tiled=True)  14.8 us
    pallas_call x1, Pallas kernels, body(): pl.pallas_call(functools.partial(backward_kernel, tall), grid=(steps,), i...  13.2 us
    pallas_call x1, Pallas kernels, body(): pl.pallas_call(functools.partial(forward_kernel, tall), grid=(steps,), in...  12.9 us
    ppermute x2, waiting for transfers between devices, widen(): above = lax.ppermute(wide, axis_y, ring(ny, 1))  11.3 us
    ppermute x2, starting transfers between devices, widen(): right = unpack(lax.ppermute(pack(side(0)), axis_x, ring(nx, -1)))  8.92 us
    ppermute x2, starting transfers between devices, widen(): below = lax.ppermute(wide, axis_y, ring(ny, -1))  7.63 us
  transfers between devices with their start and end apart: 12, of which 9 were waited for; matrix products, arithmetic and copies ran while one was open for 2% of the time, Pallas kernels for 0%

profile of v8, /device:TPU:1, one launch (start us, length us, event | category | flops | bytes accessed | tf_op | source)
XLA Modules:
  0.0 235.3 jit_solution(6288975155755604544)
XLA Ops:
  7.2 0.0 copy-start
  7.2 0.0 all-gather.2.cloned.1.call-start
  7.2 1.2 convolution_bitcast_fusion
  8.4 0.2 fusion.37
  8.6 0.1 fusion.17
  8.7 0.1 fusion.23
  8.8 5.0 %collective-permute-start.1 = (f32[2,64,128]{2,1,0:T(8,128)S(1)}, f32[2,64,128]{2,1,0:T(8,128)S(1)}, u32[]{:S(2)}, u32[]{:S(2)}) collective-permute-start(f32[2,64,128]{2,1,0:T(8,128)S(1)} %fusion.23), channel_id=1, source_target_pairs={{0,8},{8,16},{16,24},{24,0},{1,9},{9,17},{17,25},{25,1},{2,10},{10... | collective-permute-start | bytes 196616 | tf_op jit(solution)/shard_map/ppermute | solution.py:217
  13.9 0.1 fusion.18
  14.0 0.1 fusion.24
  14.1 3.6 %collective-permute-start = (f32[2,64,128]{2,1,0:T(8,128)S(1)}, f32[2,64,128]{2,1,0:T(8,128)S(1)}, u32[]{:S(2)}, u32[]{:S(2)}) collective-permute-start(f32[2,64,128]{2,1,0:T(8,128)S(1)} %fusion.24), channel_id=1, source_target_pairs={{0,24},{8,0},{16,8},{24,16},{1,25},{9,1},{17,9},{25,17},{2,26},{10... | collective-permute-start | bytes 196616 | tf_op jit(solution)/shard_map/ppermute | solution.py:218
  17.7 0.1 fusion.36
  17.8 4.8 %collective-permute-done = f32[2,64,128]{2,1,0:T(8,128)S(1)} collective-permute-done((f32[2,64,128]{2,1,0:T(8,128)S(1)}, f32[2,64,128]{2,1,0:T(8,128)S(1)}, u32[]{:S(2)}, u32[]{:S(2)}) %collective-permute-start) | collective-permute-done | bytes 65568 | tf_op jit(solution)/shard_map/ppermute | solution.py:218
  22.5 0.1 fusion.40
  22.7 0.1 fusion.41
  22.8 0.0 copy-start.4
  22.8 0.2 fusion.10
  23.0 0.0 copy-start.3
  23.0 3.3 %collective-permute-start.3 = (f32[4,2,64,128]{3,2,0,1:T(8,128)S(1)}, f32[4,2,64,128]{3,2,0,1:T(8,128)S(1)}, u32[]{:S(2)}, u32[]{:S(2)}) collective-permute-start(f32[4,2,64,128]{3,2,0,1:T(8,128)S(1)} %pad_maximum_fusion.2), channel_id=1, source_target_pairs={{0,7},{1,0},{2,1},{3,2},{4,3},{5,4},{6,5},{7,6},{8,15},{9,8},{10,9... | collective-permute-start | bytes 786440 | tf_op jit(solution)/shard_map/ppermute | solution.py:223
  26.4 2.4 %collective-permute-start.2 = (f32[4,2,64,128]{3,2,0,1:T(8,128)S(1)}, f32[4,2,64,128]{3,2,0,1:T(8,128)S(1)}, u32[]{:S(2)}, u32[]{:S(2)}) collective-permute-start(f32[4,2,64,128]{3,2,0,1:T(8,128)S(1)} %pad_maximum_fusion.2), channel_id=1, source_target_pairs={{0,1},{1,2},{2,3},{3,4},{4,5},{5,6},{6,7},{7,0},{8,9},{9,10},{10,1... | collective-permute-start | bytes 786440 | tf_op jit(solution)/shard_map/ppermute | solution.py:222
  28.8 1.8 collective-permute-done.3
  30.6 0.2 fusion.35
  30.8 5.4 %collective-permute-done.2 = f32[4,2,64,128]{3,2,0,1:T(8,128)S(1)} collective-permute-done((f32[4,2,64,128]{3,2,0,1:T(8,128)S(1)}, f32[4,2,64,128]{3,2,0,1:T(8,128)S(1)}, u32[]{:S(2)}, u32[]{:S(2)}) %collective-permute-start.2) | collective-permute-done | bytes 262176 | tf_op jit(solution)/shard_map/ppermute | solution.py:222
  36.1 0.2 maximum_select_fusion
  36.5 1.0 maximum_maximum_fusion
  37.4 0.0 all-gather.2.cloned.1.call-update
  37.5 0.6 fusion.44
  38.1 0.6 add_multiply_fusion
  38.7 1.5 fusion.14
  40.3 0.2 convolution_bitcast_fusion.1
  40.5 70.6 %all-gather.2.cloned.1.call-done.index_ref = f32[64,320,128]{2,1,0:T(8,128)} async-done(((f32[4,320,128]{2,1,0:T(8,128)}), f32[64,320,128]{2,1,0:T(8,128)}) %all-gather.2.cloned.1.call-update) | async-done | bytes 10485776 | tf_op jit(solution)/shard_map/all_gather | solution.py:410
  111.2 12.9 %forward.1.field_ref = f32[64,2,64,128]{3,2,1,0:T(8,128)S(1)} custom-call(f32[64,320,128]{2,1,0:T(8,128)} %all-gather.2.cloned.1.call-done.index_ref, f32[2,2,192,128]{3,2,1,0:T(8,128)S(1)} %pad_maximum_fusion.start_ref), custom_call_target="tpu_custom_call" | custom-call | tf_op jit(solution)/shard_map/forward/pallas_call | solution.py:417
  124.0 0.1 fusion.38
  124.1 0.1 fusion.39
  124.3 0.1 fusion.29
  124.3 0.1 fusion.31
  124.4 5.3 %collective-permute-start.4 = (f32[1,64,128]{2,1,0:T(8,128)S(1)}, f32[1,64,128]{2,1,0:T(8,128)S(1)}, u32[]{:S(2)}, u32[]{:S(2)}) collective-permute-start(f32[1,64,128]{2,1,0:T(8,128)S(1)} %fusion.31), channel_id=1, source_target_pairs={{0,24},{8,0},{16,8},{24,16},{1,25},{9,1},{17,9},{25,17},{2,26},{10... | collective-permute-start | bytes 98312 | tf_op jit(solution)/shard_map/ppermute | solution.py:218
  129.8 0.1 fusion.28
  129.9 0.1 fusion.30
  129.9 1.9 collective-permute-start.5
  131.9 0.0 collective-permute-done.4
  131.9 0.1 fusion.42
  132.0 4.8 %collective-permute-done.5 = f32[1,64,128]{2,1,0:T(8,128)S(1)} collective-permute-done((f32[1,64,128]{2,1,0:T(8,128)S(1)}, f32[1,64,128]{2,1,0:T(8,128)S(1)}, u32[]{:S(2)}, u32[]{:S(2)}) %collective-permute-start.5) | collective-permute-done | bytes 32800 | tf_op jit(solution)/shard_map/ppermute | solution.py:217
  136.8 0.1 fusion.43
  136.8 0.1 fusion.20
  136.9 0.1 maximum_bitcast_fusion.1
  137.1 4.3 %collective-permute-start.7 = (f32[2,2,64,128]{3,2,1,0:T(8,128)S(1)}, f32[2,2,64,128]{3,2,1,0:T(8,128)S(1)}, u32[]{:S(2)}, u32[]{:S(2)}) collective-permute-start(f32[2,2,64,128]{3,2,1,0:T(8,128)S(1)} %pad_maximum_fusion.3), channel_id=1, source_target_pairs={{0,7},{1,0},{2,1},{3,2},{4,3},{5,4},{6,5},{7,6},{8,15},{9,8},{10,9... | collective-permute-start | bytes 393224 | tf_op jit(solution)/shard_map/ppermute | solution.py:223
  141.4 1.9 collective-permute-start.6
  143.3 0.0 collective-permute-done.7
  143.3 5.9 %collective-permute-done.6 = f32[2,2,64,128]{3,2,1,0:T(8,128)S(1)} collective-permute-done((f32[2,2,64,128]{3,2,1,0:T(8,128)S(1)}, f32[2,2,64,128]{3,2,1,0:T(8,128)S(1)}, u32[]{:S(2)}, u32[]{:S(2)}) %collective-permute-start.6) | collective-permute-done | bytes 131104 | tf_op jit(solution)/shard_map/ppermute | solution.py:222
  149.2 13.2 %backward.1 = f32[2,8,4,64,128]{4,3,2,1,0:T(8,128)S(1)} custom-call(f32[64,320,128]{2,1,0:T(8,128)} %all-gather.2.cloned.1.call-done.index_ref, f32[2,2,192,128]{3,2,1,0:T(8,128)S(1)} %pad_maximum_fusion.1.start_ref, f32[64,2,64,128]{3,2,1,0:T(8,128)S(1)} %forward.1.field_ref), custom_call_target="tpu_custom_call" | custom-call | tf_op jit(solution)/shard_map/backward/pallas_call | solution.py:439
  162.4 0.0 copy-start.1
  162.4 0.0 copy-start.2
  162.4 0.1 slice_bitcast_fusion
  162.6 5.3 %collective-permute-start.8 = (f32[8,4,64,128]{3,2,1,0:T(8,128)S(1)}, f32[8,4,64,128]{3,2,1,0:T(8,128)S(1)}, u32[]{:S(2)}, u32[]{:S(2)}) collective-permute-start(f32[8,4,64,128]{3,2,1,0:T(8,128)S(1)} %slice_bitcast_fusion), channel_id=1, source_target_pairs={{0,32},{32,0},{64,96},{96,64},{128,160},{160,128},{192,224},{224,1... | collective-permute-start | bytes 3145736 | tf_op jit(solution)/shard_map/ppermute | solution.py:454
  167.8 2.3 collective-permute-done.8
  170.1 0.2 fusion
  170.3 31.5 %all_to_all.10.parts_ref = f32[8,4,64,128]{3,2,1,0:T(8,128)S(1)} all-to-all(f32[8,4,64,128]{3,2,1,0:T(8,128)S(1)} %fusion), channel_id=1, replica_groups={{0,64,128,192,256,320,384,448},{32,96,160,224,288,352,416,480},{1,65,12..., dimensions={0} | all-to-all | bytes 2097152 | tf_op jit(solution)/shard_map/all_to_all | solution.py:455
  201.8 1.0 share.1
  202.8 14.8 %all_to_all.11.strips_ref = f32[32,16,128]{2,1,0:T(8,128)S(1)} all-to-all(f32[32,16,128]{2,1,0:T(8,128)S(1)} %get-tuple-element.10), channel_id=1, replica_groups=mesh['angle'=16,'tx'=4,'ty'=8] {'tx','ty'}, dimensions={0} | all-to-all | bytes 524288 | tf_op jit(solution)/shard_map/all_to_all | solution.py:367
  217.7 3.6 %collective-permute-start.9 = (f32[288,128]{1,0:T(8,128)S(1)}, f32[288,128]{1,0:T(8,128)S(1)}, u32[]{:S(2)}, u32[]{:S(2)}) collective-permute-start(f32[288,128]{1,0:T(8,128)S(1)} %get-tuple-element.12), channel_id=1, source_target_pairs={{0,32},{32,64},{64,96},{96,128},{128,160},{160,192},{192,224},{224... | collective-permute-start | bytes 442376 | tf_op jit(solution)/shard_map/ppermute | solution.py:376
  221.3 0.2 collective-permute-start.10
  221.5 1.9 collective-permute-done.9.low_ref
  223.4 2.8 %collective-permute-done.10.high_ref = f32[288,128]{1,0:T(8,128)S(1)} collective-permute-done((f32[288,128]{1,0:T(8,128)S(1)}, f32[288,128]{1,0:T(8,128)S(1)}, u32[]{:S(2)}, u32[]{:S(2)}) %collective-permute-start.10) | collective-permute-done | bytes 147488 | tf_op jit(solution)/shard_map/ppermute | solution.py:377
  226.2 2.2 smooth.1
  (24 shorter events, 0.3 us)
Async XLA Ops:
  7.2 33.1 %copy-start = (f32[2,1,64,128]{3,2,1,0:T(8,128)S(1)}, f32[2,1,64,128]{3,2,1,0:T(8,128)}, u32[]{:S(2)}) copy-start(f32[2,1,64,128]{3,2,1,0:T(8,128)} %param.5) | copy-start | bytes 196612
  7.2 104.0 %all-gather.2.cloned.1.call-start = ((), (), s32[]{:S(2)}) async-start(), calls=%async_computation.2 | async-start | bytes 11141120 | tf_op jit(solution)/shard_map/all_gather | solution.py:410
  8.8 13.8 %collective-permute-start.1 = (f32[2,64,128]{2,1,0:T(8,128)S(1)}, f32[2,64,128]{2,1,0:T(8,128)S(1)}, u32[]{:S(2)}, u32[]{:S(2)}) collective-permute-start(f32[2,64,128]{2,1,0:T(8,128)S(1)} %fusion.23), channel_id=1, source_target_pairs={{0,8},{8,16},{16,24},{24,0},{1,9},{9,17},{17,25},{25,1},{2,10},{10... | collective-permute-start | bytes 196616 | tf_op jit(solution)/shard_map/ppermute | solution.py:217
  14.1 8.5 %collective-permute-start = (f32[2,64,128]{2,1,0:T(8,128)S(1)}, f32[2,64,128]{2,1,0:T(8,128)S(1)}, u32[]{:S(2)}, u32[]{:S(2)}) collective-permute-start(f32[2,64,128]{2,1,0:T(8,128)S(1)} %fusion.24), channel_id=1, source_target_pairs={{0,24},{8,0},{16,8},{24,16},{1,25},{9,1},{17,9},{25,17},{2,26},{10... | collective-permute-start | bytes 196616 | tf_op jit(solution)/shard_map/ppermute | solution.py:218
  22.8 14.7 %copy-start.4 = (s32[1,2]{1,0:T(1,128)S(1)}, s32[1,2]{1,0:T(1,128)}, u32[]{:S(2)}) copy-start(s32[1,2]{1,0:T(1,128)} %param.6) | copy-start | bytes 28
  23.0 17.3 %copy-start.3 = (f32[128,128,1]{1,0,2:T(8,128)S(1)}, f32[128,128,1]{1,0,2:T(8,128)}, u32[]{:S(2)}) copy-start(f32[128,128,1]{1,0,2:T(8,128)} %constant.49) | copy-start | bytes 196612
  23.0 7.5 %collective-permute-start.3 = (f32[4,2,64,128]{3,2,0,1:T(8,128)S(1)}, f32[4,2,64,128]{3,2,0,1:T(8,128)S(1)}, u32[]{:S(2)}, u32[]{:S(2)}) collective-permute-start(f32[4,2,64,128]{3,2,0,1:T(8,128)S(1)} %pad_maximum_fusion.2), channel_id=1, source_target_pairs={{0,7},{1,0},{2,1},{3,2},{4,3},{5,4},{6,5},{7,6},{8,15},{9,8},{10,9... | collective-permute-start | bytes 786440 | tf_op jit(solution)/shard_map/ppermute | solution.py:223
  26.4 9.8 %collective-permute-start.2 = (f32[4,2,64,128]{3,2,0,1:T(8,128)S(1)}, f32[4,2,64,128]{3,2,0,1:T(8,128)S(1)}, u32[]{:S(2)}, u32[]{:S(2)}) collective-permute-start(f32[4,2,64,128]{3,2,0,1:T(8,128)S(1)} %pad_maximum_fusion.2), channel_id=1, source_target_pairs={{0,1},{1,2},{2,3},{3,4},{4,5},{5,6},{6,7},{7,0},{8,9},{9,10},{10,1... | collective-permute-start | bytes 786440 | tf_op jit(solution)/shard_map/ppermute | solution.py:222
  124.4 7.4 %collective-permute-start.4 = (f32[1,64,128]{2,1,0:T(8,128)S(1)}, f32[1,64,128]{2,1,0:T(8,128)S(1)}, u32[]{:S(2)}, u32[]{:S(2)}) collective-permute-start(f32[1,64,128]{2,1,0:T(8,128)S(1)} %fusion.31), channel_id=1, source_target_pairs={{0,24},{8,0},{16,8},{24,16},{1,25},{9,1},{17,9},{25,17},{2,26},{10... | collective-permute-start | bytes 98312 | tf_op jit(solution)/shard_map/ppermute | solution.py:218
  129.9 6.8 %collective-permute-start.5 = (f32[1,64,128]{2,1,0:T(8,128)S(1)}, f32[1,64,128]{2,1,0:T(8,128)S(1)}, u32[]{:S(2)}, u32[]{:S(2)}) collective-permute-start(f32[1,64,128]{2,1,0:T(8,128)S(1)} %fusion.30), channel_id=1, source_target_pairs={{0,8},{8,16},{16,24},{24,0},{1,9},{9,17},{17,25},{25,1},{2,10},{10... | collective-permute-start | bytes 98312 | tf_op jit(solution)/shard_map/ppermute | solution.py:217
  137.1 6.2 %collective-permute-start.7 = (f32[2,2,64,128]{3,2,1,0:T(8,128)S(1)}, f32[2,2,64,128]{3,2,1,0:T(8,128)S(1)}, u32[]{:S(2)}, u32[]{:S(2)}) collective-permute-start(f32[2,2,64,128]{3,2,1,0:T(8,128)S(1)} %pad_maximum_fusion.3), channel_id=1, source_target_pairs={{0,7},{1,0},{2,1},{3,2},{4,3},{5,4},{6,5},{7,6},{8,15},{9,8},{10,9... | collective-permute-start | bytes 393224 | tf_op jit(solution)/shard_map/ppermute | solution.py:223
  141.4 7.8 %collective-permute-start.6 = (f32[2,2,64,128]{3,2,1,0:T(8,128)S(1)}, f32[2,2,64,128]{3,2,1,0:T(8,128)S(1)}, u32[]{:S(2)}, u32[]{:S(2)}) collective-permute-start(f32[2,2,64,128]{3,2,1,0:T(8,128)S(1)} %pad_maximum_fusion.3), channel_id=1, source_target_pairs={{0,1},{1,2},{2,3},{3,4},{4,5},{5,6},{6,7},{7,0},{8,9},{9,10},{10,1... | collective-permute-start | bytes 393224 | tf_op jit(solution)/shard_map/ppermute | solution.py:222
  162.4 39.4 %copy-start.1 = (f32[4,64,128]{2,1,0:T(8,128)S(1)}, f32[4,64,128]{2,1,0:T(8,128)}, u32[]{:S(2)}) copy-start(f32[4,64,128]{2,1,0:T(8,128)} %index_ref.1) | copy-start | bytes 393220
  162.4 39.4 %copy-start.2 = (f32[128,128]{1,0:T(8,128)S(1)}, f32[128,128]{1,0:T(8,128)}, u32[]{:S(2)}) copy-start(f32[128,128]{1,0:T(8,128)} %constant.48.order_ref) | copy-start | bytes 196612
  162.6 7.5 %collective-permute-start.8 = (f32[8,4,64,128]{3,2,1,0:T(8,128)S(1)}, f32[8,4,64,128]{3,2,1,0:T(8,128)S(1)}, u32[]{:S(2)}, u32[]{:S(2)}) collective-permute-start(f32[8,4,64,128]{3,2,1,0:T(8,128)S(1)} %slice_bitcast_fusion), channel_id=1, source_target_pairs={{0,32},{32,0},{64,96},{96,64},{128,160},{160,128},{192,224},{224,1... | collective-permute-start | bytes 3145736 | tf_op jit(solution)/shard_map/ppermute | solution.py:454
  217.7 5.7 %collective-permute-start.9 = (f32[288,128]{1,0:T(8,128)S(1)}, f32[288,128]{1,0:T(8,128)S(1)}, u32[]{:S(2)}, u32[]{:S(2)}) collective-permute-start(f32[288,128]{1,0:T(8,128)S(1)} %get-tuple-element.12), channel_id=1, source_target_pairs={{0,32},{32,64},{64,96},{96,128},{128,160},{160,192},{192,224},{224... | collective-permute-start | bytes 442376 | tf_op jit(solution)/shard_map/ppermute | solution.py:376
  221.3 4.9 %collective-permute-start.10 = (f32[288,128]{1,0:T(8,128)S(1)}, f32[288,128]{1,0:T(8,128)S(1)}, u32[]{:S(2)}, u32[]{:S(2)}) collective-permute-start(f32[288,128]{1,0:T(8,128)S(1)} %get-tuple-element.13), channel_id=1, source_target_pairs={{0,480},{32,0},{64,32},{96,64},{128,96},{160,128},{192,160},{224,1... | collective-permute-start | bytes 442376 | tf_op jit(solution)/shard_map/ppermute | solution.py:377
Sparse Core Ops, SparseCore 0:
  37.6 73.5 all-gather.1

commit v9 on v8

--- a/solution.py
+++ b/solution.py
@@ -120,7 +120,7 @@
 
         @pl.when(pid == k)
         def _(k=k):
-            @pl.loop(0, GROUP // 2)
+            @pl.loop(0, GROUP // 2, unroll=2)
             def _(pair):
                 step(2 * pair, 0, k, chunks - k)
                 step(2 * pair + 1, 1, k, chunks - k)
@@ -186,7 +186,7 @@
                 multiply(GROUP - 1)
                 step(GROUP - 2, 0, k, chunks - k)
 
-            @pl.loop(skip, GROUP // 2)
+            @pl.loop(skip, GROUP // 2, unroll=1 if skip else 2)
             def _(pair):
                 step(GROUP - 1 - 2 * pair, 1, k, chunks - k)
                 step(GROUP - 2 - 2 * pair, 0, k, chunks - k)

time: 236 us -> 235 us (level)
  no operation moved by 1% of the time
where the time goes in v9:
time: 235 us; the launch traced here: 234 us
  waiting for transfers between devices  100 us (43%)
  blocking collectives  46.4 us (20%)
  starting transfers between devices  37.1 us (16%)
  Pallas kernels  28.3 us (12%)
  between operations  14.5 us (6%)
  other arithmetic  4.82 us (2%)
    all_gather x1, waiting for transfers between devices, body(): lax.all_gather(pack_corners(*widen(reorder(index, order), 'tx', 'ty')), '...  70.6 us
    all_to_all x1, blocking collectives, body(): lax.all_to_all(both, 'angle', 0, 0, tiled=True, axis_index_groups=chip_gr...  31.5 us
    all_to_all x1, blocking collectives, step_and_smooth(): strips = lax.all_to_all(strips, ('tx', 'ty'), 0, 0, tiled=True)  14.8 us
    pallas_call x1, Pallas kernels, body(): pl.pallas_call(functools.partial(backward_kernel, tall), grid=(steps,), i...  12.7 us
    pallas_call x1, Pallas kernels, body(): pl.pallas_call(functools.partial(forward_kernel, tall), grid=(steps,), in...  12.4 us
    ppermute x2, waiting for transfers between devices, widen(): above = lax.ppermute(wide, axis_y, ring(ny, 1))  11.1 us
    ppermute x2, starting transfers between devices, widen(): right = unpack(lax.ppermute(pack(side(0)), axis_x, ring(nx, -1)))  8.92 us
    ppermute x2, starting transfers between devices, widen(): below = lax.ppermute(wide, axis_y, ring(ny, -1))  7.63 us
  transfers between devices with their start and end apart: 12, of which 9 were waited for; matrix products, arithmetic and copies ran while one was open for 2% of the time, Pallas kernels for 0%

profile of v9, /device:TPU:1, one launch (start us, length us, event | category | flops | bytes accessed | tf_op | source)
XLA Modules:
  0.0 234.3 jit_solution(2902122117933478120)
XLA Ops:
  7.2 0.0 copy-start
  7.2 0.0 all-gather.2.cloned.1.call-start
  7.2 1.2 convolution_bitcast_fusion
  8.4 0.2 fusion.37
  8.6 0.1 fusion.17
  8.7 0.1 fusion.23
  8.8 5.0 %collective-permute-start.1 = (f32[2,64,128]{2,1,0:T(8,128)S(1)}, f32[2,64,128]{2,1,0:T(8,128)S(1)}, u32[]{:S(2)}, u32[]{:S(2)}) collective-permute-start(f32[2,64,128]{2,1,0:T(8,128)S(1)} %fusion.23), channel_id=1, source_target_pairs={{0,8},{8,16},{16,24},{24,0},{1,9},{9,17},{17,25},{25,1},{2,10},{10... | collective-permute-start | bytes 196616 | tf_op jit(solution)/shard_map/ppermute | solution.py:217
  13.9 0.1 fusion.18
  14.0 0.1 fusion.24
  14.1 3.6 %collective-permute-start = (f32[2,64,128]{2,1,0:T(8,128)S(1)}, f32[2,64,128]{2,1,0:T(8,128)S(1)}, u32[]{:S(2)}, u32[]{:S(2)}) collective-permute-start(f32[2,64,128]{2,1,0:T(8,128)S(1)} %fusion.24), channel_id=1, source_target_pairs={{0,24},{8,0},{16,8},{24,16},{1,25},{9,1},{17,9},{25,17},{2,26},{10... | collective-permute-start | bytes 196616 | tf_op jit(solution)/shard_map/ppermute | solution.py:218
  17.7 0.1 fusion.36
  17.8 4.8 %collective-permute-done = f32[2,64,128]{2,1,0:T(8,128)S(1)} collective-permute-done((f32[2,64,128]{2,1,0:T(8,128)S(1)}, f32[2,64,128]{2,1,0:T(8,128)S(1)}, u32[]{:S(2)}, u32[]{:S(2)}) %collective-permute-start) | collective-permute-done | bytes 65568 | tf_op jit(solution)/shard_map/ppermute | solution.py:218
  22.5 0.1 fusion.40
  22.6 0.0 collective-permute-done.1
  22.7 0.1 fusion.41
  22.8 0.0 copy-start.4
  22.8 0.2 fusion.10
  23.0 0.0 copy-start.3
  23.0 3.3 %collective-permute-start.3 = (f32[4,2,64,128]{3,2,0,1:T(8,128)S(1)}, f32[4,2,64,128]{3,2,0,1:T(8,128)S(1)}, u32[]{:S(2)}, u32[]{:S(2)}) collective-permute-start(f32[4,2,64,128]{3,2,0,1:T(8,128)S(1)} %pad_maximum_fusion.2), channel_id=1, source_target_pairs={{0,7},{1,0},{2,1},{3,2},{4,3},{5,4},{6,5},{7,6},{8,15},{9,8},{10,9... | collective-permute-start | bytes 786440 | tf_op jit(solution)/shard_map/ppermute | solution.py:223
  26.4 2.4 %collective-permute-start.2 = (f32[4,2,64,128]{3,2,0,1:T(8,128)S(1)}, f32[4,2,64,128]{3,2,0,1:T(8,128)S(1)}, u32[]{:S(2)}, u32[]{:S(2)}) collective-permute-start(f32[4,2,64,128]{3,2,0,1:T(8,128)S(1)} %pad_maximum_fusion.2), channel_id=1, source_target_pairs={{0,1},{1,2},{2,3},{3,4},{4,5},{5,6},{6,7},{7,0},{8,9},{9,10},{10,1... | collective-permute-start | bytes 786440 | tf_op jit(solution)/shard_map/ppermute | solution.py:222
  28.8 1.8 collective-permute-done.3
  30.6 0.2 fusion.35
  30.8 5.4 %collective-permute-done.2 = f32[4,2,64,128]{3,2,0,1:T(8,128)S(1)} collective-permute-done((f32[4,2,64,128]{3,2,0,1:T(8,128)S(1)}, f32[4,2,64,128]{3,2,0,1:T(8,128)S(1)}, u32[]{:S(2)}, u32[]{:S(2)}) %collective-permute-start.2) | collective-permute-done | bytes 262176 | tf_op jit(solution)/shard_map/ppermute | solution.py:222
  36.1 0.2 maximum_select_fusion
  36.5 1.0 maximum_maximum_fusion
  37.4 0.0 all-gather.2.cloned.1.call-update
  37.5 0.6 fusion.44
  38.1 0.6 add_multiply_fusion
  38.7 1.5 fusion.14
  40.3 0.2 convolution_bitcast_fusion.1
  40.5 70.6 %all-gather.2.cloned.1.call-done.index_ref = f32[64,320,128]{2,1,0:T(8,128)} async-done(((f32[4,320,128]{2,1,0:T(8,128)}), f32[64,320,128]{2,1,0:T(8,128)}) %all-gather.2.cloned.1.call-update) | async-done | bytes 10485776 | tf_op jit(solution)/shard_map/all_gather | solution.py:410
  111.2 12.4 %forward.1.field_ref = f32[64,2,64,128]{3,2,1,0:T(8,128)S(1)} custom-call(f32[64,320,128]{2,1,0:T(8,128)} %all-gather.2.cloned.1.call-done.index_ref, f32[2,2,192,128]{3,2,1,0:T(8,128)S(1)} %pad_maximum_fusion.start_ref), custom_call_target="tpu_custom_call" | custom-call | tf_op jit(solution)/shard_map/forward/pallas_call | solution.py:417
  123.6 0.1 fusion.38
  123.7 0.1 fusion.39
  123.8 0.1 fusion.29
  123.9 0.1 fusion.31
  124.0 5.3 %collective-permute-start.4 = (f32[1,64,128]{2,1,0:T(8,128)S(1)}, f32[1,64,128]{2,1,0:T(8,128)S(1)}, u32[]{:S(2)}, u32[]{:S(2)}) collective-permute-start(f32[1,64,128]{2,1,0:T(8,128)S(1)} %fusion.31), channel_id=1, source_target_pairs={{0,24},{8,0},{16,8},{24,16},{1,25},{9,1},{17,9},{25,17},{2,26},{10... | collective-permute-start | bytes 98312 | tf_op jit(solution)/shard_map/ppermute | solution.py:218
  129.3 0.1 fusion.28
  129.4 0.1 fusion.30
  129.5 1.9 collective-permute-start.5
  131.4 0.1 fusion.42
  131.5 4.8 %collective-permute-done.5 = f32[1,64,128]{2,1,0:T(8,128)S(1)} collective-permute-done((f32[1,64,128]{2,1,0:T(8,128)S(1)}, f32[1,64,128]{2,1,0:T(8,128)S(1)}, u32[]{:S(2)}, u32[]{:S(2)}) %collective-permute-start.5) | collective-permute-done | bytes 32800 | tf_op jit(solution)/shard_map/ppermute | solution.py:217
  136.3 0.1 fusion.43
  136.4 0.1 fusion.20
  136.5 0.1 maximum_bitcast_fusion.1
  136.6 4.3 %collective-permute-start.7 = (f32[2,2,64,128]{3,2,1,0:T(8,128)S(1)}, f32[2,2,64,128]{3,2,1,0:T(8,128)S(1)}, u32[]{:S(2)}, u32[]{:S(2)}) collective-permute-start(f32[2,2,64,128]{3,2,1,0:T(8,128)S(1)} %pad_maximum_fusion.3), channel_id=1, source_target_pairs={{0,7},{1,0},{2,1},{3,2},{4,3},{5,4},{6,5},{7,6},{8,15},{9,8},{10,9... | collective-permute-start | bytes 393224 | tf_op jit(solution)/shard_map/ppermute | solution.py:223
  140.9 2.1 collective-permute-start.6
  143.0 0.0 collective-permute-done.7
  143.0 5.7 %collective-permute-done.6 = f32[2,2,64,128]{3,2,1,0:T(8,128)S(1)} collective-permute-done((f32[2,2,64,128]{3,2,1,0:T(8,128)S(1)}, f32[2,2,64,128]{3,2,1,0:T(8,128)S(1)}, u32[]{:S(2)}, u32[]{:S(2)}) %collective-permute-start.6) | collective-permute-done | bytes 131104 | tf_op jit(solution)/shard_map/ppermute | solution.py:222
  148.8 12.7 %backward.1 = f32[2,8,4,64,128]{4,3,2,1,0:T(8,128)S(1)} custom-call(f32[64,320,128]{2,1,0:T(8,128)} %all-gather.2.cloned.1.call-done.index_ref, f32[2,2,192,128]{3,2,1,0:T(8,128)S(1)} %pad_maximum_fusion.1.start_ref, f32[64,2,64,128]{3,2,1,0:T(8,128)S(1)} %forward.1.field_ref), custom_call_target="tpu_custom_call" | custom-call | tf_op jit(solution)/shard_map/backward/pallas_call | solution.py:439
  161.5 0.0 copy-start.1
  161.5 0.0 copy-start.2
  161.5 0.1 slice_bitcast_fusion
  161.6 5.3 %collective-permute-start.8 = (f32[8,4,64,128]{3,2,1,0:T(8,128)S(1)}, f32[8,4,64,128]{3,2,1,0:T(8,128)S(1)}, u32[]{:S(2)}, u32[]{:S(2)}) collective-permute-start(f32[8,4,64,128]{3,2,1,0:T(8,128)S(1)} %slice_bitcast_fusion), channel_id=1, source_target_pairs={{0,32},{32,0},{64,96},{96,64},{128,160},{160,128},{192,224},{224,1... | collective-permute-start | bytes 3145736 | tf_op jit(solution)/shard_map/ppermute | solution.py:454
  166.9 2.3 collective-permute-done.8
  169.1 0.2 fusion
  169.3 31.5 %all_to_all.10.parts_ref = f32[8,4,64,128]{3,2,1,0:T(8,128)S(1)} all-to-all(f32[8,4,64,128]{3,2,1,0:T(8,128)S(1)} %fusion), channel_id=1, replica_groups={{0,64,128,192,256,320,384,448},{32,96,160,224,288,352,416,480},{1,65,12..., dimensions={0} | all-to-all | bytes 2097152 | tf_op jit(solution)/shard_map/all_to_all | solution.py:455
  200.8 1.0 share.1
  201.8 14.8 %all_to_all.11.strips_ref = f32[32,16,128]{2,1,0:T(8,128)S(1)} all-to-all(f32[32,16,128]{2,1,0:T(8,128)S(1)} %get-tuple-element.10), channel_id=1, replica_groups=mesh['angle'=16,'tx'=4,'ty'=8] {'tx','ty'}, dimensions={0} | all-to-all | bytes 524288 | tf_op jit(solution)/shard_map/all_to_all | solution.py:367
  216.7 3.6 %collective-permute-start.9 = (f32[288,128]{1,0:T(8,128)S(1)}, f32[288,128]{1,0:T(8,128)S(1)}, u32[]{:S(2)}, u32[]{:S(2)}) collective-permute-start(f32[288,128]{1,0:T(8,128)S(1)} %get-tuple-element.12), channel_id=1, source_target_pairs={{0,32},{32,64},{64,96},{96,128},{128,160},{160,192},{192,224},{224... | collective-permute-start | bytes 442376 | tf_op jit(solution)/shard_map/ppermute | solution.py:376
  220.3 0.2 collective-permute-start.10
  220.5 1.9 collective-permute-done.9.low_ref
  222.4 2.8 %collective-permute-done.10.high_ref = f32[288,128]{1,0:T(8,128)S(1)} collective-permute-done((f32[288,128]{1,0:T(8,128)S(1)}, f32[288,128]{1,0:T(8,128)S(1)}, u32[]{:S(2)}, u32[]{:S(2)}) %collective-permute-start.10) | collective-permute-done | bytes 147488 | tf_op jit(solution)/shard_map/ppermute | solution.py:377
  225.2 2.2 smooth.1
  (24 shorter events, 0.3 us)
Async XLA Ops:
  7.2 33.1 %copy-start = (f32[2,1,64,128]{3,2,1,0:T(8,128)S(1)}, f32[2,1,64,128]{3,2,1,0:T(8,128)}, u32[]{:S(2)}) copy-start(f32[2,1,64,128]{3,2,1,0:T(8,128)} %param.5) | copy-start | bytes 196612
  7.2 104.0 %all-gather.2.cloned.1.call-start = ((), (), s32[]{:S(2)}) async-start(), calls=%async_computation.2 | async-start | bytes 11141120 | tf_op jit(solution)/shard_map/all_gather | solution.py:410
  8.8 13.8 %collective-permute-start.1 = (f32[2,64,128]{2,1,0:T(8,128)S(1)}, f32[2,64,128]{2,1,0:T(8,128)S(1)}, u32[]{:S(2)}, u32[]{:S(2)}) collective-permute-start(f32[2,64,128]{2,1,0:T(8,128)S(1)} %fusion.23), channel_id=1, source_target_pairs={{0,8},{8,16},{16,24},{24,0},{1,9},{9,17},{17,25},{25,1},{2,10},{10... | collective-permute-start | bytes 196616 | tf_op jit(solution)/shard_map/ppermute | solution.py:217
  14.1 8.5 %collective-permute-start = (f32[2,64,128]{2,1,0:T(8,128)S(1)}, f32[2,64,128]{2,1,0:T(8,128)S(1)}, u32[]{:S(2)}, u32[]{:S(2)}) collective-permute-start(f32[2,64,128]{2,1,0:T(8,128)S(1)} %fusion.24), channel_id=1, source_target_pairs={{0,24},{8,0},{16,8},{24,16},{1,25},{9,1},{17,9},{25,17},{2,26},{10... | collective-permute-start | bytes 196616 | tf_op jit(solution)/shard_map/ppermute | solution.py:218
  22.8 14.7 %copy-start.4 = (s32[1,2]{1,0:T(1,128)S(1)}, s32[1,2]{1,0:T(1,128)}, u32[]{:S(2)}) copy-start(s32[1,2]{1,0:T(1,128)} %param.6) | copy-start | bytes 28
  23.0 17.3 %copy-start.3 = (f32[128,128,1]{1,0,2:T(8,128)S(1)}, f32[128,128,1]{1,0,2:T(8,128)}, u32[]{:S(2)}) copy-start(f32[128,128,1]{1,0,2:T(8,128)} %constant.49) | copy-start | bytes 196612
  23.0 7.6 %collective-permute-start.3 = (f32[4,2,64,128]{3,2,0,1:T(8,128)S(1)}, f32[4,2,64,128]{3,2,0,1:T(8,128)S(1)}, u32[]{:S(2)}, u32[]{:S(2)}) collective-permute-start(f32[4,2,64,128]{3,2,0,1:T(8,128)S(1)} %pad_maximum_fusion.2), channel_id=1, source_target_pairs={{0,7},{1,0},{2,1},{3,2},{4,3},{5,4},{6,5},{7,6},{8,15},{9,8},{10,9... | collective-permute-start | bytes 786440 | tf_op jit(solution)/shard_map/ppermute | solution.py:223
  26.4 9.8 %collective-permute-start.2 = (f32[4,2,64,128]{3,2,0,1:T(8,128)S(1)}, f32[4,2,64,128]{3,2,0,1:T(8,128)S(1)}, u32[]{:S(2)}, u32[]{:S(2)}) collective-permute-start(f32[4,2,64,128]{3,2,0,1:T(8,128)S(1)} %pad_maximum_fusion.2), channel_id=1, source_target_pairs={{0,1},{1,2},{2,3},{3,4},{4,5},{5,6},{6,7},{7,0},{8,9},{9,10},{10,1... | collective-permute-start | bytes 786440 | tf_op jit(solution)/shard_map/ppermute | solution.py:222
  124.0 7.4 %collective-permute-start.4 = (f32[1,64,128]{2,1,0:T(8,128)S(1)}, f32[1,64,128]{2,1,0:T(8,128)S(1)}, u32[]{:S(2)}, u32[]{:S(2)}) collective-permute-start(f32[1,64,128]{2,1,0:T(8,128)S(1)} %fusion.31), channel_id=1, source_target_pairs={{0,24},{8,0},{16,8},{24,16},{1,25},{9,1},{17,9},{25,17},{2,26},{10... | collective-permute-start | bytes 98312 | tf_op jit(solution)/shard_map/ppermute | solution.py:218
  129.5 6.8 %collective-permute-start.5 = (f32[1,64,128]{2,1,0:T(8,128)S(1)}, f32[1,64,128]{2,1,0:T(8,128)S(1)}, u32[]{:S(2)}, u32[]{:S(2)}) collective-permute-start(f32[1,64,128]{2,1,0:T(8,128)S(1)} %fusion.30), channel_id=1, source_target_pairs={{0,8},{8,16},{16,24},{24,0},{1,9},{9,17},{17,25},{25,1},{2,10},{10... | collective-permute-start | bytes 98312 | tf_op jit(solution)/shard_map/ppermute | solution.py:217
  136.6 6.4 %collective-permute-start.7 = (f32[2,2,64,128]{3,2,1,0:T(8,128)S(1)}, f32[2,2,64,128]{3,2,1,0:T(8,128)S(1)}, u32[]{:S(2)}, u32[]{:S(2)}) collective-permute-start(f32[2,2,64,128]{3,2,1,0:T(8,128)S(1)} %pad_maximum_fusion.3), channel_id=1, source_target_pairs={{0,7},{1,0},{2,1},{3,2},{4,3},{5,4},{6,5},{7,6},{8,15},{9,8},{10,9... | collective-permute-start | bytes 393224 | tf_op jit(solution)/shard_map/ppermute | solution.py:223
  140.9 7.8 %collective-permute-start.6 = (f32[2,2,64,128]{3,2,1,0:T(8,128)S(1)}, f32[2,2,64,128]{3,2,1,0:T(8,128)S(1)}, u32[]{:S(2)}, u32[]{:S(2)}) collective-permute-start(f32[2,2,64,128]{3,2,1,0:T(8,128)S(1)} %pad_maximum_fusion.3), channel_id=1, source_target_pairs={{0,1},{1,2},{2,3},{3,4},{4,5},{5,6},{6,7},{7,0},{8,9},{9,10},{10,1... | collective-permute-start | bytes 393224 | tf_op jit(solution)/shard_map/ppermute | solution.py:222
  161.5 39.4 %copy-start.1 = (f32[4,64,128]{2,1,0:T(8,128)S(1)}, f32[4,64,128]{2,1,0:T(8,128)}, u32[]{:S(2)}) copy-start(f32[4,64,128]{2,1,0:T(8,128)} %index_ref.1) | copy-start | bytes 393220
  161.5 39.4 %copy-start.2 = (f32[128,128]{1,0:T(8,128)S(1)}, f32[128,128]{1,0:T(8,128)}, u32[]{:S(2)}) copy-start(f32[128,128]{1,0:T(8,128)} %constant.48.order_ref) | copy-start | bytes 196612
  161.6 7.5 %collective-permute-start.8 = (f32[8,4,64,128]{3,2,1,0:T(8,128)S(1)}, f32[8,4,64,128]{3,2,1,0:T(8,128)S(1)}, u32[]{:S(2)}, u32[]{:S(2)}) collective-permute-start(f32[8,4,64,128]{3,2,1,0:T(8,128)S(1)} %slice_bitcast_fusion), channel_id=1, source_target_pairs={{0,32},{32,0},{64,96},{96,64},{128,160},{160,128},{192,224},{224,1... | collective-permute-start | bytes 3145736 | tf_op jit(solution)/shard_map/ppermute | solution.py:454
  216.7 5.7 %collective-permute-start.9 = (f32[288,128]{1,0:T(8,128)S(1)}, f32[288,128]{1,0:T(8,128)S(1)}, u32[]{:S(2)}, u32[]{:S(2)}) collective-permute-start(f32[288,128]{1,0:T(8,128)S(1)} %get-tuple-element.12), channel_id=1, source_target_pairs={{0,32},{32,64},{64,96},{96,128},{128,160},{160,192},{192,224},{224... | collective-permute-start | bytes 442376 | tf_op jit(solution)/shard_map/ppermute | solution.py:376
  220.3 4.9 %collective-permute-start.10 = (f32[288,128]{1,0:T(8,128)S(1)}, f32[288,128]{1,0:T(8,128)S(1)}, u32[]{:S(2)}, u32[]{:S(2)}) collective-permute-start(f32[288,128]{1,0:T(8,128)S(1)} %get-tuple-element.13), channel_id=1, source_target_pairs={{0,480},{32,0},{64,32},{96,64},{128,96},{160,128},{192,160},{224,1... | collective-permute-start | bytes 442376 | tf_op jit(solution)/shard_map/ppermute | solution.py:377
Sparse Core Ops, SparseCore 0:
  37.6 73.5 all-gather.1
